TPU v7x, 32 devices: a whole 2x2x4 slice. The times are simulated.
32 devices in a mesh: dp: 16 (over z, y, core), tensor: 2 (over x).
Axes of the slice: x: 2, y: 2, z: 4, core: 2. Of those that a mesh axis runs over, the one named last changes fastest.
Arguments:
- tokens: bfloat16 [8192, 2048], P('dp'), may hold values from -6 to 6
- cotangent: bfloat16 [8192, 2048], P('dp'), may hold values from -6 to 6
- lengths: int32 [16], replicated, may hold values from 128 to 512, as said below
- attn_gain: float32 [2048], replicated, may hold values from 0.5 to 1.5
- query_gain: float32 [64], replicated, may hold values from 0.25 to 1.75
- key_gain: float32 [64], replicated, may hold values from 0.25 to 1.75
- w_query: bfloat16 [2048, 2048], P('dp', 'tensor'), may hold values from -0.125 to 0.125
- key_weight_matrix: bfloat16 [2048, 512], P('dp', 'tensor'), may hold values from -0.125 to 0.125
- value_weight_matrix: bfloat16 [2048, 512], P('dp', 'tensor'), may hold values from -0.125 to 0.125
- w_out: bfloat16 [2048, 2048], P(('tensor', 'dp')), may hold values from -0.5 to 0.5
- ffn_gain: float32 [2048], replicated, may hold values from 0.5 to 1.5
- w_gate: bfloat16 [2048, 8192], P('dp', 'tensor'), may hold values from -0.125 to 0.125
- w_up: bfloat16 [2048, 8192], P('dp', 'tensor'), may hold values from -0.125 to 0.125
- w_down: bfloat16 [8192, 2048], P(('tensor', 'dp')), may hold values from -0.0625 to 0.0625
Outputs:
- layer_out: bfloat16 [8192, 2048], P('dp')
- input_grad: float32 [8192, 2048], P('dp')
- attn_gain_grad: float32 [2048], replicated
- query_gain_grad: float32 [64], replicated
- key_gain_grad: float32 [64], replicated
- w_query_grad: float32 [2048, 2048], P('dp', 'tensor')
- w_key_grad: float32 [2048, 512], P('dp', 'tensor')
- w_value_grad: float32 [2048, 512], P('dp', 'tensor')
- w_out_grad: float32 [2048, 2048], P(('tensor', 'dp'))
- ffn_gain_grad: float32 [2048], replicated
- w_gate_grad: float32 [2048, 8192], P('dp', 'tensor')
- w_up_grad: float32 [2048, 8192], P('dp', 'tensor')
- w_down_grad: float32 [8192, 2048], P(('tensor', 'dp'))
Inputs may be any that keep to these rules, and one draw needn't show every extreme that they name: `lengths`: valid tokens at the start of each slot of 512; the rest is padding.
All inputs are finite; a program needn't handle non-finite values.
Results may differ from a plain program's by a relative error of at most 0.014.
Values may be sent and summed in bfloat16 or wider, within the bound.
A program may use at most 256 MiB of HBM per device.

v0:
```python
import math

import jax
import jax.numpy as jnp
from jax import lax
from jax.sharding import PartitionSpec as P

EPS = 1e-05
ROPE_BASE = 1000000.0
MASKED = -1e30


def rms_scale(values, gain):
    return values * lax.rsqrt(jnp.mean(values * values, axis=-1, keepdims=True) + EPS) * gain


def angles(positions, head_dim):
    half_dim = head_dim // 2
    freq = jnp.exp(
        jnp.arange(half_dim, dtype=jnp.float32) * (-2.0 * math.log(ROPE_BASE) / head_dim)
    )
    turned = positions.astype(jnp.float32)[:, None] * freq[None, :]
    return (jnp.cos(turned)[:, None, :], jnp.sin(turned)[:, None, :])


def rotate(values, cosine, sine_table):
    half_dim = values.shape[-1] // 2
    first_half = values[..., :half_dim]
    second_half = values[..., half_dim:]
    return jnp.concatenate(
        [
            first_half * cosine - second_half * sine_table,
            second_half * cosine + first_half * sine_table,
        ],
        axis=-1,
    )


def body(
    tokens,
    cotangent,
    lengths,
    attn_gain,
    query_gain,
    key_gain,
    w_query,
    key_weight_matrix,
    value_weight_matrix,
    w_out,
    ffn_gain,
    w_gate,
    w_up,
    w_down,
):
    wq_full, wk_full, wv_full, wo_full, wg_full, wu_full, wd_full = (
        lax.all_gather(w_query, "dp", axis=0, tiled=True),
        lax.all_gather(key_weight_matrix, "dp", axis=0, tiled=True),
        lax.all_gather(value_weight_matrix, "dp", axis=0, tiled=True),
        lax.all_gather(w_out, "dp", axis=0, tiled=True),
        lax.all_gather(w_gate, "dp", axis=0, tiled=True),
        lax.all_gather(w_up, "dp", axis=0, tiled=True),
        lax.all_gather(w_down, "dp", axis=0, tiled=True),
    )
    row_count = tokens.shape[0]
    head_dim = query_gain.shape[0]
    q_heads = wq_full.shape[1] // head_dim
    k_heads = wk_full.shape[1] // head_dim
    group_size = q_heads // k_heads
    score_scale = 1.0 / math.sqrt(head_dim)
    dp_index = lax.axis_index("dp")
    slot_length = lengths[dp_index]
    positions = jnp.arange(row_count, dtype=jnp.int32)
    valid_rows = (positions < slot_length).astype(jnp.float32)[:, None]
    allowed = (positions[None, :] <= positions[:, None]) & (positions[None, :] < slot_length)
    cosine, sine_table = angles(positions, head_dim)
    inputs = tokens.astype(jnp.float32)
    hidden_state = rms_scale(inputs, attn_gain).astype(jnp.bfloat16)
    q_proj = jnp.dot(hidden_state, wq_full, preferred_element_type=jnp.float32)
    key_projected = jnp.dot(hidden_state, wk_full, preferred_element_type=jnp.float32)
    value_projected = jnp.dot(hidden_state, wv_full, preferred_element_type=jnp.float32)

    def prepare(q_vals, k_vals, q_gain, k_gain):
        q_norm = rms_scale(q_vals.reshape(row_count, q_heads, head_dim), q_gain)
        k_norm = rms_scale(k_vals.reshape(row_count, k_heads, head_dim), k_gain)
        return (rotate(q_norm, cosine, sine_table), rotate(k_norm, cosine, sine_table))

    (q_rot, k_rot), prep_back = jax.vjp(prepare, q_proj, key_projected, query_gain, key_gain)
    q_low = q_rot.astype(jnp.bfloat16)
    k_low = k_rot.astype(jnp.bfloat16)
    v_low = value_projected.astype(jnp.bfloat16)
    q_grouped = q_low.reshape(row_count, k_heads, group_size, head_dim).transpose(1, 2, 0, 3)
    k_grouped = k_low.transpose(1, 0, 2)
    v_grouped = v_low.reshape(row_count, k_heads, head_dim).transpose(1, 0, 2)

    def scores_of(q_one, k_one):
        scores = (
            jnp.einsum("gid,jd->gij", q_one, k_one, preferred_element_type=jnp.float32)
            * score_scale
        )
        return jnp.where(allowed[None], scores, MASKED)

    def attend(packed):
        q_one, k_one, v_one = packed
        scores = scores_of(q_one, k_one)
        row_max = jnp.max(scores, axis=-1, keepdims=True)
        exp_scores = jnp.exp(scores - row_max)
        row_total = jnp.sum(exp_scores, axis=-1, keepdims=True)
        probs = (exp_scores / row_total).astype(jnp.bfloat16)
        attended = jnp.einsum("gij,jd->gid", probs, v_one, preferred_element_type=jnp.float32)
        return (attended, row_max[..., 0] + jnp.log(row_total[..., 0]))

    attended, log_totals = lax.map(attend, (q_grouped, k_grouped, v_grouped))
    o_low = (
        attended.transpose(2, 0, 1, 3).reshape(row_count, q_heads * head_dim).astype(jnp.bfloat16)
    )
    attn_part = jnp.dot(o_low, wo_full, preferred_element_type=jnp.float32)
    h_one = inputs + lax.psum(attn_part, "tensor")
    hidden_two = rms_scale(h_one, ffn_gain).astype(jnp.bfloat16)
    gate = jnp.dot(hidden_two, wg_full, preferred_element_type=jnp.float32)
    up_proj = jnp.dot(hidden_two, wu_full, preferred_element_type=jnp.float32)
    sigmoid_gate = jax.nn.sigmoid(gate)
    silu_gate = gate * sigmoid_gate
    act = (silu_gate * up_proj).astype(jnp.bfloat16)
    mlp_part = jnp.dot(act, wd_full, preferred_element_type=jnp.float32)
    layer_out = (
        h_one + lax.psum(mlp_part.astype(jnp.bfloat16), "tensor").astype(jnp.float32)
    ).astype(jnp.bfloat16)
    grad_out = cotangent.astype(jnp.float32) * valid_rows
    grad_out_low = grad_out.astype(jnp.bfloat16)
    g_down = jnp.dot(act.T, grad_out_low, preferred_element_type=jnp.float32)
    grad_act = jnp.dot(grad_out_low, wd_full.T, preferred_element_type=jnp.float32)
    silu_slope = sigmoid_gate * (1.0 + gate * (1.0 - sigmoid_gate))
    grad_gate = (grad_act * up_proj * silu_slope).astype(jnp.bfloat16)
    grad_up = (grad_act * silu_gate).astype(jnp.bfloat16)
    g_gate = jnp.dot(hidden_two.T, grad_gate, preferred_element_type=jnp.float32)
    g_up = jnp.dot(hidden_two.T, grad_up, preferred_element_type=jnp.float32)
    grad_hidden_two = jnp.dot(grad_gate, wg_full.T, preferred_element_type=jnp.float32) + jnp.dot(
        grad_up, wu_full.T, preferred_element_type=jnp.float32
    )
    norm_two_back = jax.vjp(rms_scale, h_one, ffn_gain)[1]
    grad_h_part, g_ffn_part = norm_two_back(grad_hidden_two)
    grad_h_one = grad_out + lax.psum(grad_h_part, "tensor")
    grad_attn_low = grad_h_one.astype(jnp.bfloat16)
    g_out = jnp.dot(o_low.T, grad_attn_low, preferred_element_type=jnp.float32)
    grad_o_low = jnp.dot(grad_attn_low, wo_full.T, preferred_element_type=jnp.float32).astype(
        jnp.bfloat16
    )
    grad_o_grouped = grad_o_low.reshape(row_count, k_heads, group_size, head_dim).transpose(
        1, 2, 0, 3
    )

    def attend_back(packed):
        q_one, k_one, v_one, total_one, grad_one = packed
        scores = scores_of(q_one, k_one)
        probs = jnp.exp(scores - total_one[..., None])
        grad_probs = jnp.einsum("gid,jd->gij", grad_one, v_one, preferred_element_type=jnp.float32)
        grad_scores = (
            probs * (grad_probs - jnp.sum(probs * grad_probs, axis=-1, keepdims=True))
        ).astype(jnp.bfloat16)
        grad_query = (
            jnp.einsum("gij,jd->gid", grad_scores, k_one, preferred_element_type=jnp.float32)
            * score_scale
        )
        grad_keys = (
            jnp.einsum("gij,gid->jd", grad_scores, q_one, preferred_element_type=jnp.float32)
            * score_scale
        )
        grad_values = jnp.einsum(
            "gij,gid->jd", probs.astype(jnp.bfloat16), grad_one, preferred_element_type=jnp.float32
        )
        return (grad_query, grad_keys, grad_values)

    grad_q_grouped, grad_k_grouped, grad_v_grouped = lax.map(
        attend_back, (q_grouped, k_grouped, v_grouped, log_totals, grad_o_grouped)
    )
    grad_q_rows = grad_q_grouped.transpose(2, 0, 1, 3).reshape(row_count, q_heads, head_dim)
    grad_k_total = grad_k_grouped.transpose(1, 0, 2)
    grad_v_rows = grad_v_grouped.transpose(1, 0, 2).reshape(row_count, k_heads * head_dim)
    grad_q_proj, grad_k_proj, g_query_part, g_key_part = prep_back((grad_q_rows, grad_k_total))
    grad_q_low = grad_q_proj.astype(jnp.bfloat16)
    grad_k_low = grad_k_proj.astype(jnp.bfloat16)
    grad_v_low = grad_v_rows.astype(jnp.bfloat16)
    g_query_w = jnp.dot(hidden_state.T, grad_q_low, preferred_element_type=jnp.float32)
    g_key_w = jnp.dot(hidden_state.T, grad_k_low, preferred_element_type=jnp.float32)
    g_value_w = jnp.dot(hidden_state.T, grad_v_low, preferred_element_type=jnp.float32)
    grad_hidden = (
        jnp.dot(grad_q_low, wq_full.T, preferred_element_type=jnp.float32)
        + jnp.dot(grad_k_low, wk_full.T, preferred_element_type=jnp.float32)
        + jnp.dot(grad_v_low, wv_full.T, preferred_element_type=jnp.float32)
    )
    norm_one_back = jax.vjp(rms_scale, inputs, attn_gain)[1]
    grad_in_part, g_attn_part = norm_one_back(grad_hidden)
    input_grad = grad_h_one + lax.psum(grad_in_part, "tensor")
    g_attn, g_query, g_key, g_ffn = lax.psum(
        (g_attn_part, g_query_part, g_key_part, g_ffn_part), ("dp", "tensor")
    )
    g_query_out, g_key_out, g_value_out, g_out_out, g_gate_out, g_up_out, g_down_out = (
        lax.psum_scatter(g_query_w, "dp", scatter_dimension=0, tiled=True),
        lax.psum_scatter(g_key_w, "dp", scatter_dimension=0, tiled=True),
        lax.psum_scatter(g_value_w, "dp", scatter_dimension=0, tiled=True),
        lax.psum_scatter(g_out, "dp", scatter_dimension=0, tiled=True),
        lax.psum_scatter(g_gate, "dp", scatter_dimension=0, tiled=True),
        lax.psum_scatter(g_up, "dp", scatter_dimension=0, tiled=True),
        lax.psum_scatter(g_down, "dp", scatter_dimension=0, tiled=True),
    )
    return (
        layer_out,
        input_grad,
        g_attn,
        g_query,
        g_key,
        g_query_out,
        g_key_out,
        g_value_out,
        g_out_out,
        g_ffn,
        g_gate_out,
        g_up_out,
        g_down_out,
    )


def solution(mesh):
    placed = (
        P("dp", None),
        P("dp", None),
        P(),
        P(),
        P(),
        P(),
        P("dp", "tensor"),
        P("dp", "tensor"),
        P("dp", "tensor"),
        P(("tensor", "dp"), None),
        P(),
        P("dp", "tensor"),
        P("dp", "tensor"),
        P(("tensor", "dp"), None),
    )
    return jax.shard_map(
        body,
        mesh=mesh,
        in_specs=placed,
        out_specs=(
            P("dp", None),
            P("dp", None),
            P(),
            P(),
            P(),
            P("dp", "tensor"),
            P("dp", "tensor"),
            P("dp", "tensor"),
            P(("tensor", "dp"), None),
            P(),
            P("dp", "tensor"),
            P("dp", "tensor"),
            P(("tensor", "dp"), None),
        ),
        check_vma=False,
    )
```

profile of v0, /device:TPU:0, one launch (start us, length us, event | category | flops | bytes accessed | tf_op | source)
XLA Modules:
  0.0 2440.4 jit_solution(9951994802238308889)
XLA Ops:
  15.6 35.2 %all-gather.10.cloned.1.call-done = bf16[2048,256]{1,0:T(8,128)(2,1)} async-done(((bf16[128,256]{1,0:T(8,128)(2,1)}), bf16[2048,256]{1,0:T(8,128)(2,1)}) %all-gather.10.cloned.1.call-update) | async-done | bytes 1048592 | tf_op jit(solution)/shard_map/all_gather | solution.py:57
  50.8 2.8 multiply_reduce_fusion.9
  54.7 35.2 %all-gather.12.cloned.1.call-done = bf16[2048,256]{1,0:T(8,128)(2,1)} async-done(((bf16[128,256]{1,0:T(8,128)(2,1)}), bf16[2048,256]{1,0:T(8,128)(2,1)}) %all-gather.12.cloned.1.call-update) | async-done | bytes 1048592 | tf_op jit(solution)/shard_map/all_gather | solution.py:58
  89.9 2.9 convolution_convert_fusion.2
  92.8 48.8 %all-gather.8.cloned.1.call-done = bf16[2048,1024]{1,0:T(8,128)(2,1)} async-done(((bf16[128,1024]{1,0:T(8,128)(2,1)}), bf16[2048,1024]{1,0:T(8,128)(2,1)}) %all-gather.8.cloned.1.call-update) | async-done | bytes 4194320 | tf_op jit(solution)/shard_map/all_gather | solution.py:56
  141.6 4.7 multiply_reduce_fusion.6
  147.6 20.5 while.30
  149.6 2.2 fusion.178
  154.7 2.2 fusion.178
  159.8 2.2 fusion.178
  165.0 2.2 fusion.178
  168.2 24.5 %all-gather.14.cloned.1.call-done = bf16[1024,2048]{1,0:T(8,128)(2,1)} async-done(((bf16[64,2048]{1,0:T(8,128)(2,1)}), bf16[1024,2048]{1,0:T(8,128)(2,1)}) %all-gather.14.cloned.1.call-update) | async-done | bytes 4194320 | tf_op jit(solution)/shard_map/all_gather | solution.py:59
  192.7 6.9 fusion.93
  202.8 103.4 %all-reduce.10.cloned.1.call-done = f32[512,2048]{1,0:T(8,128)} async-done(((f32[512,2048]{1,0:T(8,128)}), f32[512,2048]{1,0:T(8,128)}) %all-reduce.10.cloned.1.call-update) | async-done | bytes 4194320 | tf_op jit(solution)/shard_map/psum | solution.py:117
  306.1 2.8 multiply_reduce_fusion.3
  311.4 123.9 %all-gather.16.cloned.1.call-done = bf16[2048,4096]{1,0:T(8,128)(2,1)} async-done(((bf16[128,4096]{1,0:T(8,128)(2,1)}), bf16[2048,4096]{1,0:T(8,128)(2,1)}) %all-gather.16.cloned.1.call-update) | async-done | bytes 16777232 | tf_op jit(solution)/shard_map/all_gather | solution.py:60
  435.3 14.4 fusion.94
  449.7 113.1 %all-gather.18.cloned.1.call-done = bf16[2048,4096]{1,0:T(8,128)(2,1)} async-done(((bf16[128,4096]{1,0:T(8,128)(2,1)}), bf16[2048,4096]{1,0:T(8,128)(2,1)}) %all-gather.18.cloned.1.call-update) | async-done | bytes 16777232 | tf_op jit(solution)/shard_map/all_gather | solution.py:61
  562.7 14.9 fusion.95
  577.6 112.6 %all-gather.20.cloned.1.call-done = bf16[4096,2048]{1,0:T(8,128)(2,1)} async-done(((bf16[256,2048]{1,0:T(8,128)(2,1)}), bf16[4096,2048]{1,0:T(8,128)(2,1)}) %all-gather.20.cloned.1.call-update) | async-done | bytes 16777232 | tf_op jit(solution)/shard_map/all_gather | solution.py:62
  690.2 22.4 multiply_convert_fusion.1
  712.6 14.5 convolution_convert_fusion
  727.2 16.0 fusion.96
  743.2 17.1 multiply_reduce_fusion.1
  760.3 28.1 %all-reduce.12.cloned.1.call-done = bf16[512,2048]{1,0:T(8,128)(2,1)} async-done(((bf16[512,2048]{1,0:T(8,128)(2,1)}), bf16[512,2048]{1,0:T(8,128)(2,1)}) %all-reduce.12.cloned.1.call-update) | async-done | bytes 2097168 | tf_op jit(solution)/shard_map/psum | solution.py:126
  788.4 7.8 add_add_fusion.1
  796.3 107.9 %all-reduce.14.cloned.1.call-done = f32[512,2048]{1,0:T(8,128)} async-done(((f32[512,2048]{1,0:T(8,128)}), f32[512,2048]{1,0:T(8,128)}) %all-reduce.14.cloned.1.call-update) | async-done | bytes 4194320 | tf_op jit(solution)/shard_map/psum | solution.py:142
  904.3 2.9 fusion.70
  908.6 2.4 convolution_convert_fusion.1
  912.0 38.9 %while.31 = (s32[]{:T(128)}, f32[4,4,512,64]{2,3,1,0:T(8,128)}, f32[4,512,64]{1,2,0:T(8,128)}, bf16[4,512,64]{1,2,0:T(8,128)(2,1)}, bf16[4,4,512,64]{2,3,1,0:T(8...) while((s32[]{:T(128)}, f32[4,4,512,64]{2,3,1,0:T(8,128)}, ...), condition=%wide.region_14.15_spmd.clone.clone, body=%wide.region_12.14_spmd.clone.sunk.clone | while | flops 687503360 | bytes 36697768 | solution.py:173
  957.0 2.4 fusion.97
  963.4 2.9 add_add_fusion
  966.4 2.4 fusion.84
  968.8 3.3 fusion.82
  972.4 5.9 fusion.86
  980.2 5.6 fusion.99
  987.5 17.7 fusion.100
  1005.5 17.6 fusion.101
  1024.7 18.3 fusion.72
  1043.7 39.9 %all-reduce.4 = (f32[2048]{0:T(1024)}, f32[64]{0:T(128)}, f32[64]{0:T(128)}, f32[2048]{0:T(1024)}) all-reduce(f32[2048]{0:T(1024)S(1)} %get-tuple-element.152, f32[64]{0:T(128)S(1)} %copy-done.55, f32[64]{0:T(128)S(1)} %get-tuple-element.156, f32[2048]{0:T(1024)S(1)} %copy-done.50), channel_id=1, replica_groups=mesh['dp'=16,'tensor'=2] {'dp','tensor'}, use_global_device_ids=true, to_apply=%region_20.21 | all-reduce | flops 4224 | bytes 33792 | tf_op jit(solution)/shard_map/psum | solution.py:194
  1083.6 7.2 fusion.69
  1090.8 50.2 %reduce-scatter.10.cloned.1.call-done = f32[128,256]{1,0:T(8,128)} async-done(((f32[2048,256]{1,0:T(8,128)}), f32[128,256]{1,0:T(8,128)}) %reduce-scatter.10.cloned.1.call-update) | async-done | bytes 131088 | tf_op jit(solution)/shard_map/reduce_scatter | solution.py:199
  1141.0 65.3 %reduce-scatter.12.cloned.1.call-done = f32[128,256]{1,0:T(8,128)} async-done(((f32[2048,256]{1,0:T(8,128)}), f32[128,256]{1,0:T(8,128)}) %reduce-scatter.12.cloned.1.call-update) | async-done | bytes 131088 | tf_op jit(solution)/shard_map/reduce_scatter | solution.py:200
  1206.3 108.2 %reduce-scatter.8.cloned.1.call-done = f32[128,1024]{1,0:T(8,128)} async-done(((f32[2048,1024]{1,0:T(8,128)}), f32[128,1024]{1,0:T(8,128)}) %reduce-scatter.8.cloned.1.call-update) | async-done | bytes 524304 | tf_op jit(solution)/shard_map/reduce_scatter | solution.py:198
  1314.5 108.8 %reduce-scatter.14.cloned.1.call-done = f32[64,2048]{1,0:T(8,128)} async-done(((f32[1024,2048]{1,0:T(8,128)}), f32[64,2048]{1,0:T(8,128)}) %reduce-scatter.14.cloned.1.call-update) | async-done | bytes 524304 | tf_op jit(solution)/shard_map/reduce_scatter | solution.py:201
  1423.3 337.1 %reduce-scatter.16.cloned.1.call-done = f32[128,4096]{1,0:T(8,128)} async-done(((f32[2048,4096]{1,0:T(8,128)}), f32[128,4096]{1,0:T(8,128)}) %reduce-scatter.16.cloned.1.call-update) | async-done | bytes 2097168 | tf_op jit(solution)/shard_map/reduce_scatter | solution.py:202
  1760.4 336.5 %reduce-scatter.18.cloned.1.call-done = f32[128,4096]{1,0:T(8,128)} async-done(((f32[2048,4096]{1,0:T(8,128)}), f32[128,4096]{1,0:T(8,128)}) %reduce-scatter.18.cloned.1.call-update) | async-done | bytes 2097168 | tf_op jit(solution)/shard_map/reduce_scatter | solution.py:203
  2096.9 336.4 %reduce-scatter.20.cloned.1.call-done = f32[256,2048]{1,0:T(8,128)} async-done(((f32[4096,2048]{1,0:T(8,128)}), f32[256,2048]{1,0:T(8,128)}) %reduce-scatter.20.cloned.1.call-update) | async-done | bytes 2097168 | tf_op jit(solution)/shard_map/reduce_scatter | solution.py:204
  (259 shorter events, 85.3 us)
Async XLA Ops:
  7.2 43.7 %all-gather.10.cloned.1.call-start = ((), (), s32[]{:S(2)}) async-start(), calls=%async_computation.8 | async-start | bytes 1114112 | tf_op jit(solution)/shard_map/all_gather | solution.py:57
  7.9 82.0 %all-gather.12.cloned.1.call-start = ((), (), s32[]{:S(2)}) async-start(), calls=%async_computation.9 | async-start | bytes 1114112 | tf_op jit(solution)/shard_map/all_gather | solution.py:58
  8.7 132.9 %all-gather.8.cloned.1.call-start = ((), (), s32[]{:S(2)}) async-start(), calls=%async_computation.7 | async-start | bytes 4456448 | tf_op jit(solution)/shard_map/all_gather | solution.py:56
  9.4 183.3 %all-gather.14.cloned.1.call-start = ((), (), s32[]{:S(2)}) async-start(), calls=%async_computation.10 | async-start | bytes 4456448 | tf_op jit(solution)/shard_map/all_gather | solution.py:59
  10.0 296.2 %all-reduce.10.cloned.1.call-start = ((), (), s32[]{:S(2)}) async-start(), calls=%async_computation.11 | async-start | bytes 8388608 | tf_op jit(solution)/shard_map/psum | solution.py:117
  11.1 43.4 %copy-start.51 = (f32[64]{0:T(128)S(1)}, f32[64]{0:T(128)}, u32[]{:S(2)}) copy-start(f32[64]{0:T(128)} %param.23) | copy-start | bytes 772
  13.2 76.7 %copy-start.4 = (bf16[512,2048]{1,0:T(8,128)(2,1)S(1)}, bf16[512,2048]{1,0:T(8,128)(2,1)}, u32[]{:S(2)}) copy-start(bf16[512,2048]{1,0:T(8,128)(2,1)} %param.18) | copy-start | bytes 6291460
  13.2 76.7 %copy-start.44 = (f32[2048]{0:T(1024)S(1)}, f32[2048]{0:T(1024)}, u32[]{:S(2)}) copy-start(f32[2048]{0:T(1024)} %param.21) | copy-start | bytes 24580
  13.2 128.3 %copy-start.48 = (f32[512]{0:T(512)}, f32[512]{0:T(512)S(1)}, u32[]{:S(2)}) copy-start(f32[512]{0:T(512)S(1)} %fusion.79) | copy-start | bytes 6148
  15.6 131.2 %copy-start.23 = (f32[512,32]{0,1:T(8,128)}, f32[512,32]{0,1:T(8,128)S(1)}, u32[]{:S(2)}) copy-start(f32[512,32]{0,1:T(8,128)S(1)} %get-tuple-element.215) | copy-start | bytes 196612
  15.6 131.2 %copy-start.25 = (f32[512,32]{0,1:T(8,128)}, f32[512,32]{0,1:T(8,128)S(1)}, u32[]{:S(2)}) copy-start(f32[512,32]{0,1:T(8,128)S(1)} %get-tuple-element.216) | copy-start | bytes 196612
  92.8 53.5 %copy-start.53 = (f32[64]{0:T(128)S(1)}, f32[64]{0:T(128)}, u32[]{:S(2)}) copy-start(f32[64]{0:T(128)} %param.22) | copy-start | bytes 772
  168.2 31.4 %copy-start.6 = (bf16[4,4,512,64]{2,3,1,0:T(8,128)(2,1)}, bf16[4,4,512,64]{2,3,1,0:T(8,128)(2,1)S(1)}, u32[]{:S(2)}) copy-start(bf16[4,4,512,64]{2,3,1,0:T(8,128)(2,1)S(1)} %get-tuple-element.452) | copy-start | bytes 3145732
  168.2 31.4 %copy-start.17 = (bf16[4,512,64]{1,2,0:T(8,128)(2,1)}, bf16[4,512,64]{1,2,0:T(8,128)(2,1)S(1)}, u32[]{:S(2)}) copy-start(bf16[4,512,64]{1,2,0:T(8,128)(2,1)S(1)} %get-tuple-element.465) | copy-start | bytes 786436
  168.2 31.4 %copy-start.39 = (pred[512]{0:T(512)(128)(4,1)}, pred[512]{0:T(512)(128)(4,1)S(1)}, u32[]{:S(2)}) copy-start(pred[512]{0:T(512)(128)(4,1)S(1)} %get-tuple-element.492) | copy-start | bytes 1540
  199.6 235.7 %all-gather.16.cloned.1.call-start = ((), (), s32[]{:S(2)}) async-start(), calls=%async_computation.12 | async-start | bytes 17825792 | tf_op jit(solution)/shard_map/all_gather | solution.py:60
  200.2 362.5 %all-gather.18.cloned.1.call-start = ((), (), s32[]{:S(2)}) async-start(), calls=%async_computation.13 | async-start | bytes 17825792 | tf_op jit(solution)/shard_map/all_gather | solution.py:61
  200.9 489.3 %all-gather.20.cloned.1.call-start = ((), (), s32[]{:S(2)}) async-start(), calls=%async_computation.14 | async-start | bytes 17825792 | tf_op jit(solution)/shard_map/all_gather | solution.py:62
  201.7 586.7 %all-reduce.12.cloned.1.call-start = ((), (), s32[]{:S(2)}) async-start(), calls=%async_computation.15 | async-start | bytes 4194304 | tf_op jit(solution)/shard_map/psum | solution.py:126
  202.7 108.2 %copy-start.41 = (f32[2048]{0:T(1024)S(1)}, f32[2048]{0:T(1024)}, u32[]{:S(2)}) copy-start(f32[2048]{0:T(1024)} %param.28) | copy-start | bytes 24580
  311.4 123.9 %copy-start.19 = (bf16[512,2048]{1,0:T(8,128)(2,1)}, bf16[512,2048]{1,0:T(8,128)(2,1)S(1)}, u32[]{:S(2)}) copy-start(bf16[512,2048]{1,0:T(8,128)(2,1)S(1)} %multiply_convert_fusion.4) | copy-start | bytes 6291460
  449.7 240.6 %copy-start.9 = (bf16[512,2048]{1,0:T(8,128)(2,1)S(1)}, bf16[512,2048]{1,0:T(8,128)(2,1)}, u32[]{:S(2)}) copy-start(bf16[512,2048]{1,0:T(8,128)(2,1)} %param.19) | copy-start | bytes 6291460
  727.2 177.1 %all-reduce.14.cloned.1.call-start = ((), (), s32[]{:S(2)}) async-start(), calls=%async_computation.16 | async-start | bytes 8388608 | tf_op jit(solution)/shard_map/psum | solution.py:142
  727.2 16.0 copy-start.1
  796.2 108.0 %copy-start.10 = (bf16[512,2048]{1,0:T(8,128)(2,1)S(1)}, bf16[512,2048]{1,0:T(8,128)(2,1)}, u32[]{:S(2)}) copy-start(bf16[512,2048]{1,0:T(8,128)(2,1)} %param.19) | copy-start | bytes 6291460
  796.3 287.4 %all-reduce.16.cloned.1.call-start = ((), (), s32[]{:S(2)}) async-start(), calls=%async_computation.17 | async-start | bytes 8388608 | tf_op jit(solution)/shard_map/psum | solution.py:193
  904.3 4.3 copy-start.8
  908.5 3.4 copy-start.7
  908.5 3.4 copy-start.18
  908.5 3.4 copy-start.40
  911.9 38.9 %copy-start.24 = (f32[512,32]{0,1:T(8,128)S(1)}, f32[512,32]{0,1:T(8,128)}, u32[]{:S(2)}) copy-start(f32[512,32]{0,1:T(8,128)} %copy-done.23) | copy-start | bytes 196612
  911.9 38.9 %copy-start.26 = (f32[512,32]{0,1:T(8,128)S(1)}, f32[512,32]{0,1:T(8,128)}, u32[]{:S(2)}) copy-start(f32[512,32]{0,1:T(8,128)} %copy-done.25) | copy-start | bytes 196612
  917.0 2.7 copy-start.32
  926.7 2.7 copy-start.32
  936.5 2.7 copy-start.32
  946.2 2.7 copy-start.32
  950.8 2.2 copy-start.3
  950.8 2.2 copy-start.30
  950.8 2.2 copy-start.54
  954.5 2.5 copy-start.56
  957.0 2.4 copy-start.27
  966.3 174.6 %reduce-scatter.10.cloned.1.call-start = ((), (), s32[]{:S(2)}) async-start(), calls=%async_computation.19 | async-start | bytes 2228224 | tf_op jit(solution)/shard_map/reduce_scatter | solution.py:199
  968.8 237.5 %reduce-scatter.12.cloned.1.call-start = ((), (), s32[]{:S(2)}) async-start(), calls=%async_computation.20 | async-start | bytes 2228224 | tf_op jit(solution)/shard_map/reduce_scatter | solution.py:200
  972.1 342.3 %reduce-scatter.8.cloned.1.call-start = ((), (), s32[]{:S(2)}) async-start(), calls=%async_computation.18 | async-start | bytes 8912896 | tf_op jit(solution)/shard_map/reduce_scatter | solution.py:198
  978.3 445.0 %reduce-scatter.14.cloned.1.call-start = ((), (), s32[]{:S(2)}) async-start(), calls=%async_computation.21 | async-start | bytes 8912896 | tf_op jit(solution)/shard_map/reduce_scatter | solution.py:201
  985.8 774.7 %reduce-scatter.16.cloned.1.call-start = ((), (), s32[]{:S(2)}) async-start(), calls=%async_computation.22 | async-start | bytes 35651584 | tf_op jit(solution)/shard_map/reduce_scatter | solution.py:202
  1005.2 1091.7 %reduce-scatter.18.cloned.1.call-start = ((), (), s32[]{:S(2)}) async-start(), calls=%async_computation.23 | async-start | bytes 35651584 | tf_op jit(solution)/shard_map/reduce_scatter | solution.py:203
  1023.1 1410.2 %reduce-scatter.20.cloned.1.call-start = ((), (), s32[]{:S(2)}) async-start(), calls=%async_computation.24 | async-start | bytes 35651584 | tf_op jit(solution)/shard_map/reduce_scatter | solution.py:204
  (39 other events, 51.5 us)
Sparse Core Ops, SparseCore 0:
  10.2 40.6 all-gather.9
  53.0 36.8 all-gather.11
  92.1 49.4 all-gather.7
  143.6 49.0 all-gather.13
  199.7 106.3 all-reduce.9
  308.4 126.8 all-gather.15
  437.7 124.9 all-gather.17
  565.1 125.0 all-gather.19
  727.3 61.0 all-reduce.11
  796.4 107.8 all-reduce.13
  966.5 108.6 all-reduce.15
  1079.3 61.5 reduce-scatter.9
  1145.7 60.5 reduce-scatter.11
  1210.8 103.6 reduce-scatter.7
  1318.9 104.3 reduce-scatter.13
  1428.0 332.4 reduce-scatter.15
  1765.1 331.7 reduce-scatter.17
  2101.6 331.6 reduce-scatter.19
where the time goes:
time: 2450 us; the launch traced here: 2440 us
  waiting for transfers between devices  2080 us (85%)
  matrix products  235 us (10%)
  other arithmetic  47 us (2%)
  blocking collectives  39.9 us (2%)
    reduce_scatter x1, waiting for transfers between devices, body(): lax.psum_scatter(g_gate, 'dp', scatter_dimension=0, tiled=True)  337 us
    reduce_scatter x1, waiting for transfers between devices, body(): lax.psum_scatter(g_up, 'dp', scatter_dimension=0, tiled=True)  337 us
    reduce_scatter x1, waiting for transfers between devices, body(): lax.psum_scatter(g_down, 'dp', scatter_dimension=0, tiled=True)  336 us
    all_gather x1, waiting for transfers between devices, body(): lax.all_gather(w_gate, 'dp', axis=0, tiled=True)  124 us
    all_gather x1, waiting for transfers between devices, body(): lax.all_gather(w_up, 'dp', axis=0, tiled=True)  113 us
    all_gather x1, waiting for transfers between devices, body(): lax.all_gather(w_down, 'dp', axis=0, tiled=True)  113 us
    reduce_scatter x1, waiting for transfers between devices, body(): lax.psum_scatter(g_out, 'dp', scatter_dimension=0, tiled=True)  109 us
    reduce_scatter x1, waiting for transfers between devices, body(): lax.psum_scatter(g_query_w, 'dp', scatter_dimension=0, tiled=True)  108 us
  transfers between devices with their start and end apart: 18, of which 17 were waited for; matrix products, arithmetic and copies ran while one was open for 7% of the time, Pallas kernels for 0%

commit v1 on v0

v1 whole, which is shorter than its diff:
```python
import math

import jax
import jax.numpy as jnp
from jax import lax
from jax.experimental import pallas as pl
from jax.experimental.pallas import tpu as pltpu
from jax.sharding import PartitionSpec as P

EPS = 1e-05
ROPE_BASE = 1000000.0
MASKED = -1e30
LINE = 4
BF = jnp.bfloat16
F32 = jnp.float32


def rms_scale(values, gain):
    return values * lax.rsqrt(jnp.mean(values * values, axis=-1, keepdims=True) + EPS) * gain


def angles(positions, head_dim):
    half_dim = head_dim // 2
    freq = jnp.exp(
        jnp.arange(half_dim, dtype=jnp.float32) * (-2.0 * math.log(ROPE_BASE) / head_dim)
    )
    turned = positions.astype(jnp.float32)[:, None] * freq[None, :]
    return (jnp.cos(turned)[:, None, :], jnp.sin(turned)[:, None, :])


def rotate(values, cosine, sine_table):
    half_dim = values.shape[-1] // 2
    first_half = values[..., :half_dim]
    second_half = values[..., half_dim:]
    return jnp.concatenate(
        [
            first_half * cosine - second_half * sine_table,
            second_half * cosine + first_half * sine_table,
        ],
        axis=-1,
    )


def mm(left, right):
    return jnp.dot(left, right, preferred_element_type=F32)


def mm_nt(left, right):
    return lax.dot_general(left, right, (((1,), (1,)), ((), ())), preferred_element_type=F32)


def mm_tn(left, right):
    return lax.dot_general(left, right, (((0,), (0,)), ((), ())), preferred_element_type=F32)


def after(done, *values):
    held, _ = lax.optimization_barrier((values, done))
    return held if len(held) > 1 else held[0]


def slot_place(t, k):
    if k == 0:
        return t
    if k == 1:
        return jnp.where(t == 0, 1, t - 1)
    if k == 2:
        return (t + 2) % LINE
    return jnp.where(t == 3, 0, jnp.where(t == 1, 2, 3))


def coordinates():
    n = lax.axis_size("dp")
    inner = n // LINE
    here = lax.axis_index("dp")
    return here // inner, (here % inner) // 2, here % 2, lax.axis_index("tensor")


def place(blocks, spots, shape):
    listed = spots(0, 0, 0, 0)

    def kernel(*refs):
        sources = refs[: len(blocks)]
        out, held, sem, out_sem = refs[len(blocks) :]
        copies = []
        for k, (b, row, col, rows, cols, to_row, to_col) in enumerate(spots(*coordinates())):
            copies.append(
                pltpu.make_async_copy(
                    sources[b].at[pl.ds(row, rows), pl.ds(col, cols)],
                    held.at[
                        pl.ds(pl.multiple_of(to_row, rows), rows),
                        pl.ds(pl.multiple_of(to_col, cols), cols),
                    ],
                    sem.at[k],
                )
            )
        for copy in copies:
            copy.start()
        for copy in copies:
            copy.wait()
        last = pltpu.make_async_copy(held, out, out_sem)
        last.start()
        last.wait()

    item = blocks[0].dtype.itemsize
    moved = sum(2 * rows * cols * item for _, _, _, rows, cols, _, _ in listed)
    return pl.pallas_call(
        kernel,
        out_shape=jax.ShapeDtypeStruct(shape, blocks[0].dtype),
        in_specs=[pl.BlockSpec(memory_space=pl.ANY)] * len(blocks),
        out_specs=pl.BlockSpec(memory_space=pl.ANY),
        scratch_shapes=[
            pltpu.VMEM(shape, blocks[0].dtype),
            pltpu.SemaphoreType.DMA((len(listed),)),
            pltpu.SemaphoreType.DMA,
        ],
        compiler_params=pltpu.CompilerParams(vmem_limit_bytes=moved // 2 + (4 << 20)),
        cost_estimate=pl.CostEstimate(flops=0, bytes_accessed=moved, transcendentals=0),
    )(*blocks)


class Links:
    def __init__(self, n):
        self.n = n
        self.inner = n // LINE
        self.side = self.inner // 2
        self.side_bits = self.side.bit_length() - 1
        self.t, self.j, self.c, self.x = coordinates()

    def core(self, value):
        return lax.ppermute(value, "dp", [(i, i ^ 1) for i in range(self.n)])

    def over(self, value, bit):
        return lax.ppermute(value, "dp", [(i, i ^ (2 << bit)) for i in range(self.n)])

    def cross(self, value):
        return lax.ppermute(value, "tensor", [(0, 1), (1, 0)])

    def along(self, value, moves):
        pairs = [
            (a * self.inner + i, b * self.inner + i) for a, b in moves for i in range(self.inner)
        ]
        return lax.ppermute(value, "dp", pairs)

    def right(self, value, senders):
        return self.along(value, [(a, a + 1) for a in senders])

    def left(self, value, senders):
        return self.along(value, [(a, a - 1) for a in senders])

    def turn(self, value, shift):
        return self.along(value, [(a, (a + shift) % LINE) for a in range(LINE)])

    def line_gather(self, value):
        t = self.t
        r1 = self.right(value, (0, 1, 2))
        l1 = self.left(value, (1, 2, 3))
        r2 = self.right(r1, (1, 2))
        l2 = self.left(l1, (1, 2))
        r3 = self.right(r2, (2,))
        l3 = self.left(l2, (1,))
        return (
            value,
            jnp.where(t == 0, l1, r1),
            jnp.where(t < 2, l2, r2),
            jnp.where(t == 0, l3, jnp.where(t == 3, r3, l1)),
        )

    def line_scatter(self, parts):
        t = self.t
        p0, p1, p2, p3 = parts
        first = p3.astype(BF)
        r1 = self.right(first, (0,))
        l1 = self.left(first, (3,))
        second = (p2 + r1.astype(F32) + l1.astype(F32)).astype(BF)
        r2 = self.right(second, (0, 1))
        l2 = self.left(second, (2, 3))
        r3 = self.right((jnp.where(t == 0, p1, p3) + r2.astype(F32)).astype(BF), (0, 1, 2))
        l3 = self.left((p1 + l2.astype(F32)).astype(BF), (1, 2, 3))
        return p0 + r3.astype(F32) + l3.astype(F32)

    def line_send(self, parts):
        p0, p1, p2, p3 = parts
        first, second, third = p1.astype(BF), p2.astype(BF), p3.astype(BF)
        got = [
            self.left(first, (1, 2, 3)),
            self.right(first, (0,)),
            self.turn(second, 2),
            self.along(third, ((0, 3), (3, 0))),
            self.right(third, (1, 2)),
        ]
        return p0 + sum(g.astype(F32) for g in got)

    def side_all(self, value):
        blocks = [value]
        for bit in range(self.side_bits):
            blocks += [self.over(block, bit) for block in blocks]
        return blocks

    def side_sum(self, blocks):
        for bit in reversed(range(self.side_bits)):
            width = 1 << bit
            blocks = [
                a.astype(F32) + self.over(b.astype(BF), bit).astype(F32)
                for a, b in zip(blocks[:width], blocks[width:])
            ]
        return blocks[0]

    def pair_order(self, mine, other, where):
        low = jnp.where(where == 0, mine, other)
        high = jnp.where(where == 0, other, mine)
        return jnp.concatenate([low, high], 0)

    def pick(self, value, index, axis):
        return lax.dynamic_index_in_dim(value, index, axis, keepdims=False)

    def cross_sum(self, value, axis):
        kept = self.pick(value, self.x, axis)
        sent = self.pick(value, 1 - self.x, axis)
        return kept.astype(F32) + self.cross(sent.astype(BF)).astype(F32)

    def gather_rows(self, blocks):
        rows, cols = blocks[0].shape
        pieces, where = [], []
        for k, block in enumerate(blocks):
            for r, piece in enumerate(self.side_all(block)):
                pieces += [piece, self.core(piece)]
                where += [(k, r, 0), (k, r, 1)]

        def spots(t, j, c, x):
            return [
                (
                    i, 0, 0, rows, cols,
                    (((slot_place(t, k) * self.side) + (j ^ r)) * 2 + (c ^ s)) * rows, 0,
                )
                for i, (k, r, s) in enumerate(where)
            ]

        return place(pieces, spots, (self.n * rows, cols))

    def sum_rows(self, value):
        rows, cols = value.shape[0] // self.n, value.shape[1]
        parts = value.reshape(LINE, self.side, 2, rows, cols)
        kept = self.pick(parts, self.c, 2).astype(F32)
        parts = kept + self.core(self.pick(parts, 1 - self.c, 2)).astype(F32)
        parts = parts.astype(BF)
        parts = self.side_sum([self.pick(parts, self.j ^ r, 1) for r in range(self.side)])
        return self.line_scatter(
            [self.pick(parts, slot_place(self.t, k), 0).astype(F32) for k in range(LINE)]
        )

    def total(self, value):
        value = value + self.core(value)
        for bit in range(self.side_bits):
            value = value + self.over(value, bit)
        value = value + self.cross(value)
        value = value + self.along(value, ((0, 1), (1, 0), (2, 3), (3, 2)))
        return value + self.turn(value, 2)


def make_body(n):
    def body(
        tokens,
        cotangent,
        lengths,
        attn_gain,
        query_gain,
        key_gain,
        w_query,
        key_weight_matrix,
        value_weight_matrix,
        w_out,
        ffn_gain,
        w_gate,
        w_up,
        w_down,
    ):
        net = Links(n)
        t, j, c, x = net.t, net.j, net.c, net.x
        row_count, width = tokens.shape
        half = row_count // 2
        head_dim = query_gain.shape[0]
        q_cols = w_query.shape[1]
        k_cols = key_weight_matrix.shape[1]
        q_heads = q_cols // head_dim
        k_heads = k_cols // head_dim
        group_size = q_heads // k_heads
        score_scale = 1.0 / math.sqrt(head_dim)
        dp_index = lax.axis_index("dp")
        slot_length = lengths[dp_index]

        depth = w_gate.shape[0]
        piece = w_down.shape[0]
        side = net.side
        strip = side * piece
        qkv_own = jnp.concatenate([w_query, key_weight_matrix, value_weight_matrix], axis=1)
        qkv_blocks = net.line_gather(qkv_own)
        qkv_full = net.gather_rows(qkv_blocks)
        wo_blocks = net.line_gather(after(qkv_blocks, w_out))
        wo_full = net.gather_rows(wo_blocks)

        strips = []
        for weight in (w_gate, w_up):
            cols = weight.reshape(depth, LINE, side, 2, piece)
            strips.append(
                [
                    net.pick(cols, place_c, 3).transpose(1, 0, 2, 3).reshape(LINE, depth, strip)
                    for place_c in (c, 1 - c)
                ]
            )
        kept = jnp.stack([strips[0][0], strips[1][0]], 1)
        sent = jnp.stack([strips[0][1], strips[1][1]], 1)
        pairs = jnp.stack([kept, net.core(sent)], 1)
        pairs = after(qkv_blocks, pairs)
        pieces, where = [], []
        turned = []
        for shift in range(LINE):
            block = net.pick(pairs, (t + shift) % LINE, 0)
            block = block if shift == 0 else net.turn(block, shift)
            turned.append(block)
            gate_part = block[:, 0].reshape(2 * depth, strip)
            up_part = block[:, 1].reshape(2 * depth, strip)
            for kind, over_x in ((0, (gate_part, net.cross(gate_part))), (1, (up_part,))):
                for at_x, part in enumerate(over_x):
                    for r, got in enumerate(net.side_all(part)):
                        pieces.append(got)
                        where.append((kind, shift, r, at_x))
                        if kind == 1:
                            pieces.append(net.cross(got))
                            where.append((kind, shift, r, 1))

        def unit_weight(wanted):
            chosen = [(p, w) for p, w in zip(pieces, where) if w[0] == wanted]

            def spots(t, j, c, x):
                return [
                    (
                        i, s * depth, 0, depth, strip,
                        ((((t - shift) % LINE) * side + (j ^ r)) * 2 + (c ^ s)) * depth,
                        (x ^ at_x) * strip,
                    )
                    for i, (_, (_, shift, r, at_x)) in enumerate(chosen)
                    for s in range(2)
                ]

            return place([p for p, _ in chosen], spots, (width, 2 * strip))

        wg = unit_weight(0)
        wu = unit_weight(1)
        down_pieces = []
        for got in net.side_all(w_down):
            down_pieces += [got, net.cross(got)]

        def down_spots(t, j, c, x):
            return [
                (2 * r + s, 0, 0, piece, width, ((x ^ s) * side + (j ^ r)) * piece, 0)
                for r in range(side)
                for s in range(2)
            ]

        wd = place(down_pieces, down_spots, (2 * strip, width))

        positions = jnp.arange(row_count, dtype=jnp.int32)
        start = x * half
        half_positions = start + jnp.arange(half, dtype=jnp.int32)
        half_valid = (half_positions < slot_length)[:, None]
        grad_half = lax.dynamic_slice_in_dim(cotangent, start, half, 0)
        grad_half = jnp.where(half_valid, grad_half, jnp.zeros_like(grad_half))
        grad_blocks = [
            jnp.concatenate([block, net.core(block)], axis=0)
            for block in net.line_gather(after(turned, grad_half))
        ]

        allowed = (positions[None, :] <= positions[:, None]) & (positions[None, :] < slot_length)
        cosine, sine_table = angles(positions, head_dim)
        inputs = tokens.astype(F32)
        hidden_state = rms_scale(inputs, attn_gain).astype(BF)
        qkv = mm(hidden_state, qkv_full)
        q_proj = qkv[:, :q_cols]
        key_projected = qkv[:, q_cols : q_cols + k_cols]
        value_projected = qkv[:, q_cols + k_cols :]

        def prepare(q_vals, k_vals, q_gain, k_gain):
            q_norm = rms_scale(q_vals.reshape(row_count, q_heads, head_dim), q_gain)
            k_norm = rms_scale(k_vals.reshape(row_count, k_heads, head_dim), k_gain)
            return (rotate(q_norm, cosine, sine_table), rotate(k_norm, cosine, sine_table))

        (q_rot, k_rot), prep_back = jax.vjp(prepare, q_proj, key_projected, query_gain, key_gain)
        q_low = q_rot.astype(BF)
        k_low = k_rot.astype(BF)
        v_low = value_projected.astype(BF)
        q_grouped = q_low.reshape(row_count, k_heads, group_size, head_dim).transpose(1, 2, 0, 3)
        k_grouped = k_low.transpose(1, 0, 2)
        v_grouped = v_low.reshape(row_count, k_heads, head_dim).transpose(1, 0, 2)

        def scores_of(q_one, k_one):
            scores = (
                jnp.einsum("gid,jd->gij", q_one, k_one, preferred_element_type=F32) * score_scale
            )
            return jnp.where(allowed[None], scores, MASKED)

        def attend(packed):
            q_one, k_one, v_one = packed
            scores = scores_of(q_one, k_one)
            row_max = jnp.max(scores, axis=-1, keepdims=True)
            exp_scores = jnp.exp(scores - row_max)
            row_total = jnp.sum(exp_scores, axis=-1, keepdims=True)
            probs = (exp_scores / row_total).astype(BF)
            attended = jnp.einsum("gij,jd->gid", probs, v_one, preferred_element_type=F32)
            return (attended, row_max[..., 0] + jnp.log(row_total[..., 0]))

        attended, log_totals = lax.map(attend, (q_grouped, k_grouped, v_grouped))
        o_low = (
            attended.transpose(2, 0, 1, 3).reshape(row_count, q_heads * head_dim).astype(BF)
        )
        attn_part = mm(o_low, wo_full).reshape(2, half, width)
        input_half = lax.dynamic_slice_in_dim(inputs, start, half, 0)
        h_one = input_half + net.cross_sum(attn_part, 0)
        hidden_two = rms_scale(h_one, ffn_gain).astype(BF)

        hidden_blocks = [
            jnp.concatenate([block, net.core(block)], axis=0)
            for block in net.line_gather(hidden_two)
        ]

        def core_sum(value):
            low = value[half:].astype(BF)
            return value[:half] + net.core(low).astype(F32)

        out_parts, grad_parts, acts, grad_gates, grad_ups = [], [], [], [], []
        for hidden, grad in zip(hidden_blocks, grad_blocks):
            gate = mm(hidden, wg)
            up_proj = mm(hidden, wu)
            sigmoid_gate = jax.nn.sigmoid(gate)
            silu_gate = gate * sigmoid_gate
            act = (silu_gate * up_proj).astype(BF)
            out_parts.append(core_sum(mm(act, wd)))
            grad_act = mm_nt(grad, wd)
            silu_slope = sigmoid_gate * (1.0 + gate * (1.0 - sigmoid_gate))
            grad_gate = (grad_act * up_proj * silu_slope).astype(BF)
            grad_up = (grad_act * silu_gate).astype(BF)
            grad_parts.append(core_sum(mm_nt(grad_gate, wg) + mm_nt(grad_up, wu)))
            acts.append(act)
            grad_gates.append(grad_gate)
            grad_ups.append(grad_up)

        grad_hidden_two = net.line_send(grad_parts)
        out_parts = after(grad_hidden_two, *out_parts)
        layer_half = (h_one + net.line_scatter(out_parts)).astype(BF)
        layer_out = net.pair_order(layer_half, net.cross(layer_half), x)
        norm_two_back = jax.vjp(rms_scale, h_one, ffn_gain)[1]
        grad_h_part, g_ffn_part = norm_two_back(grad_hidden_two)
        grad_h_one = grad_half.astype(F32) + grad_h_part
        grad_attn_half = grad_h_one.astype(BF)
        grad_attn_low = net.pair_order(grad_attn_half, net.cross(grad_attn_half), x)

        act_all = jnp.concatenate(acts, 0)
        hidden_all = jnp.concatenate(hidden_blocks, 0)
        grad_all = jnp.concatenate(grad_blocks, 0)
        g_gate = mm_tn(hidden_all, jnp.concatenate(grad_gates, 0)).astype(BF)
        g_up = mm_tn(hidden_all, jnp.concatenate(grad_ups, 0)).astype(BF)
        g_down = mm_tn(act_all, grad_all).astype(BF)

        def home_units(value):
            rows = value.reshape(LINE, 2 * depth, strip)
            blocks = []
            for shift in range(LINE):
                block = net.pick(rows, (t + shift) % LINE, 0)
                block = block if shift == 0 else net.turn(block, shift)
                block = block.reshape(2, depth, strip)
                blocks.append(net.pick(block, c, 0))
                blocks.append(net.core(net.pick(block, 1 - c, 0)))
            if piece % 128:
                stacked = jnp.stack(blocks).reshape(LINE, 2, depth, side, piece)
                order_t = (t - jnp.arange(LINE)) % LINE
                stacked = jnp.take(stacked, order_t, axis=0)
                stacked = jnp.take(stacked, c ^ jnp.arange(2), axis=1)
                return stacked.transpose(2, 0, 3, 1, 4).reshape(depth, LINE * 2 * strip)

            def spots(t, j, c, x):
                return [
                    (
                        2 * shift + s, 0, r * piece, depth, piece, 0,
                        ((((t - shift) % LINE) * side + r) * 2 + (c ^ s)) * piece,
                    )
                    for shift in range(LINE)
                    for s in range(2)
                    for r in range(side)
                ]

            return place(blocks, spots, (depth, LINE * 2 * strip))

        def side_rows(value):
            rows = value.reshape(LINE, side, 2 * depth, value.shape[1])
            return [net.pick(rows, j ^ r, 1) for r in range(side)]

        def cross_cols(value):
            kept = lax.dynamic_slice_in_dim(value, x * strip, strip, value.ndim - 1)
            sent = lax.dynamic_slice_in_dim(value, (1 - x) * strip, strip, value.ndim - 1)
            return kept.astype(F32) + net.cross(sent.astype(BF)).astype(F32)

        gate_sum = net.side_sum(side_rows(cross_cols(g_gate).astype(BF))).astype(BF)
        up_sum = cross_cols(net.side_sum(side_rows(g_up))).astype(BF)
        g_gate_out = home_units(gate_sum).astype(F32)
        g_up_out = home_units(up_sum).astype(F32)
        down_sum = net.cross_sum(g_down.reshape(2, side, piece, width), 0).astype(BF)
        g_down_out = net.side_sum([net.pick(down_sum, j ^ r, 0) for r in range(side)])

        g_out = mm_tn(o_low, grad_attn_low).astype(BF)
        grad_o_low = mm_nt(grad_attn_low, wo_full).astype(BF)
        grad_o_grouped = grad_o_low.reshape(row_count, k_heads, group_size, head_dim).transpose(
            1, 2, 0, 3
        )

        def attend_back(packed):
            q_one, k_one, v_one, total_one, grad_one = packed
            scores = scores_of(q_one, k_one)
            probs = jnp.exp(scores - total_one[..., None])
            grad_probs = jnp.einsum("gid,jd->gij", grad_one, v_one, preferred_element_type=F32)
            grad_scores = (
                probs * (grad_probs - jnp.sum(probs * grad_probs, axis=-1, keepdims=True))
            ).astype(BF)
            grad_query = (
                jnp.einsum("gij,jd->gid", grad_scores, k_one, preferred_element_type=F32)
                * score_scale
            )
            grad_keys = (
                jnp.einsum("gij,gid->jd", grad_scores, q_one, preferred_element_type=F32)
                * score_scale
            )
            grad_values = jnp.einsum(
                "gij,gid->jd", probs.astype(BF), grad_one, preferred_element_type=F32
            )
            return (grad_query, grad_keys, grad_values)

        grad_q_grouped, grad_k_grouped, grad_v_grouped = lax.map(
            attend_back, (q_grouped, k_grouped, v_grouped, log_totals, grad_o_grouped)
        )
        grad_q_rows = grad_q_grouped.transpose(2, 0, 1, 3).reshape(row_count, q_heads, head_dim)
        grad_k_total = grad_k_grouped.transpose(1, 0, 2)
        grad_v_rows = grad_v_grouped.transpose(1, 0, 2).reshape(row_count, k_heads * head_dim)
        grad_q_proj, grad_k_proj, g_query_part, g_key_part = prep_back((grad_q_rows, grad_k_total))
        grad_qkv = jnp.concatenate(
            [grad_q_proj.astype(BF), grad_k_proj.astype(BF), grad_v_rows.astype(BF)], axis=1
        )
        g_qkv = mm_tn(hidden_state, grad_qkv).astype(BF)
        g_out_out = net.sum_rows(g_out)
        g_qkv_out = net.sum_rows(g_qkv)
        grad_hidden = mm_nt(grad_qkv, qkv_full).reshape(2, half, width)
        grad_hidden_half = net.cross_sum(grad_hidden, 0)
        norm_one_back = jax.vjp(rms_scale, input_half, attn_gain)[1]
        grad_in_half, g_attn_part = norm_one_back(grad_hidden_half)
        input_grad_half = (grad_h_one + grad_in_half).astype(BF)
        input_grad = net.pair_order(input_grad_half, net.cross(input_grad_half), x).astype(F32)
        small = jnp.concatenate([g_attn_part, g_ffn_part, g_query_part, g_key_part])
        small = net.total(small)
        return (
            layer_out,
            input_grad,
            small[:width],
            small[2 * width : 2 * width + head_dim],
            small[2 * width + head_dim :],
            g_qkv_out[:, :q_cols],
            g_qkv_out[:, q_cols : q_cols + k_cols],
            g_qkv_out[:, q_cols + k_cols :],
            g_out_out,
            small[width : 2 * width],
            g_gate_out,
            g_up_out,
            g_down_out,
        )

    return body


def solution(mesh):
    placed = (
        P("dp", None),
        P("dp", None),
        P(),
        P(),
        P(),
        P(),
        P("dp", "tensor"),
        P("dp", "tensor"),
        P("dp", "tensor"),
        P(("tensor", "dp"), None),
        P(),
        P("dp", "tensor"),
        P("dp", "tensor"),
        P(("tensor", "dp"), None),
    )
    return jax.shard_map(
        make_body(mesh.shape["dp"]),
        mesh=mesh,
        in_specs=placed,
        out_specs=(
            P("dp", None),
            P("dp", None),
            P(),
            P(),
            P(),
            P("dp", "tensor"),
            P("dp", "tensor"),
            P("dp", "tensor"),
            P(("tensor", "dp"), None),
            P(),
            P("dp", "tensor"),
            P("dp", "tensor"),
            P(("tensor", "dp"), None),
        ),
        check_vma=False,
    )
```

time: 2450 us -> 1000 us (0.41)
  waiting for transfers between devices: 2080 us -> 371 us
  starting transfers between devices: 1.45 us -> 200 us
  local copies, waits for them, and re-layouts: 22 us -> 98.1 us
  other arithmetic: 47 us -> 105 us
  blocking collectives: 39.9 us -> 0 us
  matrix products: 235 us -> 200 us
    reduce_scatter x7 -> x0, waiting for transfers between devices: 1340 us -> none  [the longest x1 337 us: body(): lax.psum_scatter(g_gate, 'dp', scatter_dimension=0, tiled=True)]
    all_gather x7 -> x0, waiting for transfers between devices: 493 us -> none  [the longest x1 124 us: body(): lax.all_gather(w_gate, 'dp', axis=0, tiled=True)]
    ppermute x0 -> x152, waiting for transfers between devices: none -> 371 us  [the longest x58 226 us: along(): return lax.ppermute(value, 'dp', pairs)]
    psum x4 -> x0, waiting for transfers between devices: 239 us -> none  [the longest x1 108 us: body(): grad_h_one = grad_out + lax.psum(grad_h_part, 'tensor')]
    ppermute x0 -> x152, starting transfers between devices: none -> 200 us  [the longest x58 140 us: along(): return lax.ppermute(value, 'dp', pairs)]
    psum x1 -> x0, blocking collectives: 39.9 us -> none  [body(): lax.psum((g_attn_part, g_query_part, g_key_part, g_ffn_part), ('dp', 'ten...]
    dot_general x49 -> x61, matrix products: 235 us -> 200 us  [the longest x14 51 us: mm(): return jnp.dot(left, right, preferred_element_type=F32)]
    convert_element_type x5 -> x24, other arithmetic: 4.74 us -> 29.8 us  [the longest x1 4.13 us: body(): inputs = tokens.astype(F32)]
  transfers between devices with their start and end apart: 18 -> 152, of which waited for: 17 -> 42; matrix products, arithmetic and copies ran while one was open for 7% -> 38% of each run, Pallas kernels for 0% -> 1%
where the time goes in v1:
time: 1000 us; the launch traced here: 992 us
  waiting for transfers between devices  371 us (37%)
  starting transfers between devices  200 us (20%)
  matrix products  200 us (20%)
  other arithmetic  105 us (10%)
  local copies, waits for them, and re-layouts  98.1 us (10%)
  Pallas kernels  13.7 us (1%)
    ppermute x58, waiting for transfers between devices, along(): return lax.ppermute(value, 'dp', pairs)  226 us
    ppermute x58, starting transfers between devices, along(): return lax.ppermute(value, 'dp', pairs)  140 us
    ppermute x23, waiting for transfers between devices, cross(): return lax.ppermute(value, 'tensor', [(0, 1), (1, 0)])  92.8 us
    ppermute x27, waiting for transfers between devices, over(): return lax.ppermute(value, 'dp', [(i, i ^ 2 << bit) for i in range(self.n)])  51.5 us
    dot_general x14, matrix products, mm(): return jnp.dot(left, right, preferred_element_type=F32)  51 us
    dot_general x14, matrix products, mm_nt(): lax.dot_general(left, right, (((1,), (1,)), ((), ())), preferred_element_...  50.2 us
    dot_general x5, matrix products, mm_tn(): lax.dot_general(left, right, (((0,), (0,)), ((), ())), preferred_element_...  49.7 us
    unnamed x341, local copies, waits for them, and re-layouts  30.7 us
  transfers between devices with their start and end apart: 152, of which 42 were waited for; matrix products, arithmetic and copies ran while one was open for 38% of the time, Pallas kernels for 1%

profile of v1, /device:TPU:0, one launch (start us, length us, event | category | flops | bytes accessed | tf_op | source)
XLA Modules:
  0.0 992.0 jit_solution(3350147975467617798)
XLA Ops:
  4.6 6.3 collective-permute-start.4
  27.8 8.7 collective-permute-done.8
  42.1 6.4 collective-permute-done.13
  57.5 5.1 collective-permute-start.22
  81.0 16.7 %collective-permute-done.46 = bf16[2,2,128,512]{3,2,1,0:T(8,128)(2,1)} collective-permute-done((bf16[2,2,128,512]{3,2,1,0:T(8,128)(2,1)}, bf16[2,2,128,512]{3,2,1,0:T(8,128)(2,1)}, u32[]{:S(2)}, u32[]{:S(2)}) %collective-permute-start.46) | collective-permute-done | bytes 524320 | tf_op jit(solution)/shard_map/ppermute | solution.py:142
  102.0 9.5 collective-permute-done.16.refs_14_
  111.5 6.8 collective-permute-done.6.refs_6_
  123.0 5.9 collective-permute-done.31
  182.9 23.3 %collective-permute-done.44.refs_6_ = bf16[256,512]{1,0:T(8,128)(2,1)} collective-permute-done((bf16[256,512]{1,0:T(8,128)(2,1)S(1)}, bf16[256,512]{1,0:T(8,128)(2,1)}, u32[]{:S(2)}, u32[]{:S(2)}) %collective-permute-start.44) | collective-permute-done | bytes 262176 | tf_op jit(solution)/shard_map/ppermute | solution.py:136
  226.0 5.1 collective-permute-done.62.refs_11_
  248.4 5.2 collective-permute-done.53.refs_15_
  253.6 25.6 %while.30 = (s32[]{:T(128)}, bf16[4,4,512,64]{2,3,1,0:T(8,128)(2,1)}, f32[4,4,512]{2,1,0:T(4,128)}, bf16[4,4,512,64]{2,3,1,0:T(8,128)(2,1)}, bf16[4,512,64]{1,2,...) while((s32[]{:T(128)}, bf16[4,4,512,64]{2,3,1,0:T(8,128)(2,1)}, ...), condition=%wide.region_6.7_spmd.clone.clone, body=%wide.region_3.6_spmd.clone.sunk.clone | while | flops 281540608 | bytes 14617677 | solution.py:411
  292.4 4.6 collective-permute-start.85
  305.9 12.7 %collective-permute-done.84 = bf16[256,2048]{1,0:T(8,128)(2,1)S(1)} collective-permute-done((bf16[256,2048]{1,0:T(8,128)(2,1)S(1)}, bf16[256,2048]{1,0:T(8,128)(2,1)S(1)}, u32[]{:S(2)}, u32[]{:S(2)}) %collective-permute-start.84) | collective-permute-done | bytes 1048608 | tf_op jit(solution)/shard_map/ppermute | solution.py:142
  323.5 4.9 fusion.106
  331.6 8.7 collective-permute-start.71
  341.5 8.3 collective-permute-done.90
  358.2 14.1 %collective-permute-done.70 = bf16[256,2048]{1,0:T(8,128)(2,1)S(1)} collective-permute-done((bf16[256,2048]{1,0:T(8,128)(2,1)S(1)}, bf16[256,2048]{1,0:T(8,128)(2,1)S(1)}, u32[]{:S(2)}, u32[]{:S(2)}) %collective-permute-start.70) | collective-permute-done | bytes 1048608 | tf_op jit(solution)/shard_map/ppermute | solution.py:142
  376.7 6.5 multiply_convert_fusion.9
  406.3 17.8 %collective-permute-done.74 = bf16[256,2048]{1,0:T(8,128)(2,1)S(1)} collective-permute-done((bf16[256,2048]{1,0:T(8,128)(2,1)S(1)}, bf16[256,2048]{1,0:T(8,128)(2,1)S(1)}, u32[]{:S(2)}, u32[]{:S(2)}) %collective-permute-start.74) | collective-permute-done | bytes 1048608 | tf_op jit(solution)/shard_map/ppermute | solution.py:142
  429.4 5.3 multiply_convert_fusion.7
  448.6 5.2 fusion.118
  459.9 13.3 %collective-permute-done.78 = bf16[256,2048]{1,0:T(8,128)(2,1)S(1)} collective-permute-done((bf16[256,2048]{1,0:T(8,128)(2,1)S(1)}, bf16[256,2048]{1,0:T(8,128)(2,1)S(1)}, u32[]{:S(2)}, u32[]{:S(2)}) %collective-permute-start.78) | collective-permute-done | bytes 1048608 | tf_op jit(solution)/shard_map/ppermute | solution.py:142
  479.5 5.2 multiply_convert_fusion.5
  499.9 5.2 multiply_convert_fusion.3
  509.6 12.3 %fusion.89 = bf16[2048,1024]{1,0:T(8,128)(2,1)S(1)} fusion(bf16[2048,2048]{1,0:T(8,128)(2,1)S(1)} %constant_dynamic-update-slice_fusion.3, bf16[512,1024]{1,0:T(8,128)(2,1)} %copy-done.153, bf16[512,1024]{1,0:T(8,128)(2,1)} %copy-done.152, bf16[512,1024]{1,0:T(8,128)(2,1)} %copy-done.151, bf16[512,1024]{1,0:T(8,128)(2,1)} %copy-done.150), kind=kOutput, calls=%fused_computation.102 | convolution fusion | flops 8608808960 | bytes 16777216 | tf_op jit(solution)/shard_map/dot_general | solution.py:53
  521.9 13.2 %fusion.92 = bf16[2048,1024]{1,0:T(8,128)(2,1)S(1)} fusion(bf16[2048,2048]{1,0:T(8,128)(2,1)} %copy-done.121, bf16[512,1024]{1,0:T(8,128)(2,1)} %get-tuple-element.241, bf16[512,1024]{1,0:T(8,128)(2,1)} %get-tuple-element.238, bf16[512,1024]{1,0:T(8,128)(2,1)} %get-tuple-element.235, bf16[512,1024]{1,0:T(8,128)(2,1)} %get-tuple-element.232), kind=kOutput, calls=%fused_computation.103 | convolution fusion | flops 8608808960 | bytes 16777216 | tf_op jit(solution)/shard_map/dot_general | solution.py:53
  535.2 13.6 %fusion.95 = bf16[1024,2048]{1,0:T(8,128)(2,1)S(1)} fusion(bf16[2048,2048]{1,0:T(8,128)(2,1)} %constant_dynamic-update-slice_fusion.11, bf16[512,1024]{1,0:T(8,128)(2,1)} %get-tuple-element.243, bf16[512,1024]{1,0:T(8,128)(2,1)} %get-tuple-element.240, bf16[512,1024]{1,0:T(8,128)(2,1)} %get-tuple-element.237, bf16[512,1024]{1,0:T(8,128)(2,1)} %get-tuple-element.234), kind=kOutput, calls=%fused_computation.104 | convolution fusion | flops 8608808960 | bytes 16777216 | tf_op jit(solution)/shard_map/dot_general | solution.py:53
  548.8 5.0 convolution_add_fusion
  564.0 4.4 collective-permute-start.99
  575.6 54.0 %collective-permute-done.94 = bf16[256,2048]{1,0:T(8,128)(2,1)} collective-permute-done((bf16[256,2048]{1,0:T(8,128)(2,1)S(1)}, bf16[256,2048]{1,0:T(8,128)(2,1)}, u32[]{:S(2)}, u32[]{:S(2)}) %collective-permute-start.94) | collective-permute-done | bytes 1048608 | tf_op jit(solution)/shard_map/ppermute | solution.py:142
  631.4 4.7 multiply_reduce_fusion.3
  637.2 23.3 %collective-permute-start.101 = (bf16[256,2048]{1,0:T(8,128)(2,1)}, bf16[256,2048]{1,0:T(8,128)(2,1)}, u32[]{:S(2)}, u32[]{:S(2)}) collective-permute-start(bf16[256,2048]{1,0:T(8,128)(2,1)} %convert_element_type.473), channel_id=1, source_target_pairs={{0,8},{2,10},{4,12},{6,14},{1,9},{3,11},{5,13},{7,15}} | collective-permute-start | bytes 3145736 | tf_op jit(solution)/shard_map/ppermute | solution.py:142
  671.7 6.8 collective-permute-done.132
  682.1 18.8 %collective-permute-done.108 = bf16[256,2048]{1,0:T(8,128)(2,1)S(1)} collective-permute-done((bf16[256,2048]{1,0:T(8,128)(2,1)S(1)}, bf16[256,2048]{1,0:T(8,128)(2,1)S(1)}, u32[]{:S(2)}, u32[]{:S(2)}) %collective-permute-start.108) | collective-permute-done | bytes 1048608 | tf_op jit(solution)/shard_map/ppermute | solution.py:136
  708.6 38.7 %while.31 = (s32[]{:T(128)}, f32[4,4,512,64]{2,3,1,0:T(8,128)}, f32[4,512,64]{1,2,0:T(8,128)}, bf16[4,512,64]{1,2,0:T(8,128)(2,1)}, bf16[4,4,512,64]{2,3,1,0:T(8...) while((s32[]{:T(128)}, f32[4,4,512,64]{2,3,1,0:T(8,128)}, ...), condition=%wide.region_11.12_spmd.clone.clone, body=%wide.region_9.11_spmd.clone.sunk.clone | while | flops 687503360 | bytes 38794884 | solution.py:535
  753.1 4.4 fusion.145
  771.3 7.0 convolution_convert_fusion
  787.6 11.6 %collective-permute-done.146 = bf16[256,512]{1,0:T(8,128)(2,1)S(1)} collective-permute-done((bf16[256,512]{1,0:T(8,128)(2,1)S(1)}, bf16[256,512]{1,0:T(8,128)(2,1)S(1)}, u32[]{:S(2)}, u32[]{:S(2)}) %collective-permute-start.146) | collective-permute-done | bytes 262176 | tf_op jit(solution)/shard_map/ppermute | solution.py:142
  811.1 6.4 collective-permute-done.137
  824.6 8.8 collective-permute-start.103
  849.0 7.2 collective-permute-done.103
  857.9 6.2 collective-permute-start.104
  867.5 22.6 %collective-permute-done.115 = f32[4224]{0:T(1024)S(1)} collective-permute-done((f32[4224]{0:T(1024)S(1)}, f32[4224]{0:T(1024)S(1)}, u32[]{:S(2)}, u32[]{:S(2)}) %collective-permute-start.115) | collective-permute-done | bytes 16928 | tf_op jit(solution)/shard_map/ppermute | solution.py:142
  897.7 15.9 %collective-permute-done.125 = bf16[4,64,2048]{2,1,0:T(8,128)(2,1)S(1)} collective-permute-done((bf16[4,64,2048]{2,1,0:T(8,128)(2,1)S(1)}, bf16[4,64,2048]{2,1,0:T(8,128)(2,1)S(1)}, u32[]{:S(2)}, u32[]{:S(2)}) %collective-permute-start.125) | collective-permute-done | bytes 1048608 | tf_op jit(solution)/shard_map/ppermute | solution.py:133
  917.7 22.9 %collective-permute-done.107 = bf16[256,2048]{1,0:T(8,128)(2,1)S(1)} collective-permute-done((bf16[256,2048]{1,0:T(8,128)(2,1)S(1)}, bf16[256,2048]{1,0:T(8,128)(2,1)S(1)}, u32[]{:S(2)}, u32[]{:S(2)}) %collective-permute-start.107) | collective-permute-done | bytes 1048608 | tf_op jit(solution)/shard_map/ppermute | solution.py:136
  944.9 5.0 collective-permute-done.117
  954.8 6.7 collective-permute-done.118
  (855 shorter events, 495.9 us)
Async XLA Ops:
  12.9 43.3 %collective-permute-start = (bf16[128,1536]{1,0:T(8,128)(2,1)S(1)}, bf16[128,1536]{1,0:T(8,128)(2,1)S(1)}, u32[]{:S(2)}, u32[]{:S(2)}) collective-permute-start(bf16[128,1536]{1,0:T(8,128)(2,1)S(1)} %constant_dynamic-update-slice_fusion.refs_0_), channel_id=1, source_target_pairs={{0,2},{2,0},{4,6},{6,4},{8,10},{10,8},{12,14},{14,12},{16,18},{18,... | collective-permute-start | bytes 1179656 | tf_op jit(solution)/shard_map/ppermute | solution.py:130
  40.1 37.2 %collective-permute-start.66 = (bf16[256,2048]{1,0:T(8,128)(2,1)S(1)}, bf16[256,2048]{1,0:T(8,128)(2,1)}, u32[]{:S(2)}, u32[]{:S(2)}) collective-permute-start(bf16[256,2048]{1,0:T(8,128)(2,1)S(1)} %copy-done.7), channel_id=1, source_target_pairs={{0,1},{1,0},{2,3},{3,2},{4,5},{5,4},{6,7},{7,6},{8,9},{9,8},{10,11... | collective-permute-start | bytes 3145736 | tf_op jit(solution)/shard_map/ppermute | solution.py:136
  62.9 34.8 %collective-permute-start.46 = (bf16[2,2,128,512]{3,2,1,0:T(8,128)(2,1)}, bf16[2,2,128,512]{3,2,1,0:T(8,128)(2,1)}, u32[]{:S(2)}, u32[]{:S(2)}) collective-permute-start(bf16[2,2,128,512]{3,2,1,0:T(8,128)(2,1)} %bitcast.472), channel_id=1, source_target_pairs={{0,16},{2,18},{4,20},{6,22},{8,24},{10,26},{12,28},{14,30},{16,0},... | collective-permute-start | bytes 1572872 | tf_op jit(solution)/shard_map/ppermute | solution.py:142
  168.3 53.1 %collective-permute-start.68 = (bf16[256,2048]{1,0:T(8,128)(2,1)}, bf16[256,2048]{1,0:T(8,128)(2,1)S(1)}, u32[]{:S(2)}, u32[]{:S(2)}) collective-permute-start(bf16[256,2048]{1,0:T(8,128)(2,1)} %collective-permute-done.67.refs_2_), channel_id=1, source_target_pairs={{0,1},{1,0},{2,3},{3,2},{4,5},{5,4},{6,7},{7,6},{8,9},{9,8},{10,11... | collective-permute-start | bytes 3145736 | tf_op jit(solution)/shard_map/ppermute | solution.py:136
  173.2 33.1 %collective-permute-start.44 = (bf16[256,512]{1,0:T(8,128)(2,1)S(1)}, bf16[256,512]{1,0:T(8,128)(2,1)}, u32[]{:S(2)}, u32[]{:S(2)}) collective-permute-start(bf16[256,512]{1,0:T(8,128)(2,1)S(1)} %bitcast.422), channel_id=1, source_target_pairs={{0,1},{1,0},{2,3},{3,2},{4,5},{5,4},{6,7},{7,6},{8,9},{9,8},{10,11... | collective-permute-start | bytes 786440 | tf_op jit(solution)/shard_map/ppermute | solution.py:136
  178.8 33.1 %collective-permute-start.48 = (bf16[256,512]{1,0:T(8,128)(2,1)S(1)}, bf16[256,512]{1,0:T(8,128)(2,1)}, u32[]{:S(2)}, u32[]{:S(2)}) collective-permute-start(bf16[256,512]{1,0:T(8,128)(2,1)S(1)} %bitcast.425), channel_id=1, source_target_pairs={{0,1},{1,0},{2,3},{3,2},{4,5},{5,4},{6,7},{7,6},{8,9},{9,8},{10,11... | collective-permute-start | bytes 786440 | tf_op jit(solution)/shard_map/ppermute | solution.py:136
  180.8 35.5 %collective-permute-start.43 = (bf16[256,512]{1,0:T(8,128)(2,1)S(1)}, bf16[256,512]{1,0:T(8,128)(2,1)S(1)}, u32[]{:S(2)}, u32[]{:S(2)}) collective-permute-start(bf16[256,512]{1,0:T(8,128)(2,1)S(1)} %bitcast.423), channel_id=1, source_target_pairs={{0,4},{2,6},{4,0},{6,2},{8,12},{10,14},{12,8},{14,10},{16,20},{18,... | collective-permute-start | bytes 786440 | tf_op jit(solution)/shard_map/ppermute | solution.py:133
  181.4 38.1 %collective-permute-start.47 = (bf16[256,512]{1,0:T(8,128)(2,1)S(1)}, bf16[256,512]{1,0:T(8,128)(2,1)S(1)}, u32[]{:S(2)}, u32[]{:S(2)}) collective-permute-start(bf16[256,512]{1,0:T(8,128)(2,1)S(1)} %bitcast.426), channel_id=1, source_target_pairs={{0,4},{2,6},{4,0},{6,2},{8,12},{10,14},{12,8},{14,10},{16,20},{18,... | collective-permute-start | bytes 786440 | tf_op jit(solution)/shard_map/ppermute | solution.py:133
  245.5 58.1 %collective-permute-start.82 = (bf16[256,2048]{1,0:T(8,128)(2,1)}, bf16[256,2048]{1,0:T(8,128)(2,1)}, u32[]{:S(2)}, u32[]{:S(2)}) collective-permute-start(bf16[256,2048]{1,0:T(8,128)(2,1)} %dynamic-slice_select_fusion), channel_id=1, source_target_pairs={{0,2},{2,0},{4,6},{6,4},{8,10},{10,8},{12,14},{14,12},{16,18},{18,... | collective-permute-start | bytes 3145736 | tf_op jit(solution)/shard_map/ppermute | solution.py:130
  245.5 45.5 %collective-permute-start.23 = (bf16[64,2048]{1,0:T(8,128)(2,1)S(1)}, bf16[64,2048]{1,0:T(8,128)(2,1)}, u32[]{:S(2)}, u32[]{:S(2)}) collective-permute-start(bf16[64,2048]{1,0:T(8,128)(2,1)S(1)} %copy-done.5), channel_id=1, source_target_pairs={{0,2},{2,0},{4,6},{6,4},{8,10},{10,8},{12,14},{14,12},{16,18},{18,... | collective-permute-start | bytes 786440 | tf_op jit(solution)/shard_map/ppermute | solution.py:130
  246.0 46.5 %collective-permute-start.33 = (bf16[64,2048]{1,0:T(8,128)(2,1)S(1)}, bf16[64,2048]{1,0:T(8,128)(2,1)}, u32[]{:S(2)}, u32[]{:S(2)}) collective-permute-start(bf16[64,2048]{1,0:T(8,128)(2,1)S(1)} %copy-done.4), channel_id=1, source_target_pairs={{0,2},{2,0},{4,6},{6,4},{8,10},{10,8},{12,14},{14,12},{16,18},{18,... | collective-permute-start | bytes 786440 | tf_op jit(solution)/shard_map/ppermute | solution.py:130
  248.4 48.7 %collective-permute-start.25 = (bf16[64,2048]{1,0:T(8,128)(2,1)}, bf16[64,2048]{1,0:T(8,128)(2,1)}, u32[]{:S(2)}, u32[]{:S(2)}) collective-permute-start(bf16[64,2048]{1,0:T(8,128)(2,1)} %collective-permute-done.24.refs_6_), channel_id=1, source_target_pairs={{0,2},{2,0},{4,6},{6,4},{8,10},{10,8},{12,14},{14,12},{16,18},{18,... | collective-permute-start | bytes 786440 | tf_op jit(solution)/shard_map/ppermute | solution.py:130
  253.6 43.5 %collective-permute-start.35 = (bf16[64,2048]{1,0:T(8,128)(2,1)}, bf16[64,2048]{1,0:T(8,128)(2,1)}, u32[]{:S(2)}, u32[]{:S(2)}) collective-permute-start(bf16[64,2048]{1,0:T(8,128)(2,1)} %collective-permute-done.34.refs_14_), channel_id=1, source_target_pairs={{0,2},{2,0},{4,6},{6,4},{8,10},{10,8},{12,14},{14,12},{16,18},{18,... | collective-permute-start | bytes 786440 | tf_op jit(solution)/shard_map/ppermute | solution.py:130
  329.8 42.5 %collective-permute-start.70 = (bf16[256,2048]{1,0:T(8,128)(2,1)S(1)}, bf16[256,2048]{1,0:T(8,128)(2,1)S(1)}, u32[]{:S(2)}, u32[]{:S(2)}) collective-permute-start(bf16[256,2048]{1,0:T(8,128)(2,1)S(1)} %get-tuple-element.219), channel_id=1, source_target_pairs={{8,0},{10,2},{12,4},{14,6},{16,8},{18,10},{20,12},{22,14},{24,16},... | collective-permute-start | bytes 3145736 | tf_op jit(solution)/shard_map/ppermute | solution.py:142
  331.6 40.6 %collective-permute-start.71 = (bf16[256,2048]{1,0:T(8,128)(2,1)S(1)}, bf16[256,2048]{1,0:T(8,128)(2,1)S(1)}, u32[]{:S(2)}, u32[]{:S(2)}) collective-permute-start(bf16[256,2048]{1,0:T(8,128)(2,1)S(1)} %get-tuple-element.219), channel_id=1, source_target_pairs={{0,8},{2,10},{4,12},{6,14},{8,16},{10,18},{12,20},{14,22},{16,24},... | collective-permute-start | bytes 3145736 | tf_op jit(solution)/shard_map/ppermute | solution.py:142
  351.3 43.2 %collective-permute-start.92 = (bf16[256,2048]{1,0:T(8,128)(2,1)S(1)}, bf16[256,2048]{1,0:T(8,128)(2,1)S(1)}, u32[]{:S(2)}, u32[]{:S(2)}) collective-permute-start(bf16[256,2048]{1,0:T(8,128)(2,1)S(1)} %get-tuple-element.209), channel_id=1, source_target_pairs={{0,2},{2,0},{4,6},{6,4},{8,10},{10,8},{12,14},{14,12},{16,18},{18,... | collective-permute-start | bytes 3145736 | tf_op jit(solution)/shard_map/ppermute | solution.py:130
  351.3 44.6 %collective-permute-start.95 = (bf16[256,2048]{1,0:T(8,128)(2,1)S(1)}, bf16[256,2048]{1,0:T(8,128)(2,1)S(1)}, u32[]{:S(2)}, u32[]{:S(2)}) collective-permute-start(bf16[256,2048]{1,0:T(8,128)(2,1)S(1)} %collective-permute-done.90), channel_id=1, source_target_pairs={{8,0},{10,2},{12,4},{14,6},{9,1},{11,3},{13,5},{15,7}} | collective-permute-start | bytes 3145736 | tf_op jit(solution)/shard_map/ppermute | solution.py:142
  356.3 41.0 %collective-permute-start.96 = (bf16[256,2048]{1,0:T(8,128)(2,1)S(1)}, bf16[256,2048]{1,0:T(8,128)(2,1)}, u32[]{:S(2)}, u32[]{:S(2)}) collective-permute-start(bf16[256,2048]{1,0:T(8,128)(2,1)S(1)} %collective-permute-done.91), channel_id=1, source_target_pairs={{16,24},{18,26},{20,28},{22,30},{17,25},{19,27},{21,29},{23,31}} | collective-permute-start | bytes 3145736 | tf_op jit(solution)/shard_map/ppermute | solution.py:142
  372.8 32.2 %collective-permute-start.72 = (bf16[256,2048]{1,0:T(8,128)(2,1)S(1)}, bf16[256,2048]{1,0:T(8,128)(2,1)S(1)}, u32[]{:S(2)}, u32[]{:S(2)}) collective-permute-start(bf16[256,2048]{1,0:T(8,128)(2,1)S(1)} %get-tuple-element.217), channel_id=1, source_target_pairs={{0,2},{2,0},{4,6},{6,4},{8,10},{10,8},{12,14},{14,12},{16,18},{18,... | collective-permute-start | bytes 3145736 | tf_op jit(solution)/shard_map/ppermute | solution.py:130
  390.7 172.6 %collective-permute-start.83 = (bf16[256,2048]{1,0:T(8,128)(2,1)}, bf16[256,2048]{1,0:T(8,128)(2,1)}, u32[]{:S(2)}, u32[]{:S(2)}) collective-permute-start(bf16[256,2048]{1,0:T(8,128)(2,1)} %slice.235), channel_id=1, source_target_pairs={{0,2},{2,0},{4,6},{6,4},{8,10},{10,8},{12,14},{14,12},{16,18},{18,... | collective-permute-start | bytes 3145736 | tf_op jit(solution)/shard_map/ppermute | solution.py:130
  394.5 50.5 %collective-permute-start.69 = (bf16[256,2048]{1,0:T(8,128)(2,1)}, bf16[256,2048]{1,0:T(8,128)(2,1)S(1)}, u32[]{:S(2)}, u32[]{:S(2)}) collective-permute-start(bf16[256,2048]{1,0:T(8,128)(2,1)} %slice.239), channel_id=1, source_target_pairs={{0,2},{2,0},{4,6},{6,4},{8,10},{10,8},{12,14},{14,12},{16,18},{18,... | collective-permute-start | bytes 3145736 | tf_op jit(solution)/shard_map/ppermute | solution.py:130
  405.0 42.9 %collective-permute-start.97 = (bf16[256,2048]{1,0:T(8,128)(2,1)}, bf16[256,2048]{1,0:T(8,128)(2,1)}, u32[]{:S(2)}, u32[]{:S(2)}) collective-permute-start(bf16[256,2048]{1,0:T(8,128)(2,1)} %get-tuple-element.207), channel_id=1, source_target_pairs={{0,2},{2,0},{4,6},{6,4},{8,10},{10,8},{12,14},{14,12},{16,18},{18,... | collective-permute-start | bytes 3145736 | tf_op jit(solution)/shard_map/ppermute | solution.py:130
  456.2 38.0 %collective-permute-start.73 = (bf16[256,2048]{1,0:T(8,128)(2,1)}, bf16[256,2048]{1,0:T(8,128)(2,1)}, u32[]{:S(2)}, u32[]{:S(2)}) collective-permute-start(bf16[256,2048]{1,0:T(8,128)(2,1)} %slice.238), channel_id=1, source_target_pairs={{0,2},{2,0},{4,6},{6,4},{8,10},{10,8},{12,14},{14,12},{16,18},{18,... | collective-permute-start | bytes 3145736 | tf_op jit(solution)/shard_map/ppermute | solution.py:130
  457.5 106.5 %collective-permute-start.88 = (bf16[256,2048]{1,0:T(8,128)(2,1)}, bf16[256,2048]{1,0:T(8,128)(2,1)}, u32[]{:S(2)}, u32[]{:S(2)}) collective-permute-start(bf16[256,2048]{1,0:T(8,128)(2,1)} %fusion.104), channel_id=1, source_target_pairs={{8,0},{10,2},{12,4},{14,6},{16,8},{18,10},{20,12},{22,14},{24,16},... | collective-permute-start | bytes 3145736 | tf_op jit(solution)/shard_map/ppermute | solution.py:142
  473.1 102.0 %collective-permute-start.89 = (bf16[256,2048]{1,0:T(8,128)(2,1)}, bf16[256,2048]{1,0:T(8,128)(2,1)}, u32[]{:S(2)}, u32[]{:S(2)}) collective-permute-start(bf16[256,2048]{1,0:T(8,128)(2,1)} %fusion.104), channel_id=1, source_target_pairs={{0,8},{2,10},{4,12},{6,14},{1,9},{3,11},{5,13},{7,15}} | collective-permute-start | bytes 3145736 | tf_op jit(solution)/shard_map/ppermute | solution.py:142
  494.2 62.2 %collective-permute-start.93 = (bf16[256,2048]{1,0:T(8,128)(2,1)}, bf16[256,2048]{1,0:T(8,128)(2,1)}, u32[]{:S(2)}, u32[]{:S(2)}) collective-permute-start(bf16[256,2048]{1,0:T(8,128)(2,1)} %slice.233), channel_id=1, source_target_pairs={{0,2},{2,0},{4,6},{6,4},{8,10},{10,8},{12,14},{14,12},{16,18},{18,... | collective-permute-start | bytes 3145736 | tf_op jit(solution)/shard_map/ppermute | solution.py:130
  497.5 61.0 %collective-permute-start.77 = (bf16[256,2048]{1,0:T(8,128)(2,1)}, bf16[256,2048]{1,0:T(8,128)(2,1)}, u32[]{:S(2)}, u32[]{:S(2)}) collective-permute-start(bf16[256,2048]{1,0:T(8,128)(2,1)} %slice.237), channel_id=1, source_target_pairs={{0,2},{2,0},{4,6},{6,4},{8,10},{10,8},{12,14},{14,12},{16,18},{18,... | collective-permute-start | bytes 3145736 | tf_op jit(solution)/shard_map/ppermute | solution.py:130
  558.5 71.1 %collective-permute-start.94 = (bf16[256,2048]{1,0:T(8,128)(2,1)S(1)}, bf16[256,2048]{1,0:T(8,128)(2,1)}, u32[]{:S(2)}, u32[]{:S(2)}) collective-permute-start(bf16[256,2048]{1,0:T(8,128)(2,1)S(1)} %fusion.103), channel_id=1, source_target_pairs={{0,16},{2,18},{4,20},{6,22},{8,24},{10,26},{12,28},{14,30},{16,0},... | collective-permute-start | bytes 3145736 | tf_op jit(solution)/shard_map/ppermute | solution.py:142
  563.3 68.1 %collective-permute-start.100 = (bf16[256,2048]{1,0:T(8,128)(2,1)S(1)}, bf16[256,2048]{1,0:T(8,128)(2,1)S(1)}, u32[]{:S(2)}, u32[]{:S(2)}) collective-permute-start(bf16[256,2048]{1,0:T(8,128)(2,1)S(1)} %fusion.102), channel_id=1, source_target_pairs={{8,16},{10,18},{12,20},{14,22},{16,24},{18,26},{20,28},{22,30},{9,... | collective-permute-start | bytes 3145736 | tf_op jit(solution)/shard_map/ppermute | solution.py:142
  564.0 67.4 %collective-permute-start.99 = (bf16[256,2048]{1,0:T(8,128)(2,1)S(1)}, bf16[256,2048]{1,0:T(8,128)(2,1)}, u32[]{:S(2)}, u32[]{:S(2)}) collective-permute-start(bf16[256,2048]{1,0:T(8,128)(2,1)S(1)} %fusion.102), channel_id=1, source_target_pairs={{0,24},{2,26},{4,28},{6,30},{24,0},{26,2},{28,4},{30,6},{1,25},{3,... | collective-permute-start | bytes 3145736 | tf_op jit(solution)/shard_map/ppermute | solution.py:142
  571.6 91.6 %collective-permute-start.150 = (bf16[2,256,2048]{2,1,0:T(8,128)(2,1)}, bf16[2,256,2048]{2,1,0:T(8,128)(2,1)S(1)}, u32[]{:S(2)}, u32[]{:S(2)}) collective-permute-start(bf16[2,256,2048]{2,1,0:T(8,128)(2,1)} %dynamic-slice_bitcast_fusion.1), channel_id=1, source_target_pairs={{0,1},{1,0},{2,3},{3,2},{4,5},{5,4},{6,7},{7,6},{8,9},{9,8},{10,11... | collective-permute-start | bytes 6291464 | tf_op jit(solution)/shard_map/ppermute | solution.py:136
  575.1 91.7 %collective-permute-start.141 = (bf16[4,256,1024]{2,1,0:T(8,128)(2,1)}, bf16[4,256,1024]{2,1,0:T(8,128)(2,1)}, u32[]{:S(2)}, u32[]{:S(2)}) collective-permute-start(bf16[4,256,1024]{2,1,0:T(8,128)(2,1)} %dynamic-slice_bitcast_fusion.2), channel_id=1, source_target_pairs={{0,4},{2,6},{4,0},{6,2},{8,12},{10,14},{12,8},{14,10},{16,20},{18,... | collective-permute-start | bytes 6291464 | tf_op jit(solution)/shard_map/ppermute | solution.py:133
  629.6 48.8 %collective-permute-start.132 = (bf16[2048,512]{1,0:T(8,128)(2,1)}, bf16[2048,512]{1,0:T(8,128)(2,1)S(1)}, u32[]{:S(2)}, u32[]{:S(2)}) collective-permute-start(bf16[2048,512]{1,0:T(8,128)(2,1)} %constant_dynamic-slice_fusion.2), channel_id=1, source_target_pairs={{0,1},{1,0},{2,3},{3,2},{4,5},{5,4},{6,7},{7,6},{8,9},{9,8},{10,11... | collective-permute-start | bytes 6291464 | tf_op jit(solution)/shard_map/ppermute | solution.py:136
  637.2 120.5 %collective-permute-start.101 = (bf16[256,2048]{1,0:T(8,128)(2,1)}, bf16[256,2048]{1,0:T(8,128)(2,1)}, u32[]{:S(2)}, u32[]{:S(2)}) collective-permute-start(bf16[256,2048]{1,0:T(8,128)(2,1)} %convert_element_type.473), channel_id=1, source_target_pairs={{0,8},{2,10},{4,12},{6,14},{1,9},{3,11},{5,13},{7,15}} | collective-permute-start | bytes 3145736 | tf_op jit(solution)/shard_map/ppermute | solution.py:142
  660.5 99.0 %collective-permute-start.102 = (bf16[256,2048]{1,0:T(8,128)(2,1)}, bf16[256,2048]{1,0:T(8,128)(2,1)}, u32[]{:S(2)}, u32[]{:S(2)}) collective-permute-start(bf16[256,2048]{1,0:T(8,128)(2,1)} %convert_element_type.473), channel_id=1, source_target_pairs={{24,16},{26,18},{28,20},{30,22},{25,17},{27,19},{29,21},{31,23}} | collective-permute-start | bytes 3145736 | tf_op jit(solution)/shard_map/ppermute | solution.py:142
  663.1 37.7 %collective-permute-start.108 = (bf16[256,2048]{1,0:T(8,128)(2,1)S(1)}, bf16[256,2048]{1,0:T(8,128)(2,1)S(1)}, u32[]{:S(2)}, u32[]{:S(2)}) collective-permute-start(bf16[256,2048]{1,0:T(8,128)(2,1)S(1)} %fusion.177), channel_id=1, source_target_pairs={{0,1},{1,0},{2,3},{3,2},{4,5},{5,4},{6,7},{7,6},{8,9},{9,8},{10,11... | collective-permute-start | bytes 3145736 | tf_op jit(solution)/shard_map/ppermute | solution.py:136
  667.4 135.8 %collective-permute-start.151 = (bf16[256,2048]{1,0:T(8,128)(2,1)}, bf16[256,2048]{1,0:T(8,128)(2,1)}, u32[]{:S(2)}, u32[]{:S(2)}) collective-permute-start(bf16[256,2048]{1,0:T(8,128)(2,1)} %dynamic-slice_bitcast_fusion.4), channel_id=1, source_target_pairs={{0,4},{2,6},{4,0},{6,2},{8,12},{10,14},{12,8},{14,10},{16,20},{18,... | collective-permute-start | bytes 3145736 | tf_op jit(solution)/shard_map/ppermute | solution.py:133
  678.4 99.9 %collective-permute-start.142 = (bf16[4,256,512]{2,1,0:T(8,128)(2,1)}, bf16[4,256,512]{2,1,0:T(8,128)(2,1)}, u32[]{:S(2)}, u32[]{:S(2)}) collective-permute-start(bf16[4,256,512]{2,1,0:T(8,128)(2,1)} %dynamic-slice_convert_fusion), channel_id=1, source_target_pairs={{0,1},{1,0},{2,3},{3,2},{4,5},{5,4},{6,7},{7,6},{8,9},{9,8},{10,11... | collective-permute-start | bytes 3145736 | tf_op jit(solution)/shard_map/ppermute | solution.py:136
  700.9 82.4 %collective-permute-start.133 = (bf16[4,256,512]{2,1,0:T(8,128)(2,1)}, bf16[4,256,512]{2,1,0:T(8,128)(2,1)}, u32[]{:S(2)}, u32[]{:S(2)}) collective-permute-start(bf16[4,256,512]{2,1,0:T(8,128)(2,1)} %dynamic-slice_bitcast_fusion.5), channel_id=1, source_target_pairs={{0,4},{2,6},{4,0},{6,2},{8,12},{10,14},{12,8},{14,10},{16,20},{18,... | collective-permute-start | bytes 3145736 | tf_op jit(solution)/shard_map/ppermute | solution.py:133
  757.7 48.8 %collective-permute-start.109 = (bf16[256,2048]{1,0:T(8,128)(2,1)S(1)}, bf16[256,2048]{1,0:T(8,128)(2,1)S(1)}, u32[]{:S(2)}, u32[]{:S(2)}) collective-permute-start(bf16[256,2048]{1,0:T(8,128)(2,1)S(1)} %fusion.137), channel_id=1, source_target_pairs={{0,1},{1,0},{2,3},{3,2},{4,5},{5,4},{6,7},{7,6},{8,9},{9,8},{10,11... | collective-permute-start | bytes 3145736 | tf_op jit(solution)/shard_map/ppermute | solution.py:136
  811.0 79.2 %collective-permute-start.124 = (bf16[4,2,64,2048]{3,2,0,1:T(8,128)(2,1)}, bf16[4,2,64,2048]{3,2,0,1:T(8,128)(2,1)S(1)}, u32[]{:S(2)}, u32[]{:S(2)}) collective-permute-start(bf16[4,2,64,2048]{3,2,0,1:T(8,128)(2,1)} %bitcast.458), channel_id=1, source_target_pairs={{0,2},{2,0},{4,6},{6,4},{8,10},{10,8},{12,14},{14,12},{16,18},{18,... | collective-permute-start | bytes 6291464 | tf_op jit(solution)/shard_map/ppermute | solution.py:130
  846.3 69.8 %collective-permute-start.116 = (bf16[4,2,128,1536]{3,2,0,1:T(8,128)(2,1)S(1)}, bf16[4,2,128,1536]{3,2,0,1:T(8,128)(2,1)S(1)}, u32[]{:S(2)}, u32[]{:S(2)}) collective-permute-start(bf16[4,2,128,1536]{3,2,0,1:T(8,128)(2,1)S(1)} %bitcast.456), channel_id=1, source_target_pairs={{0,2},{2,0},{4,6},{6,4},{8,10},{10,8},{12,14},{14,12},{16,18},{18,... | collective-permute-start | bytes 9437192 | tf_op jit(solution)/shard_map/ppermute | solution.py:130
  857.9 34.9 %collective-permute-start.104 = (bf16[256,2048]{1,0:T(8,128)(2,1)}, bf16[256,2048]{1,0:T(8,128)(2,1)S(1)}, u32[]{:S(2)}, u32[]{:S(2)}) collective-permute-start(bf16[256,2048]{1,0:T(8,128)(2,1)} %get-tuple-element.260), channel_id=1, source_target_pairs={{0,8},{2,10},{4,12},{6,14},{8,16},{10,18},{12,20},{14,22},{16,24},... | collective-permute-start | bytes 3145736 | tf_op jit(solution)/shard_map/ppermute | solution.py:142
  895.6 46.6 %collective-permute-start.110 = (bf16[256,2048]{1,0:T(8,128)(2,1)S(1)}, bf16[256,2048]{1,0:T(8,128)(2,1)S(1)}, u32[]{:S(2)}, u32[]{:S(2)}) collective-permute-start(bf16[256,2048]{1,0:T(8,128)(2,1)S(1)} %get-tuple-element.254), channel_id=1, source_target_pairs={{0,1},{1,0},{2,3},{3,2},{4,5},{5,4},{6,7},{7,6},{8,9},{9,8},{10,11... | collective-permute-start | bytes 3145736 | tf_op jit(solution)/shard_map/ppermute | solution.py:136
  897.4 43.2 %collective-permute-start.107 = (bf16[256,2048]{1,0:T(8,128)(2,1)S(1)}, bf16[256,2048]{1,0:T(8,128)(2,1)S(1)}, u32[]{:S(2)}, u32[]{:S(2)}) collective-permute-start(bf16[256,2048]{1,0:T(8,128)(2,1)S(1)} %get-tuple-element.255), channel_id=1, source_target_pairs={{0,1},{1,0},{2,3},{3,2},{4,5},{5,4},{6,7},{7,6},{8,9},{9,8},{10,11... | collective-permute-start | bytes 3145736 | tf_op jit(solution)/shard_map/ppermute | solution.py:136
  914.0 38.6 %collective-permute-start.126 = (bf16[64,2048]{1,0:T(8,128)(2,1)S(1)}, bf16[64,2048]{1,0:T(8,128)(2,1)S(1)}, u32[]{:S(2)}, u32[]{:S(2)}) collective-permute-start(bf16[64,2048]{1,0:T(8,128)(2,1)S(1)} %bitcast_convert_fusion.1), channel_id=1, source_target_pairs={{0,8},{2,10},{4,12},{6,14},{1,9},{3,11},{5,13},{7,15}} | collective-permute-start | bytes 786440 | tf_op jit(solution)/shard_map/ppermute | solution.py:142
  915.4 37.3 %collective-permute-start.127 = (bf16[64,2048]{1,0:T(8,128)(2,1)S(1)}, bf16[64,2048]{1,0:T(8,128)(2,1)S(1)}, u32[]{:S(2)}, u32[]{:S(2)}) collective-permute-start(bf16[64,2048]{1,0:T(8,128)(2,1)S(1)} %bitcast_convert_fusion.1), channel_id=1, source_target_pairs={{24,16},{26,18},{28,20},{30,22},{25,17},{27,19},{29,21},{31,23}} | collective-permute-start | bytes 786440 | tf_op jit(solution)/shard_map/ppermute | solution.py:142
  917.1 32.8 %collective-permute-start.117 = (bf16[4,128,1536]{2,1,0:T(8,128)(2,1)S(1)}, bf16[4,128,1536]{2,1,0:T(8,128)(2,1)S(1)}, u32[]{:S(2)}, u32[]{:S(2)}) collective-permute-start(bf16[4,128,1536]{2,1,0:T(8,128)(2,1)S(1)} %dynamic-slice_bitcast_fusion.3), channel_id=1, source_target_pairs={{0,4},{2,6},{4,0},{6,2},{8,12},{10,14},{12,8},{14,10},{16,20},{18,... | collective-permute-start | bytes 4718600 | tf_op jit(solution)/shard_map/ppermute | solution.py:133
  (273 other events, 4111.1 us)

commit v2 on v1

--- a/solution.py
+++ b/solution.py
@@ -1,3 +1,4 @@
+import functools
 import math
 
 import jax
@@ -19,26 +20,258 @@
     return values * lax.rsqrt(jnp.mean(values * values, axis=-1, keepdims=True) + EPS) * gain
 
 
-def angles(positions, head_dim):
+def angle_tables(count, head_dim, lanes):
     half_dim = head_dim // 2
     freq = jnp.exp(
         jnp.arange(half_dim, dtype=jnp.float32) * (-2.0 * math.log(ROPE_BASE) / head_dim)
     )
-    turned = positions.astype(jnp.float32)[:, None] * freq[None, :]
-    return (jnp.cos(turned)[:, None, :], jnp.sin(turned)[:, None, :])
-
-
-def rotate(values, cosine, sine_table):
-    half_dim = values.shape[-1] // 2
-    first_half = values[..., :half_dim]
-    second_half = values[..., half_dim:]
-    return jnp.concatenate(
-        [
-            first_half * cosine - second_half * sine_table,
-            second_half * cosine + first_half * sine_table,
+    turned = jnp.arange(count, dtype=jnp.int32).astype(jnp.float32)[:, None] * freq[None, :]
+    cosine, sine = jnp.cos(turned), jnp.sin(turned)
+    repeats = lanes // head_dim
+    return (
+        jnp.tile(jnp.concatenate([cosine, cosine], 1), (1, repeats)),
+        jnp.tile(jnp.concatenate([-sine, sine], 1), (1, repeats)),
+    )
+
+
+LANES = 128
+HEAD = LANES // 2
+
+
+def low_lanes(shape):
+    return lax.broadcasted_iota(jnp.int32, shape, 1) < HEAD
+
+
+def per_head(values):
+    low = low_lanes(values.shape)
+    first = jnp.sum(jnp.where(low, values, 0.0), axis=1, keepdims=True)
+    second = jnp.sum(jnp.where(low, 0.0, values), axis=1, keepdims=True)
+    return jnp.where(low, first, second) * (1.0 / HEAD)
+
+
+def halves_swapped(values):
+    lane = lax.broadcasted_iota(jnp.int32, values.shape, 1)
+    return jnp.where(
+        lane % HEAD < HEAD // 2,
+        pltpu.roll(values, LANES - HEAD // 2, 1),
+        pltpu.roll(values, HEAD // 2, 1),
+    )
+
+
+def head_norm(values):
+    scale = lax.rsqrt(per_head(values * values) + EPS)
+    return values * scale, scale
+
+
+def head_turn(values, cosine, sine):
+    return values * cosine + halves_swapped(values) * sine
+
+
+def head_back(grad, normed, scale, gain, cosine, sine):
+    grad = grad * cosine - halves_swapped(grad) * sine
+    gain_grad = jnp.sum(grad * normed, axis=0, keepdims=True)
+    grad = grad * gain
+    return scale * (grad - normed * per_head(grad * normed)), gain_grad
+
+
+def one_head(pair, second):
+    low = low_lanes(pair.shape)
+    return jnp.where(low == jnp.logical_not(second), pair, pltpu.roll(pair, HEAD, 1))
+
+
+def two_rows(slab):
+    low = low_lanes(slab.shape)
+    return jnp.concatenate([jnp.where(low, slab, 0.0), jnp.where(low, 0.0, slab)], 0).astype(BF)
+
+
+def allowed_mask(block, first_row, columns, length):
+    row = lax.broadcasted_iota(jnp.int32, (2 * block, columns), 0) % block + first_row
+    col = lax.broadcasted_iota(jnp.int32, (2 * block, columns), 1)
+    return (col <= row) & (col < length)
+
+
+def attend_kernel(block, scale, length, q, k, v, cosine, sine, q_gain, k_gain, out, totals):
+    second = pl.program_id(0) % 2 == 1
+    rows = q.shape[0]
+    cos, sin = cosine[...], sine[...]
+    keys = one_head(head_turn(head_norm(k[...])[0] * k_gain[...], cos, sin), second).astype(BF)
+    vals = one_head(v[...], second).astype(BF)
+    lane = lax.broadcasted_iota(jnp.int32, (block, LANES), 1)
+    for first in range(0, rows, block):
+        span = pl.ds(first, block)
+        seen = first + block
+        allowed = allowed_mask(block, first, seen, length[0])
+        kept = jnp.zeros((block, LANES), F32)
+        for slab in range(q.shape[1] // LANES):
+            cols = pl.ds(slab * LANES, LANES)
+            turned = head_turn(
+                head_norm(q[span, cols])[0] * q_gain[...], cosine[span, :], sine[span, :]
+            )
+            scores = mm_nt(two_rows(turned), keys[:seen]) * scale
+            scores = jnp.where(allowed, scores, MASKED)
+            top = jnp.max(scores, axis=1, keepdims=True)
+            probs = jnp.exp(scores - top)
+            total = jnp.sum(probs, axis=1, keepdims=True)
+            probs = (probs * (1.0 / total)).astype(BF)
+            both = mm(probs, vals[:seen])
+            out[span, cols] = jnp.where(low_lanes((block, LANES)), both[:block], both[block:]).astype(
+                BF
+            )
+            log_total = top + jnp.log(total)
+            kept = jnp.where(lane == 2 * slab, log_total[:block], kept)
+            kept = jnp.where(lane == 2 * slab + 1, log_total[block:], kept)
+        totals[span, :] = kept
+
+
+def attend_back_kernel(
+    block, scale, length, q, k, v, cosine, sine, q_gain, k_gain, totals, grad_out,
+    grad_q, grad_k, grad_v, q_gain_grad, k_gain_grad, keys_sum, vals_sum,
+):
+    step = pl.program_id(0)
+    second = step % 2 == 1
+    rows = q.shape[0]
+    cos, sin = cosine[...], sine[...]
+    k_normed, k_scale = head_norm(k[...])
+    keys = one_head(head_turn(k_normed * k_gain[...], cos, sin), second).astype(BF)
+    vals = one_head(v[...], second).astype(BF)
+    lane = lax.broadcasted_iota(jnp.int32, (block, LANES), 1)
+    keys_sum[...] = jnp.zeros_like(keys_sum)
+    vals_sum[...] = jnp.zeros_like(vals_sum)
+
+    @pl.when(step == 0)
+    def _():
+        q_gain_grad[...] = jnp.zeros_like(q_gain_grad)
+        k_gain_grad[...] = jnp.zeros_like(k_gain_grad)
+
+    for first in range(0, rows, block):
+        span = pl.ds(first, block)
+        seen = first + block
+        allowed = allowed_mask(block, first, seen, length[0])
+        kept = totals[span, :]
+        for slab in range(q.shape[1] // LANES):
+            cols = pl.ds(slab * LANES, LANES)
+            q_normed, q_scale = head_norm(q[span, cols])
+            turned = two_rows(head_turn(q_normed * q_gain[...], cosine[span, :], sine[span, :]))
+            log_total = jnp.concatenate(
+                [
+                    jnp.sum(jnp.where(lane == 2 * slab + i, kept, 0.0), axis=1, keepdims=True)
+                    for i in range(2)
+                ],
+                0,
+            )
+            scores = mm_nt(turned, keys[:seen]) * scale
+            probs = jnp.exp(jnp.where(allowed, scores, MASKED) - log_total)
+            grad_rows = two_rows(grad_out[span, cols].astype(F32))
+            grad_probs = mm_nt(grad_rows, vals[:seen])
+            drop = jnp.sum(probs * grad_probs, axis=1, keepdims=True)
+            grad_scores = (probs * (grad_probs - drop)).astype(BF)
+            both = mm(grad_scores, keys[:seen]) * scale
+            grad_turned = jnp.where(low_lanes((block, LANES)), both[:block], both[block:])
+            grad_proj, gain_part = head_back(
+                grad_turned, q_normed, q_scale, q_gain[...], cosine[span, :], sine[span, :]
+            )
+            grad_q[span, cols] = grad_proj.astype(BF)
+            q_gain_grad[...] += gain_part
+            keys_sum[:seen] += mm_tn(grad_scores, turned)
+            vals_sum[:seen] += mm_tn(probs.astype(BF), grad_rows)
+
+    keys_grad = keys_sum[...] * scale
+    keys_grad = keys_grad + pltpu.roll(keys_grad, HEAD, 1)
+    vals_grad = vals_sum[...]
+    vals_grad = vals_grad + pltpu.roll(vals_grad, HEAD, 1)
+    grad_proj, gain_part = head_back(
+        keys_grad,
+        one_head(k_normed, second),
+        one_head(k_scale, second),
+        k_gain[...],
+        cos,
+        sin,
+    )
+    k_gain_grad[...] += gain_part * 0.5
+    keep_low = low_lanes(grad_k.shape)
+
+    @pl.when(step % 2 == 0)
+    def _():
+        grad_k[...] = grad_proj.astype(BF)
+        grad_v[...] = vals_grad.astype(BF)
+
+    @pl.when(step % 2 == 1)
+    def _():
+        grad_k[...] = jnp.where(keep_low, grad_k[...].astype(F32), grad_proj).astype(BF)
+        grad_v[...] = jnp.where(keep_low, grad_v[...].astype(F32), vals_grad).astype(BF)
+
+
+def attention_specs(rows, group, k_heads, q_cols):
+    wide = group * HEAD
+    k_first = q_cols // LANES
+    v_first = k_first + k_heads * HEAD // LANES
+    return [
+        pl.BlockSpec(memory_space=pltpu.SMEM),
+        pl.BlockSpec((rows, wide), lambda g: (0, g)),
+        pl.BlockSpec((rows, LANES), lambda g: (0, k_first + g // 2)),
+        pl.BlockSpec((rows, LANES), lambda g: (0, v_first + g // 2)),
+        pl.BlockSpec((rows, LANES), lambda g: (0, 0)),
+        pl.BlockSpec((rows, LANES), lambda g: (0, 0)),
+        pl.BlockSpec((1, LANES), lambda g: (0, 0)),
+        pl.BlockSpec((1, LANES), lambda g: (0, 0)),
+    ]
+
+
+def attend(length, qkv, tables, gains, q_cols, k_heads):
+    rows = qkv.shape[0]
+    group = q_cols // HEAD // k_heads
+    block = rows // 2
+    return pl.pallas_call(
+        functools.partial(attend_kernel, block, 1.0 / math.sqrt(HEAD)),
+        grid=(k_heads,),
+        in_specs=attention_specs(rows, group, k_heads, q_cols),
+        out_specs=[
+            pl.BlockSpec((rows, group * HEAD), lambda g: (0, g)),
+            pl.BlockSpec((rows, LANES), lambda g: (0, g)),
         ],
-        axis=-1,
-    )
+        out_shape=[
+            jax.ShapeDtypeStruct((rows, q_cols), BF),
+            jax.ShapeDtypeStruct((rows, k_heads * LANES), F32),
+        ],
+        compiler_params=pltpu.CompilerParams(vmem_limit_bytes=40 << 20),
+        cost_estimate=pl.CostEstimate(
+            flops=20 * rows * rows * q_cols, bytes_accessed=8 << 20, transcendentals=rows * rows
+        ),
+    )(length, qkv, qkv, qkv, *tables, *gains)
+
+
+def attend_back(length, qkv, tables, gains, totals, grad_out, q_cols, k_heads):
+    rows = qkv.shape[0]
+    group = q_cols // HEAD // k_heads
+    block = rows // 2
+    return pl.pallas_call(
+        functools.partial(attend_back_kernel, block, 1.0 / math.sqrt(HEAD)),
+        grid=(k_heads,),
+        in_specs=attention_specs(rows, group, k_heads, q_cols)
+        + [
+            pl.BlockSpec((rows, LANES), lambda g: (0, g)),
+            pl.BlockSpec((rows, group * HEAD), lambda g: (0, g)),
+        ],
+        out_specs=[
+            pl.BlockSpec((rows, group * HEAD), lambda g: (0, g)),
+            pl.BlockSpec((rows, LANES), lambda g: (0, g // 2)),
+            pl.BlockSpec((rows, LANES), lambda g: (0, g // 2)),
+            pl.BlockSpec((1, LANES), lambda g: (0, 0)),
+            pl.BlockSpec((1, LANES), lambda g: (0, 0)),
+        ],
+        out_shape=[
+            jax.ShapeDtypeStruct((rows, q_cols), BF),
+            jax.ShapeDtypeStruct((rows, k_heads * HEAD), BF),
+            jax.ShapeDtypeStruct((rows, k_heads * HEAD), BF),
+            jax.ShapeDtypeStruct((1, LANES), F32),
+            jax.ShapeDtypeStruct((1, LANES), F32),
+        ],
+        scratch_shapes=[pltpu.VMEM((rows, LANES), F32), pltpu.VMEM((rows, LANES), F32)],
+        compiler_params=pltpu.CompilerParams(vmem_limit_bytes=40 << 20),
+        cost_estimate=pl.CostEstimate(
+            flops=50 * rows * rows * q_cols, bytes_accessed=10 << 20, transcendentals=rows * rows
+        ),
+    )(length, qkv, qkv, qkv, *tables, *gains, totals, grad_out)
 
 
 def mm(left, right):
@@ -116,6 +349,268 @@
         compiler_params=pltpu.CompilerParams(vmem_limit_bytes=moved // 2 + (4 << 20)),
         cost_estimate=pl.CostEstimate(flops=0, bytes_accessed=moved, transcendentals=0),
     )(*blocks)
+
+
+class Sends:
+    def __init__(self, sems):
+        self.sems = sems
+        self.made = []
+
+    def start(self, source, target, recv_sem, device, cond=None):
+        sem = self.sems.at[len(self.made)]
+
+        def copy():
+            return pltpu.make_async_remote_copy(
+                src_ref=source,
+                dst_ref=target,
+                send_sem=sem,
+                recv_sem=recv_sem,
+                device_id=device,
+                device_id_type=pl.DeviceIdType.MESH,
+            )
+
+        self.made.append((cond, copy))
+        when(cond, lambda: copy().start())
+
+    def wait_sent(self):
+        for cond, copy in self.made:
+            when(cond, lambda copy=copy: copy().wait_send())
+
+
+def when(cond, act):
+    if cond is None:
+        act()
+    else:
+        pl.when(cond)(act)
+
+
+def both(first, second):
+    if first is None:
+        return second
+    return first if second is None else jnp.logical_and(first, second)
+
+
+def arrived(ref, recv_sem, device):
+    pltpu.make_async_remote_copy(
+        src_ref=ref, dst_ref=ref, send_sem=recv_sem, recv_sem=recv_sem,
+        device_id=device, device_id_type=pl.DeviceIdType.MESH,
+    ).wait_recv()
+
+
+def greet(devices):
+    barrier = pltpu.get_barrier_semaphore()
+    for device in devices:
+        pl.semaphore_signal(
+            barrier, inc=1, device_id=device, device_id_type=pl.DeviceIdType.MESH
+        )
+    pl.semaphore_wait(barrier, len(devices))
+
+
+def gather_kernel(side, piece, sliced, *refs):
+    w_query, w_key, w_value, w_out, w_gate, w_up, w_down = refs[:7]
+    outs = refs[7:11]
+    qkv, out, units, down = bufs = refs[11:15]
+    load_sems, send_sems, qkv_sems, out_sems, unit_sems, down_sems, store_sems = refs[15:]
+    t, j, c, x = coordinates()
+    bits = side.bit_length() - 1
+
+    def at(tt, jj, cc, xx=None):
+        return (((tt * side) + jj) * 2 + cc, x if xx is None else xx)
+
+    def block(tt, jj, cc):
+        return ((tt * side) + jj) * 2 + cc
+
+    here = at(t, j, c)
+    core = at(t, j, 1 - c)
+    across = at(t, j, c, 1 - x)
+    beside = [at(t, j ^ (1 << bit), c) for bit in range(bits)]
+    others = [
+        at((t + dt) % LINE, j, c ^ dc) for dt in range(LINE) for dc in range(2) if dt or dc
+    ]
+    mine = block(t, j, c)
+    q_cols, k_cols = w_query.shape[1], w_key.shape[1]
+    loads = [
+        (w_query, qkv.at[mine, :, pl.ds(0, q_cols)]),
+        (w_key, qkv.at[mine, :, pl.ds(q_cols, k_cols)]),
+        (w_value, qkv.at[mine, :, pl.ds(q_cols + k_cols, k_cols)]),
+        (w_out, out.at[mine]),
+        (w_down, down.at[x * side + j]),
+    ]
+    depth = w_query.shape[0]
+
+    def unit_block(which, tt, jj, cc):
+        weight = (w_gate, w_up)[which]
+        if sliced:
+            col = pl.multiple_of(block(tt, jj, cc) * piece, piece)
+            return weight.at[:, pl.ds(col, piece)]
+        return weight.at[tt, cc]
+
+    def unit_target(which, tt, jj, cc):
+        if sliced:
+            return units.at[which, tt * 2 + cc, :, pl.ds(jj * piece, piece)]
+        return units.at[which, tt * 2 + cc]
+
+    parts = range(side) if sliced else range(1)
+    loads += [
+        (unit_block(w, t, jj, c), unit_target(w, t, jj, c)) for w in range(2) for jj in parts
+    ]
+    loads = [
+        pltpu.make_async_copy(a, b, load_sems.at[i]) for i, (a, b) in enumerate(loads)
+    ]
+    for load in loads:
+        load.start()
+    greet(others + beside + [across])
+    sends = Sends(send_sems)
+    for load in loads[:5]:
+        load.wait()
+
+    lines = ((qkv, qkv_sems), (out, out_sems))
+
+    def spread(buf, sems, tt, r, cond):
+        idx = block(tt, j ^ r, c)
+        for bit in range(bits):
+            if (1 << bit) > r:
+                sends.start(buf.at[idx], buf.at[idx], sems.at[idx], beside[bit], cond)
+        sends.start(buf.at[idx], buf.at[idx], sems.at[idx], core, cond)
+
+    def pass_on(buf, sems, tt, to_right, to_left):
+        idx = block(tt, j, c)
+        if to_right is not False:
+            sends.start(buf.at[idx], buf.at[idx], sems.at[idx], at(t + 1, j, c), to_right)
+        if to_left is not False:
+            sends.start(buf.at[idx], buf.at[idx], sems.at[idx], at(t - 1, j, c), to_left)
+
+    def spread_rest(buf, sems, tt, cond):
+        for r in range(1, side):
+            idx = block(tt, j ^ r, c)
+            when(cond, lambda idx=idx: arrived(buf.at[idx], sems.at[idx], here))
+            spread(buf, sems, tt, r, cond)
+
+    for buf, sems in lines:
+        pass_on(buf, sems, t, t < LINE - 1, t > 0)
+        spread(buf, sems, t, 0, None)
+    own_down = x * side + j
+    sends.start(down.at[own_down], down.at[own_down], down_sems.at[own_down], across)
+    for bit in range(bits):
+        sends.start(down.at[own_down], down.at[own_down], down_sems.at[own_down], beside[bit])
+    for dt in range(LINE):
+        for dc in range(2):
+            if dt or dc:
+                tt, cc = (t + dt) % LINE, c ^ dc
+                for w in range(2):
+                    for jj in parts:
+                        sends.start(
+                            unit_block(w, tt, jj, cc),
+                            unit_target(w, t, jj, c),
+                            unit_sems.at[w, t * 2 + c, jj],
+                            at(tt, j, cc),
+                        )
+    for k in range(1, LINE):
+        for buf, sems in lines:
+            from_left, from_right = t >= k, t + k < LINE
+            for cond, tt in ((from_left, t - k), (from_right, t + k)):
+                idx = block(tt, j, c)
+                when(cond, lambda idx=idx: arrived(buf.at[idx], sems.at[idx], here))
+                if k < LINE - 1:
+                    if tt is not None and cond is from_left:
+                        pass_on(buf, sems, tt, both(cond, t < LINE - 1), False)
+                    else:
+                        pass_on(buf, sems, tt, False, both(cond, t > 0))
+                spread(buf, sems, tt, 0, cond)
+            if k == 1:
+                spread_rest(buf, sems, t, None)
+            else:
+                spread_rest(buf, sems, t - k + 1, t >= k - 1)
+                spread_rest(buf, sems, t + k - 1, t + k - 1 < LINE)
+        if k == 1:
+            for r in range(1, side):
+                idx = x * side + (j ^ r)
+                arrived(down.at[idx], down_sems.at[idx], here)
+                for bit in range(bits):
+                    if (1 << bit) > r:
+                        sends.start(
+                            down.at[idx], down.at[idx], down_sems.at[idx], beside[bit]
+                        )
+                sends.start(down.at[idx], down.at[idx], down_sems.at[idx], across)
+    stores = []
+
+    def store(i):
+        copy = pltpu.make_async_copy(bufs[i], outs[i], store_sems.at[i])
+        copy.start()
+        stores.append(copy)
+
+    for i, (buf, sems) in enumerate(lines):
+        spread_rest(buf, sems, t - LINE + 1, t >= LINE - 1)
+        spread_rest(buf, sems, t + LINE - 1, t < 1)
+        for tt in range(LINE):
+            for jj in range(side):
+                idx = block(tt, jj, 1 - c)
+                arrived(buf.at[idx], sems.at[idx], here)
+        store(i)
+    for load in loads[5:]:
+        load.wait()
+    for dt in range(LINE):
+        for dc in range(2):
+            if dt or dc:
+                tt, cc = (t + dt) % LINE, c ^ dc
+                for w in range(2):
+                    for jj in parts:
+                        arrived(
+                            unit_target(w, tt, jj, cc), unit_sems.at[w, tt * 2 + cc, jj], here
+                        )
+    store(2)
+    for jj in range(side):
+        idx = (1 - x) * side + jj
+        arrived(down.at[idx], down_sems.at[idx], here)
+    store(3)
+    sends.wait_sent()
+    for copy in stores:
+        copy.wait()
+
+
+def gather_weights(n, w_query, w_key, w_value, w_out, w_gate, w_up, w_down):
+    side = n // LINE // 2
+    depth, piece, width = w_gate.shape[0], w_down.shape[0], w_down.shape[1]
+    strip = side * piece
+    sliced = piece % LANES == 0
+    if not sliced:
+        w_gate, w_up = (
+            w.reshape(depth, LINE, side, 2, piece)
+            .transpose(1, 3, 0, 2, 4)
+            .reshape(LINE, 2, depth, strip)
+            for w in (w_gate, w_up)
+        )
+    shapes = [
+        (n, depth, w_query.shape[1] + 2 * w_key.shape[1]),
+        (n,) + w_out.shape,
+        (2, LINE * 2, depth, strip),
+        (2 * side, piece, width),
+    ]
+    slots = 2 * LINE - 1
+    line_sends = 2 * (LINE - 1) + slots * (2 * side - 1)
+    sends = 2 * line_sends + 2 * side - 1 + 14 * side
+    any_space = pl.BlockSpec(memory_space=pl.ANY)
+    moved = 2 * sum(math.prod(shape) for shape in shapes)
+    return pl.pallas_call(
+        functools.partial(gather_kernel, side, piece, sliced),
+        out_shape=[jax.ShapeDtypeStruct(shape, BF) for shape in shapes],
+        in_specs=[any_space] * 7,
+        out_specs=[any_space] * 4,
+        scratch_shapes=[pltpu.VMEM(shape, BF) for shape in shapes]
+        + [
+            pltpu.SemaphoreType.DMA((5 + 2 * side,)),
+            pltpu.SemaphoreType.DMA((sends,)),
+            pltpu.SemaphoreType.DMA((n,)),
+            pltpu.SemaphoreType.DMA((n,)),
+            pltpu.SemaphoreType.DMA((2, LINE * 2, side)),
+            pltpu.SemaphoreType.DMA((2 * side,)),
+            pltpu.SemaphoreType.DMA((4,)),
+        ],
+        compiler_params=pltpu.CompilerParams(
+            collective_id=0, has_side_effects=True, vmem_limit_bytes=moved + (4 << 20)
+        ),
+        cost_estimate=pl.CostEstimate(flops=0, bytes_accessed=40 * moved, transcendentals=0),
+    )(w_query, w_key, w_value, w_out, w_gate, w_up, w_down)
 
 
 class Links:
@@ -281,10 +776,7 @@
         head_dim = query_gain.shape[0]
         q_cols = w_query.shape[1]
         k_cols = key_weight_matrix.shape[1]
-        q_heads = q_cols // head_dim
         k_heads = k_cols // head_dim
-        group_size = q_heads // k_heads
-        score_scale = 1.0 / math.sqrt(head_dim)
         dp_index = lax.axis_index("dp")
         slot_length = lengths[dp_index]
 
@@ -292,74 +784,38 @@
         piece = w_down.shape[0]
         side = net.side
         strip = side * piece
-        qkv_own = jnp.concatenate([w_query, key_weight_matrix, value_weight_matrix], axis=1)
-        qkv_blocks = net.line_gather(qkv_own)
-        qkv_full = net.gather_rows(qkv_blocks)
-        wo_blocks = net.line_gather(after(qkv_blocks, w_out))
-        wo_full = net.gather_rows(wo_blocks)
-
-        strips = []
-        for weight in (w_gate, w_up):
-            cols = weight.reshape(depth, LINE, side, 2, piece)
-            strips.append(
-                [
-                    net.pick(cols, place_c, 3).transpose(1, 0, 2, 3).reshape(LINE, depth, strip)
-                    for place_c in (c, 1 - c)
-                ]
-            )
-        kept = jnp.stack([strips[0][0], strips[1][0]], 1)
-        sent = jnp.stack([strips[0][1], strips[1][1]], 1)
-        pairs = jnp.stack([kept, net.core(sent)], 1)
-        pairs = after(qkv_blocks, pairs)
-        pieces, where = [], []
-        turned = []
-        for shift in range(LINE):
-            block = net.pick(pairs, (t + shift) % LINE, 0)
-            block = block if shift == 0 else net.turn(block, shift)
-            turned.append(block)
-            gate_part = block[:, 0].reshape(2 * depth, strip)
-            up_part = block[:, 1].reshape(2 * depth, strip)
-            for kind, over_x in ((0, (gate_part, net.cross(gate_part))), (1, (up_part,))):
-                for at_x, part in enumerate(over_x):
-                    for r, got in enumerate(net.side_all(part)):
-                        pieces.append(got)
-                        where.append((kind, shift, r, at_x))
-                        if kind == 1:
-                            pieces.append(net.cross(got))
-                            where.append((kind, shift, r, 1))
-
-        def unit_weight(wanted):
-            chosen = [(p, w) for p, w in zip(pieces, where) if w[0] == wanted]
-
+        qkv_full, wo_full, units, wd = gather_weights(
+            n, w_query, key_weight_matrix, value_weight_matrix, w_out, w_gate, w_up, w_down
+        )
+        qkv_full = qkv_full.reshape(width, q_cols + 2 * k_cols)
+        wo_full = wo_full.reshape(q_cols, width)
+        wd = wd.reshape(2 * strip, width)
+
+        gate_own = units[0].reshape(LINE * 2 * depth, strip)
+        up_own = units[1].reshape(LINE * 2 * depth, strip)
+        gate_pieces, up_pieces = [], []
+        for part in (gate_own, net.cross(gate_own)):
+            gate_pieces.append(net.side_all(part))
+        up_pieces.append(net.side_all(up_own))
+        up_pieces.append([net.cross(part) for part in up_pieces[0]])
+
+        def unit_weight(pieces):
             def spots(t, j, c, x):
                 return [
                     (
-                        i, s * depth, 0, depth, strip,
-                        ((((t - shift) % LINE) * side + (j ^ r)) * 2 + (c ^ s)) * depth,
-                        (x ^ at_x) * strip,
+                        s * side + r, tt * 2 * depth, 0, 2 * depth, strip,
+                        (tt * side + (j ^ r)) * 2 * depth, (x ^ s) * strip,
                     )
-                    for i, (_, (_, shift, r, at_x)) in enumerate(chosen)
                     for s in range(2)
+                    for r in range(side)
+                    for tt in range(LINE)
                 ]
 
-            return place([p for p, _ in chosen], spots, (width, 2 * strip))
-
-        wg = unit_weight(0)
-        wu = unit_weight(1)
-        down_pieces = []
-        for got in net.side_all(w_down):
-            down_pieces += [got, net.cross(got)]
-
-        def down_spots(t, j, c, x):
-            return [
-                (2 * r + s, 0, 0, piece, width, ((x ^ s) * side + (j ^ r)) * piece, 0)
-                for r in range(side)
-                for s in range(2)
-            ]
-
-        wd = place(down_pieces, down_spots, (2 * strip, width))
-
-        positions = jnp.arange(row_count, dtype=jnp.int32)
+            return place(pieces[0] + pieces[1], spots, (width, 2 * strip))
+
+        wg = unit_weight(gate_pieces)
+        wu = unit_weight(up_pieces)
+
         start = x * half
         half_positions = start + jnp.arange(half, dtype=jnp.int32)
         half_valid = (half_positions < slot_length)[:, None]
@@ -367,51 +823,16 @@
         grad_half = jnp.where(half_valid, grad_half, jnp.zeros_like(grad_half))
         grad_blocks = [
             jnp.concatenate([block, net.core(block)], axis=0)
-            for block in net.line_gather(after(turned, grad_half))
+            for block in net.line_gather(after(units, grad_half))
         ]
 
-        allowed = (positions[None, :] <= positions[:, None]) & (positions[None, :] < slot_length)
-        cosine, sine_table = angles(positions, head_dim)
+        tables = angle_tables(row_count, head_dim, LANES)
+        gains = [jnp.tile(gain, LANES // head_dim)[None, :] for gain in (query_gain, key_gain)]
         inputs = tokens.astype(F32)
         hidden_state = rms_scale(inputs, attn_gain).astype(BF)
         qkv = mm(hidden_state, qkv_full)
-        q_proj = qkv[:, :q_cols]
-        key_projected = qkv[:, q_cols : q_cols + k_cols]
-        value_projected = qkv[:, q_cols + k_cols :]
-
-        def prepare(q_vals, k_vals, q_gain, k_gain):
-            q_norm = rms_scale(q_vals.reshape(row_count, q_heads, head_dim), q_gain)
-            k_norm = rms_scale(k_vals.reshape(row_count, k_heads, head_dim), k_gain)
-            return (rotate(q_norm, cosine, sine_table), rotate(k_norm, cosine, sine_table))
-
-        (q_rot, k_rot), prep_back = jax.vjp(prepare, q_proj, key_projected, query_gain, key_gain)
-        q_low = q_rot.astype(BF)
-        k_low = k_rot.astype(BF)
-        v_low = value_projected.astype(BF)
-        q_grouped = q_low.reshape(row_count, k_heads, group_size, head_dim).transpose(1, 2, 0, 3)
-        k_grouped = k_low.transpose(1, 0, 2)
-        v_grouped = v_low.reshape(row_count, k_heads, head_dim).transpose(1, 0, 2)
-
-        def scores_of(q_one, k_one):
-            scores = (
-                jnp.einsum("gid,jd->gij", q_one, k_one, preferred_element_type=F32) * score_scale
-            )
-            return jnp.where(allowed[None], scores, MASKED)
-
-        def attend(packed):
-            q_one, k_one, v_one = packed
-            scores = scores_of(q_one, k_one)
-            row_max = jnp.max(scores, axis=-1, keepdims=True)
-            exp_scores = jnp.exp(scores - row_max)
-            row_total = jnp.sum(exp_scores, axis=-1, keepdims=True)
-            probs = (exp_scores / row_total).astype(BF)
-            attended = jnp.einsum("gij,jd->gid", probs, v_one, preferred_element_type=F32)
-            return (attended, row_max[..., 0] + jnp.log(row_total[..., 0]))
-
-        attended, log_totals = lax.map(attend, (q_grouped, k_grouped, v_grouped))
-        o_low = (
-            attended.transpose(2, 0, 1, 3).reshape(row_count, q_heads * head_dim).astype(BF)
-        )
+        length = slot_length[None]
+        o_low, log_totals = attend(length, qkv, tables, gains, q_cols, k_heads)
         attn_part = mm(o_low, wo_full).reshape(2, half, width)
         input_half = lax.dynamic_slice_in_dim(inputs, start, half, 0)
         h_one = input_half + net.cross_sum(attn_part, 0)
@@ -453,6 +874,9 @@
         grad_attn_half = grad_h_one.astype(BF)
         grad_attn_low = net.pair_order(grad_attn_half, net.cross(grad_attn_half), x)
 
+        acts[0], grad_gates[0], grad_ups[0] = after(
+            grad_parts, acts[0], grad_gates[0], grad_ups[0]
+        )
         act_all = jnp.concatenate(acts, 0)
         hidden_all = jnp.concatenate(hidden_blocks, 0)
         grad_all = jnp.concatenate(grad_blocks, 0)
@@ -507,41 +931,12 @@
 
         g_out = mm_tn(o_low, grad_attn_low).astype(BF)
         grad_o_low = mm_nt(grad_attn_low, wo_full).astype(BF)
-        grad_o_grouped = grad_o_low.reshape(row_count, k_heads, group_size, head_dim).transpose(
-            1, 2, 0, 3
+        grad_q, grad_k, grad_v, q_part, k_part = attend_back(
+            length, qkv, tables, gains, log_totals, grad_o_low, q_cols, k_heads
         )
-
-        def attend_back(packed):
-            q_one, k_one, v_one, total_one, grad_one = packed
-            scores = scores_of(q_one, k_one)
-            probs = jnp.exp(scores - total_one[..., None])
-            grad_probs = jnp.einsum("gid,jd->gij", grad_one, v_one, preferred_element_type=F32)
-            grad_scores = (
-                probs * (grad_probs - jnp.sum(probs * grad_probs, axis=-1, keepdims=True))
-            ).astype(BF)
-            grad_query = (
-                jnp.einsum("gij,jd->gid", grad_scores, k_one, preferred_element_type=F32)
-                * score_scale
-            )
-            grad_keys = (
-                jnp.einsum("gij,gid->jd", grad_scores, q_one, preferred_element_type=F32)
-                * score_scale
-            )
-            grad_values = jnp.einsum(
-                "gij,gid->jd", probs.astype(BF), grad_one, preferred_element_type=F32
-            )
-            return (grad_query, grad_keys, grad_values)
-
-        grad_q_grouped, grad_k_grouped, grad_v_grouped = lax.map(
-            attend_back, (q_grouped, k_grouped, v_grouped, log_totals, grad_o_grouped)
-        )
-        grad_q_rows = grad_q_grouped.transpose(2, 0, 1, 3).reshape(row_count, q_heads, head_dim)
-        grad_k_total = grad_k_grouped.transpose(1, 0, 2)
-        grad_v_rows = grad_v_grouped.transpose(1, 0, 2).reshape(row_count, k_heads * head_dim)
-        grad_q_proj, grad_k_proj, g_query_part, g_key_part = prep_back((grad_q_rows, grad_k_total))
-        grad_qkv = jnp.concatenate(
-            [grad_q_proj.astype(BF), grad_k_proj.astype(BF), grad_v_rows.astype(BF)], axis=1
-        )
+        g_query_part = q_part.reshape(-1, head_dim).sum(0)
+        g_key_part = k_part.reshape(-1, head_dim).sum(0)
+        grad_qkv = jnp.concatenate([grad_q, grad_k, grad_v], axis=1)
         g_qkv = mm_tn(hidden_state, grad_qkv).astype(BF)
         g_out_out = net.sum_rows(g_out)
         g_qkv_out = net.sum_rows(g_qkv)

time: 1000 us -> 945 us (0.945)
  Pallas kernels: 13.7 us -> 148 us
  starting transfers between devices: 200 us -> 132 us
  matrix products: 200 us -> 144 us
  other arithmetic: 105 us -> 75.1 us
  local copies, waits for them, and re-layouts: 98.1 us -> 73.1 us
  waiting for transfers between devices: 371 us -> 359 us
    pallas_call x0 -> x3, Pallas kernels: none -> 146 us  [the longest x1 101 us: gather_weights(): pl.pallas_call(functools.partial(gather_kernel, side, piece, sliced), out...]
    dot_general x28 -> x0, matrix products: 48.9 us -> none  [the longest x4 11.7 us: attend(): jnp.einsum('gij,jd->gid', probs, v_one, preferred_element_type=F32)]
    ppermute x58 -> x43, waiting for transfers between devices: 226 us -> 185 us  [along(): return lax.ppermute(value, 'dp', pairs)]
    ppermute x27 -> x9, waiting for transfers between devices: 51.5 us -> 85.2 us  [over(): return lax.ppermute(value, 'dp', [(i, i ^ 2 << bit) for i in range(self.n)])]
    ppermute x58 -> x43, starting transfers between devices: 140 us -> 110 us  [along(): return lax.ppermute(value, 'dp', pairs)]
    ppermute x23 -> x12, starting transfers between devices: 30.7 us -> 9.75 us  [cross(): return lax.ppermute(value, 'tensor', [(0, 1), (1, 0)])]
    dynamic_slice x10 -> x0, local copies, waits for them, and re-layouts: 16.7 us -> none  [pick(): return lax.dynamic_index_in_dim(value, index, axis, keepdims=False)]
    ppermute x27 -> x9, starting transfers between devices: 22.3 us -> 6.72 us  [over(): return lax.ppermute(value, 'dp', [(i, i ^ 2 << bit) for i in range(self.n)])]
  transfers between devices with their start and end apart: 152 -> 91, of which waited for: 42 -> 33; matrix products, arithmetic and copies ran while one was open for 38% -> 26% of each run, Pallas kernels for 1% -> 3%
where the time goes in v2:
time: 945 us; the launch traced here: 935 us
  waiting for transfers between devices  359 us (38%)
  Pallas kernels  148 us (16%)
  matrix products  144 us (15%)
  starting transfers between devices  132 us (14%)
  other arithmetic  75.1 us (8%)
  local copies, waits for them, and re-layouts  73.1 us (8%)
    ppermute x43, waiting for transfers between devices, along(): return lax.ppermute(value, 'dp', pairs)  185 us
    ppermute x43, starting transfers between devices, along(): return lax.ppermute(value, 'dp', pairs)  110 us
    pallas_call x1, Pallas kernels, gather_weights(): pl.pallas_call(functools.partial(gather_kernel, side, piece, sliced), out...  101 us
    ppermute x12, waiting for transfers between devices, cross(): return lax.ppermute(value, 'tensor', [(0, 1), (1, 0)])  85.9 us
    ppermute x9, waiting for transfers between devices, over(): return lax.ppermute(value, 'dp', [(i, i ^ 2 << bit) for i in range(self.n)])  85.2 us
    dot_general x14, matrix products, mm(): return jnp.dot(left, right, preferred_element_type=F32)  52.3 us
    dot_general x14, matrix products, mm_nt(): lax.dot_general(left, right, (((1,), (1,)), ((), ())), preferred_element_...  46.1 us
    dot_general x5, matrix products, mm_tn(): lax.dot_general(left, right, (((0,), (0,)), ((), ())), preferred_element_...  46 us
  transfers between devices with their start and end apart: 91, of which 33 were waited for; matrix products, arithmetic and copies ran while one was open for 26% of the time, Pallas kernels for 3%

profile of v2, /device:TPU:0, one launch (start us, length us, event | category | flops | bytes accessed | tf_op | source)
XLA Modules:
  0.0 935.0 jit_solution(555193671662101651)
XLA Ops:
  15.7 101.4 %shard_map.237 = (bf16[16,128,1536]{2,1,0:T(8,128)(2,1)S(1)}, bf16[16,64,2048]{2,1,0:T(8,128)(2,1)S(1)}, bf16[2,8,128,512]{3,2,1,0:T(8,128)(2,1)S(1)}, bf16[4,256,2048]{2,1,0:T(8,128)(2,1)S(1)}) custom-call(bf16[128,1024]{1,0:T(8,128)(2,1)S(1)} %copy-done.6, bf16[128,256]{1,0:T(8,128)(2,1)S(1)} %copy-done.8, bf16[128,256]{1,0:T(8,128)(2,1)S(1)} %copy-done.9, ...), custom_call_target="tpu_custom_call" | custom-call | bytes 671088640 | tf_op jit(solution)/shard_map/pallas_call | solution.py:594
  126.7 18.3 %shard_map.238 = (bf16[512,1024]{1,0:T(8,128)(2,1)S(1)}, f32[512,512]{1,0:T(8,128)S(1)}) custom-call(s32[1]{0:T(128)} %dynamic_slice.193.length, f32[512,1536]{1,0:T(8,128)S(1)} %fusion.77.q.k.v, f32[512,1536]{1,0:T(8,128)S(1)} %fusion.77.q.k.v, f32[512,1536]{1,0:T(8,128)S(1)} %fusion.77.q.k.v, f32[512,128]{1,0:T(8,128)S(1)} %copy.27.cosine, ...), custom_call_target="tpu_custom_call" | custom-call | flops 5368709120 | bytes 8388608 | tf_op jit(solution)/shard_map/pallas_call | solution.py:224
  146.9 4.3 fusion.110
  159.6 5.8 collective-permute-start.24
  171.6 8.5 collective-permute-done
  196.1 5.2 fusion.39
  203.2 9.0 collective-permute-start.10
  216.9 5.2 collective-permute-done.29
  227.8 16.5 %collective-permute-done.9 = bf16[256,2048]{1,0:T(8,128)(2,1)S(1)} collective-permute-done((bf16[256,2048]{1,0:T(8,128)(2,1)}, bf16[256,2048]{1,0:T(8,128)(2,1)S(1)}, u32[]{:S(2)}, u32[]{:S(2)}) %collective-permute-start.9) | collective-permute-done | bytes 1048608 | tf_op jit(solution)/shard_map/ppermute | solution.py:637
  249.8 22.1 %collective-permute-done.7.refs_3_ = bf16[1024,512]{1,0:T(8,128)(2,1)S(1)} collective-permute-done((bf16[1024,512]{1,0:T(8,128)(2,1)S(1)}, bf16[1024,512]{1,0:T(8,128)(2,1)S(1)}, u32[]{:S(2)}, u32[]{:S(2)}) %collective-permute-start.7) | collective-permute-done | bytes 1048608 | tf_op jit(solution)/shard_map/ppermute | solution.py:631
  277.4 4.7 multiply_convert_fusion.8
  288.3 11.4 %collective-permute-start.35 = (bf16[256,2048]{1,0:T(8,128)(2,1)S(1)}, bf16[256,2048]{1,0:T(8,128)(2,1)S(1)}, u32[]{:S(2)}, u32[]{:S(2)}) collective-permute-start(bf16[256,2048]{1,0:T(8,128)(2,1)S(1)} %collective-permute-done.30), channel_id=1, source_target_pairs={{16,24},{18,26},{20,28},{22,30},{17,25},{19,27},{21,29},{23,31}} | collective-permute-start | bytes 3145736 | tf_op jit(solution)/shard_map/ppermute | solution.py:637
  302.0 3.9 fusion.43
  309.4 8.8 collective-permute-done.34
  322.9 16.1 %collective-permute-done.13 = bf16[256,2048]{1,0:T(8,128)(2,1)S(1)} collective-permute-done((bf16[256,2048]{1,0:T(8,128)(2,1)S(1)}, bf16[256,2048]{1,0:T(8,128)(2,1)S(1)}, u32[]{:S(2)}, u32[]{:S(2)}) %collective-permute-start.13) | collective-permute-done | bytes 1048608 | tf_op jit(solution)/shard_map/ppermute | solution.py:637
  342.7 4.9 multiply_convert_fusion.6
  347.6 4.4 fusion.116
  355.7 4.9 convolution_add_fusion.2
  370.9 11.1 %collective-permute-done.17 = bf16[256,2048]{1,0:T(8,128)(2,1)} collective-permute-done((bf16[256,2048]{1,0:T(8,128)(2,1)S(1)}, bf16[256,2048]{1,0:T(8,128)(2,1)}, u32[]{:S(2)}, u32[]{:S(2)}) %collective-permute-start.17) | collective-permute-done | bytes 1048608 | tf_op jit(solution)/shard_map/ppermute | solution.py:637
  389.1 5.8 multiply_convert_fusion.4
  421.8 5.7 multiply_convert_fusion.2
  441.2 5.1 collective-permute-start.33
  447.0 4.0 collective-permute-start.38
  451.7 15.1 %collective-permute-done.27 = bf16[256,2048]{1,0:T(8,128)(2,1)S(1)} collective-permute-done((bf16[256,2048]{1,0:T(8,128)(2,1)}, bf16[256,2048]{1,0:T(8,128)(2,1)S(1)}, u32[]{:S(2)}, u32[]{:S(2)}) %collective-permute-start.27) | collective-permute-done | bytes 1048608 | tf_op jit(solution)/shard_map/ppermute | solution.py:637
  466.8 70.5 %collective-permute-done.33 = bf16[256,2048]{1,0:T(8,128)(2,1)S(1)} collective-permute-done((bf16[256,2048]{1,0:T(8,128)(2,1)S(1)}, bf16[256,2048]{1,0:T(8,128)(2,1)S(1)}, u32[]{:S(2)}, u32[]{:S(2)}) %collective-permute-start.33) | collective-permute-done | bytes 1048608 | tf_op jit(solution)/shard_map/ppermute | solution.py:637
  547.5 11.6 %fusion.30 = bf16[2048,1024]{1,0:T(8,128)(2,1)S(1)} fusion(bf16[2048,2048]{1,0:T(8,128)(2,1)} %constant_dynamic-update-slice_fusion.3, bf16[512,1024]{1,0:T(8,128)(2,1)S(1)} %copy-done.86, bf16[512,1024]{1,0:T(8,128)(2,1)S(1)} %copy-done.84, bf16[512,1024]{1,0:T(8,128)(2,1)S(1)} %copy-done.83, bf16[512,1024]{1,0:T(8,128)(2,1)S(1)} %copy-done.82), kind=kOutput, calls=%fused_computation.36 | convolution fusion | flops 8608808960 | bytes 16777216 | tf_op jit(solution)/shard_map/dot_general | solution.py:286
  563.5 11.6 %fusion.27 = bf16[2048,1024]{1,0:T(8,128)(2,1)S(1)} fusion(bf16[2048,2048]{1,0:T(8,128)(2,1)} %constant_dynamic-update-slice_fusion.3, bf16[512,1024]{1,0:T(8,128)(2,1)S(1)} %copy-done.76, bf16[512,1024]{1,0:T(8,128)(2,1)S(1)} %copy-done.74, bf16[512,1024]{1,0:T(8,128)(2,1)S(1)} %copy-done.72, bf16[512,1024]{1,0:T(8,128)(2,1)S(1)} %copy-done.70), kind=kOutput, calls=%fused_computation.35 | convolution fusion | flops 8608808960 | bytes 16777216 | tf_op jit(solution)/shard_map/dot_general | solution.py:286
  575.1 14.7 %fusion.33 = bf16[1024,2048]{1,0:T(8,128)(2,1)S(1)} fusion(bf16[2048,2048]{1,0:T(8,128)(2,1)} %constant_dynamic-update-slice_fusion.11, bf16[512,1024]{1,0:T(8,128)(2,1)} %get-tuple-element.85, bf16[512,1024]{1,0:T(8,128)(2,1)} %get-tuple-element.82, bf16[512,1024]{1,0:T(8,128)(2,1)} %copy-done.78, bf16[512,1024]{1,0:T(8,128)(2,1)} %copy-done.77), kind=kOutput, calls=%fused_computation.37 | convolution fusion | flops 8608808960 | bytes 16777216 | tf_op jit(solution)/shard_map/dot_general | solution.py:286
  602.0 26.3 %shard_map.241 = (bf16[512,1024]{1,0:T(8,128)(2,1)S(1)}, bf16[512,256]{1,0:T(8,128)(2,1)S(1)}, bf16[512,256]{1,0:T(8,128)(2,1)S(1)}, f32[1,128]{1,0:T(1,128)S(1)}, f32[1,128]{1,0:T(1,128)S(1)}) custom-call(s32[1]{0:T(128)} %dynamic_slice.193.length, f32[512,1536]{1,0:T(8,128)S(1)} %copy-done.18, f32[512,1536]{1,0:T(8,128)S(1)} %copy-done.18, ...), custom_call_target="tpu_custom_call" | custom-call | flops 13421772800 | bytes 10485760 | tf_op jit(solution)/shard_map/pallas_call | solution.py:247
  634.5 5.8 convolution_convert_fusion
  648.3 4.0 dynamic-slice_bitcast_fusion
  652.2 31.2 %collective-permute-done.48 = bf16[256,2048]{1,0:T(8,128)(2,1)S(1)} collective-permute-done((bf16[256,2048]{1,0:T(8,128)(2,1)}, bf16[256,2048]{1,0:T(8,128)(2,1)S(1)}, u32[]{:S(2)}, u32[]{:S(2)}) %collective-permute-start.48) | collective-permute-done | bytes 1048608 | tf_op jit(solution)/shard_map/ppermute | solution.py:631
  687.0 4.2 add_convert_fusion.4
  697.9 4.6 collective-permute-start.43
  702.6 27.6 %collective-permute-done.80 = bf16[4,256,1024]{2,1,0:T(8,128)(2,1)} collective-permute-done((bf16[4,256,1024]{2,1,0:T(8,128)(2,1)}, bf16[4,256,1024]{2,1,0:T(8,128)(2,1)}, u32[]{:S(2)}, u32[]{:S(2)}) %collective-permute-start.80) | collective-permute-done | bytes 2097184 | tf_op jit(solution)/shard_map/ppermute | solution.py:628
  754.2 18.5 %collective-permute-done.72 = bf16[4,256,512]{2,1,0:T(8,128)(2,1)} collective-permute-done((bf16[4,256,512]{2,1,0:T(8,128)(2,1)}, bf16[4,256,512]{2,1,0:T(8,128)(2,1)}, u32[]{:S(2)}, u32[]{:S(2)}) %collective-permute-start.72) | collective-permute-done | bytes 1048608 | tf_op jit(solution)/shard_map/ppermute | solution.py:628
  774.4 13.5 %collective-permute-done.90 = bf16[256,2048]{1,0:T(8,128)(2,1)S(1)} collective-permute-done((bf16[256,2048]{1,0:T(8,128)(2,1)}, bf16[256,2048]{1,0:T(8,128)(2,1)S(1)}, u32[]{:S(2)}, u32[]{:S(2)}) %collective-permute-start.90) | collective-permute-done | bytes 1048608 | tf_op jit(solution)/shard_map/ppermute | solution.py:628
  800.9 13.1 %collective-permute-done.76 = bf16[256,512]{1,0:T(8,128)(2,1)S(1)} collective-permute-done((bf16[256,512]{1,0:T(8,128)(2,1)S(1)}, bf16[256,512]{1,0:T(8,128)(2,1)S(1)}, u32[]{:S(2)}, u32[]{:S(2)}) %collective-permute-start.76) | collective-permute-done | bytes 262176 | tf_op jit(solution)/shard_map/ppermute | solution.py:637
  814.0 5.4 collective-permute-start.87
  821.0 6.6 collective-permute-done.85
  840.1 16.6 %collective-permute-done.49 = bf16[256,2048]{1,0:T(8,128)(2,1)S(1)} collective-permute-done((bf16[256,2048]{1,0:T(8,128)(2,1)S(1)}, bf16[256,2048]{1,0:T(8,128)(2,1)S(1)}, u32[]{:S(2)}, u32[]{:S(2)}) %collective-permute-start.49) | collective-permute-done | bytes 1048608 | tf_op jit(solution)/shard_map/ppermute | solution.py:631
  860.6 5.1 collective-permute-start.65
  865.7 25.0 %collective-permute-done.56 = bf16[4,128,1536]{2,1,0:T(8,128)(2,1)S(1)} collective-permute-done((bf16[4,128,1536]{2,1,0:T(8,128)(2,1)S(1)}, bf16[4,128,1536]{2,1,0:T(8,128)(2,1)S(1)}, u32[]{:S(2)}, u32[]{:S(2)}) %collective-permute-start.56) | collective-permute-done | bytes 1572896 | tf_op jit(solution)/shard_map/ppermute | solution.py:628
  891.9 5.1 collective-permute-start.57
  899.2 7.4 collective-permute-done.57
  906.7 4.4 collective-permute-start.59
  913.6 5.0 collective-permute-start.68
  922.1 5.3 collective-permute-start.60
  (487 shorter events, 286.6 us)
Async XLA Ops:
  167.2 34.1 %collective-permute-start.5 = (bf16[1024,512]{1,0:T(8,128)(2,1)S(1)}, bf16[1024,512]{1,0:T(8,128)(2,1)S(1)}, u32[]{:S(2)}, u32[]{:S(2)}) collective-permute-start(bf16[1024,512]{1,0:T(8,128)(2,1)S(1)} %bitcast.222), channel_id=1, source_target_pairs={{0,4},{2,6},{4,0},{6,2},{8,12},{10,14},{12,8},{14,10},{16,20},{18,... | collective-permute-start | bytes 3145736 | tf_op jit(solution)/shard_map/ppermute | solution.py:628
  193.5 28.6 %collective-permute-start.29 = (bf16[256,2048]{1,0:T(8,128)(2,1)}, bf16[256,2048]{1,0:T(8,128)(2,1)S(1)}, u32[]{:S(2)}, u32[]{:S(2)}) collective-permute-start(bf16[256,2048]{1,0:T(8,128)(2,1)} %collective-permute-done.23), channel_id=1, source_target_pairs={{8,0},{10,2},{12,4},{14,6},{16,8},{18,10},{20,12},{22,14},{9,1},{1... | collective-permute-start | bytes 3145736 | tf_op jit(solution)/shard_map/ppermute | solution.py:637
  194.8 27.8 %collective-permute-start.30 = (bf16[256,2048]{1,0:T(8,128)(2,1)}, bf16[256,2048]{1,0:T(8,128)(2,1)S(1)}, u32[]{:S(2)}, u32[]{:S(2)}) collective-permute-start(bf16[256,2048]{1,0:T(8,128)(2,1)} %collective-permute-done.24), channel_id=1, source_target_pairs={{8,16},{10,18},{12,20},{14,22},{16,24},{18,26},{20,28},{22,30},{9,... | collective-permute-start | bytes 3145736 | tf_op jit(solution)/shard_map/ppermute | solution.py:637
  201.9 42.5 %collective-permute-start.9 = (bf16[256,2048]{1,0:T(8,128)(2,1)}, bf16[256,2048]{1,0:T(8,128)(2,1)S(1)}, u32[]{:S(2)}, u32[]{:S(2)}) collective-permute-start(bf16[256,2048]{1,0:T(8,128)(2,1)} %get-tuple-element.68), channel_id=1, source_target_pairs={{8,0},{10,2},{12,4},{14,6},{16,8},{18,10},{20,12},{22,14},{24,16},... | collective-permute-start | bytes 3145736 | tf_op jit(solution)/shard_map/ppermute | solution.py:637
  203.2 41.7 %collective-permute-start.10 = (bf16[256,2048]{1,0:T(8,128)(2,1)}, bf16[256,2048]{1,0:T(8,128)(2,1)S(1)}, u32[]{:S(2)}, u32[]{:S(2)}) collective-permute-start(bf16[256,2048]{1,0:T(8,128)(2,1)} %get-tuple-element.68), channel_id=1, source_target_pairs={{0,8},{2,10},{4,12},{6,14},{8,16},{10,18},{12,20},{14,22},{16,24},... | collective-permute-start | bytes 3145736 | tf_op jit(solution)/shard_map/ppermute | solution.py:637
  222.1 27.7 %collective-permute-start.6 = (bf16[1024,512]{1,0:T(8,128)(2,1)S(1)}, bf16[1024,512]{1,0:T(8,128)(2,1)S(1)}, u32[]{:S(2)}, u32[]{:S(2)}) collective-permute-start(bf16[1024,512]{1,0:T(8,128)(2,1)S(1)} %bitcast.223), channel_id=1, source_target_pairs={{0,1},{1,0},{2,3},{3,2},{4,5},{5,4},{6,7},{7,6},{8,9},{9,8},{10,11... | collective-permute-start | bytes 3145736 | tf_op jit(solution)/shard_map/ppermute | solution.py:631
  222.6 49.3 %collective-permute-start.7 = (bf16[1024,512]{1,0:T(8,128)(2,1)S(1)}, bf16[1024,512]{1,0:T(8,128)(2,1)S(1)}, u32[]{:S(2)}, u32[]{:S(2)}) collective-permute-start(bf16[1024,512]{1,0:T(8,128)(2,1)S(1)} %collective-permute-done.5.refs_1_), channel_id=1, source_target_pairs={{0,1},{1,0},{2,3},{3,2},{4,5},{5,4},{6,7},{7,6},{8,9},{9,8},{10,11... | collective-permute-start | bytes 3145736 | tf_op jit(solution)/shard_map/ppermute | solution.py:631
  227.3 49.3 %collective-permute-start.2 = (bf16[1024,512]{1,0:T(8,128)(2,1)S(1)}, bf16[1024,512]{1,0:T(8,128)(2,1)S(1)}, u32[]{:S(2)}, u32[]{:S(2)}) collective-permute-start(bf16[1024,512]{1,0:T(8,128)(2,1)S(1)} %bitcast.220), channel_id=1, source_target_pairs={{0,4},{2,6},{4,0},{6,2},{8,12},{10,14},{12,8},{14,10},{16,20},{18,... | collective-permute-start | bytes 3145736 | tf_op jit(solution)/shard_map/ppermute | solution.py:628
  244.4 32.2 %collective-permute-start.4 = (bf16[1024,512]{1,0:T(8,128)(2,1)S(1)}, bf16[1024,512]{1,0:T(8,128)(2,1)S(1)}, u32[]{:S(2)}, u32[]{:S(2)}) collective-permute-start(bf16[1024,512]{1,0:T(8,128)(2,1)S(1)} %collective-permute-done.3.refs_2_), channel_id=1, source_target_pairs={{0,4},{2,6},{4,0},{6,2},{8,12},{10,14},{12,8},{14,10},{16,20},{18,... | collective-permute-start | bytes 3145736 | tf_op jit(solution)/shard_map/ppermute | solution.py:628
  244.9 62.7 %collective-permute-start.31 = (bf16[256,2048]{1,0:T(8,128)(2,1)S(1)}, bf16[256,2048]{1,0:T(8,128)(2,1)S(1)}, u32[]{:S(2)}, u32[]{:S(2)}) collective-permute-start(bf16[256,2048]{1,0:T(8,128)(2,1)S(1)} %get-tuple-element.58), channel_id=1, source_target_pairs={{0,2},{2,0},{4,6},{6,4},{8,10},{10,8},{12,14},{14,12},{16,18},{18,... | collective-permute-start | bytes 3145736 | tf_op jit(solution)/shard_map/ppermute | solution.py:625
  249.8 72.1 %collective-permute-start.11 = (bf16[256,2048]{1,0:T(8,128)(2,1)S(1)}, bf16[256,2048]{1,0:T(8,128)(2,1)S(1)}, u32[]{:S(2)}, u32[]{:S(2)}) collective-permute-start(bf16[256,2048]{1,0:T(8,128)(2,1)S(1)} %get-tuple-element.66), channel_id=1, source_target_pairs={{0,2},{2,0},{4,6},{6,4},{8,10},{10,8},{12,14},{14,12},{16,18},{18,... | collective-permute-start | bytes 3145736 | tf_op jit(solution)/shard_map/ppermute | solution.py:625
  287.0 31.2 %collective-permute-start.34 = (bf16[256,2048]{1,0:T(8,128)(2,1)S(1)}, bf16[256,2048]{1,0:T(8,128)(2,1)S(1)}, u32[]{:S(2)}, u32[]{:S(2)}) collective-permute-start(bf16[256,2048]{1,0:T(8,128)(2,1)S(1)} %collective-permute-done.29), channel_id=1, source_target_pairs={{8,0},{10,2},{12,4},{14,6},{9,1},{11,3},{13,5},{15,7}} | collective-permute-start | bytes 3145736 | tf_op jit(solution)/shard_map/ppermute | solution.py:637
  288.3 29.9 %collective-permute-start.35 = (bf16[256,2048]{1,0:T(8,128)(2,1)S(1)}, bf16[256,2048]{1,0:T(8,128)(2,1)S(1)}, u32[]{:S(2)}, u32[]{:S(2)}) collective-permute-start(bf16[256,2048]{1,0:T(8,128)(2,1)S(1)} %collective-permute-done.30), channel_id=1, source_target_pairs={{16,24},{18,26},{20,28},{22,30},{17,25},{19,27},{21,29},{23,31}} | collective-permute-start | bytes 3145736 | tf_op jit(solution)/shard_map/ppermute | solution.py:637
  306.3 32.8 %collective-permute-start.13 = (bf16[256,2048]{1,0:T(8,128)(2,1)S(1)}, bf16[256,2048]{1,0:T(8,128)(2,1)S(1)}, u32[]{:S(2)}, u32[]{:S(2)}) collective-permute-start(bf16[256,2048]{1,0:T(8,128)(2,1)S(1)} %collective-permute-done.9), channel_id=1, source_target_pairs={{8,0},{10,2},{12,4},{14,6},{16,8},{18,10},{20,12},{22,14},{9,1},{1... | collective-permute-start | bytes 3145736 | tf_op jit(solution)/shard_map/ppermute | solution.py:637
  307.6 31.5 %collective-permute-start.14 = (bf16[256,2048]{1,0:T(8,128)(2,1)S(1)}, bf16[256,2048]{1,0:T(8,128)(2,1)S(1)}, u32[]{:S(2)}, u32[]{:S(2)}) collective-permute-start(bf16[256,2048]{1,0:T(8,128)(2,1)S(1)} %collective-permute-done.10), channel_id=1, source_target_pairs={{8,16},{10,18},{12,20},{14,22},{16,24},{18,26},{20,28},{22,30},{9,... | collective-permute-start | bytes 3145736 | tf_op jit(solution)/shard_map/ppermute | solution.py:637
  318.2 123.0 %collective-permute-start.22 = (bf16[256,2048]{1,0:T(8,128)(2,1)S(1)}, bf16[256,2048]{1,0:T(8,128)(2,1)}, u32[]{:S(2)}, u32[]{:S(2)}) collective-permute-start(bf16[256,2048]{1,0:T(8,128)(2,1)S(1)} %slice.150), channel_id=1, source_target_pairs={{0,2},{2,0},{4,6},{6,4},{8,10},{10,8},{12,14},{14,12},{16,18},{18,... | collective-permute-start | bytes 3145736 | tf_op jit(solution)/shard_map/ppermute | solution.py:625
  318.2 42.3 %collective-permute-start.8 = (bf16[256,2048]{1,0:T(8,128)(2,1)S(1)}, bf16[256,2048]{1,0:T(8,128)(2,1)S(1)}, u32[]{:S(2)}, u32[]{:S(2)}) collective-permute-start(bf16[256,2048]{1,0:T(8,128)(2,1)S(1)} %slice.154), channel_id=1, source_target_pairs={{0,2},{2,0},{4,6},{6,4},{8,10},{10,8},{12,14},{14,12},{16,18},{18,... | collective-permute-start | bytes 3145736 | tf_op jit(solution)/shard_map/ppermute | solution.py:625
  321.9 85.5 %collective-permute-start.36 = (bf16[256,2048]{1,0:T(8,128)(2,1)}, bf16[256,2048]{1,0:T(8,128)(2,1)}, u32[]{:S(2)}, u32[]{:S(2)}) collective-permute-start(bf16[256,2048]{1,0:T(8,128)(2,1)} %get-tuple-element.56), channel_id=1, source_target_pairs={{0,2},{2,0},{4,6},{6,4},{8,10},{10,8},{12,14},{14,12},{16,18},{18,... | collective-permute-start | bytes 3145736 | tf_op jit(solution)/shard_map/ppermute | solution.py:625
  340.4 27.5 %collective-permute-start.15 = (bf16[256,2048]{1,0:T(8,128)(2,1)S(1)}, bf16[256,2048]{1,0:T(8,128)(2,1)}, u32[]{:S(2)}, u32[]{:S(2)}) collective-permute-start(bf16[256,2048]{1,0:T(8,128)(2,1)S(1)} %get-tuple-element.64), channel_id=1, source_target_pairs={{0,2},{2,0},{4,6},{6,4},{8,10},{10,8},{12,14},{14,12},{16,18},{18,... | collective-permute-start | bytes 3145736 | tf_op jit(solution)/shard_map/ppermute | solution.py:625
  354.4 27.6 %collective-permute-start.17 = (bf16[256,2048]{1,0:T(8,128)(2,1)S(1)}, bf16[256,2048]{1,0:T(8,128)(2,1)}, u32[]{:S(2)}, u32[]{:S(2)}) collective-permute-start(bf16[256,2048]{1,0:T(8,128)(2,1)S(1)} %collective-permute-done.13), channel_id=1, source_target_pairs={{8,0},{10,2},{12,4},{14,6},{9,1},{11,3},{13,5},{15,7}} | collective-permute-start | bytes 3145736 | tf_op jit(solution)/shard_map/ppermute | solution.py:637
  367.9 36.8 %collective-permute-start.26 = (bf16[256,2048]{1,0:T(8,128)(2,1)}, bf16[256,2048]{1,0:T(8,128)(2,1)}, u32[]{:S(2)}, u32[]{:S(2)}) collective-permute-start(bf16[256,2048]{1,0:T(8,128)(2,1)} %slice.149), channel_id=1, source_target_pairs={{0,2},{2,0},{4,6},{6,4},{8,10},{10,8},{12,14},{14,12},{16,18},{18,... | collective-permute-start | bytes 3145736 | tf_op jit(solution)/shard_map/ppermute | solution.py:625
  382.0 30.0 %collective-permute-start.12 = (bf16[256,2048]{1,0:T(8,128)(2,1)}, bf16[256,2048]{1,0:T(8,128)(2,1)S(1)}, u32[]{:S(2)}, u32[]{:S(2)}) collective-permute-start(bf16[256,2048]{1,0:T(8,128)(2,1)} %slice.153), channel_id=1, source_target_pairs={{0,2},{2,0},{4,6},{6,4},{8,10},{10,8},{12,14},{14,12},{16,18},{18,... | collective-permute-start | bytes 3145736 | tf_op jit(solution)/shard_map/ppermute | solution.py:625
  385.1 32.9 %collective-permute-start.19 = (bf16[256,2048]{1,0:T(8,128)(2,1)}, bf16[256,2048]{1,0:T(8,128)(2,1)}, u32[]{:S(2)}, u32[]{:S(2)}) collective-permute-start(bf16[256,2048]{1,0:T(8,128)(2,1)} %get-tuple-element.62), channel_id=1, source_target_pairs={{0,2},{2,0},{4,6},{6,4},{8,10},{10,8},{12,14},{14,12},{16,18},{18,... | collective-permute-start | bytes 3145736 | tf_op jit(solution)/shard_map/ppermute | solution.py:625
  404.8 32.8 %collective-permute-start.32 = (bf16[256,2048]{1,0:T(8,128)(2,1)}, bf16[256,2048]{1,0:T(8,128)(2,1)}, u32[]{:S(2)}, u32[]{:S(2)}) collective-permute-start(bf16[256,2048]{1,0:T(8,128)(2,1)} %slice.148), channel_id=1, source_target_pairs={{0,2},{2,0},{4,6},{6,4},{8,10},{10,8},{12,14},{14,12},{16,18},{18,... | collective-permute-start | bytes 3145736 | tf_op jit(solution)/shard_map/ppermute | solution.py:625
  407.4 44.3 %collective-permute-start.28 = (bf16[256,2048]{1,0:T(8,128)(2,1)}, bf16[256,2048]{1,0:T(8,128)(2,1)}, u32[]{:S(2)}, u32[]{:S(2)}) collective-permute-start(bf16[256,2048]{1,0:T(8,128)(2,1)} %slice_add_fusion.2), channel_id=1, source_target_pairs={{0,8},{2,10},{4,12},{6,14},{1,9},{3,11},{5,13},{7,15}} | collective-permute-start | bytes 3145736 | tf_op jit(solution)/shard_map/ppermute | solution.py:637
  411.9 34.4 %collective-permute-start.16 = (bf16[256,2048]{1,0:T(8,128)(2,1)S(1)}, bf16[256,2048]{1,0:T(8,128)(2,1)S(1)}, u32[]{:S(2)}, u32[]{:S(2)}) collective-permute-start(bf16[256,2048]{1,0:T(8,128)(2,1)S(1)} %slice.152), channel_id=1, source_target_pairs={{0,2},{2,0},{4,6},{6,4},{8,10},{10,8},{12,14},{14,12},{16,18},{18,... | collective-permute-start | bytes 3145736 | tf_op jit(solution)/shard_map/ppermute | solution.py:625
  441.2 96.1 %collective-permute-start.33 = (bf16[256,2048]{1,0:T(8,128)(2,1)S(1)}, bf16[256,2048]{1,0:T(8,128)(2,1)S(1)}, u32[]{:S(2)}, u32[]{:S(2)}) collective-permute-start(bf16[256,2048]{1,0:T(8,128)(2,1)S(1)} %slice_add_fusion.1), channel_id=1, source_target_pairs={{0,16},{2,18},{4,20},{6,22},{8,24},{10,26},{12,28},{14,30},{16,0},... | collective-permute-start | bytes 3145736 | tf_op jit(solution)/shard_map/ppermute | solution.py:637
  446.3 91.0 %collective-permute-start.39 = (bf16[256,2048]{1,0:T(8,128)(2,1)S(1)}, bf16[256,2048]{1,0:T(8,128)(2,1)S(1)}, u32[]{:S(2)}, u32[]{:S(2)}) collective-permute-start(bf16[256,2048]{1,0:T(8,128)(2,1)S(1)} %slice_add_fusion), channel_id=1, source_target_pairs={{8,16},{10,18},{12,20},{14,22},{16,24},{18,26},{20,28},{22,30},{9,... | collective-permute-start | bytes 3145736 | tf_op jit(solution)/shard_map/ppermute | solution.py:637
  447.0 90.3 %collective-permute-start.38 = (bf16[256,2048]{1,0:T(8,128)(2,1)S(1)}, bf16[256,2048]{1,0:T(8,128)(2,1)}, u32[]{:S(2)}, u32[]{:S(2)}) collective-permute-start(bf16[256,2048]{1,0:T(8,128)(2,1)S(1)} %slice_add_fusion), channel_id=1, source_target_pairs={{0,24},{2,26},{4,28},{6,30},{24,0},{26,2},{28,4},{30,6},{1,25},{3,... | collective-permute-start | bytes 3145736 | tf_op jit(solution)/shard_map/ppermute | solution.py:637
  541.3 52.3 %collective-permute-start.41 = (bf16[256,2048]{1,0:T(8,128)(2,1)S(1)}, bf16[256,2048]{1,0:T(8,128)(2,1)S(1)}, u32[]{:S(2)}, u32[]{:S(2)}) collective-permute-start(bf16[256,2048]{1,0:T(8,128)(2,1)S(1)} %convert_element_type.398), channel_id=1, source_target_pairs={{24,16},{26,18},{28,20},{30,22},{25,17},{27,19},{29,21},{31,23}} | collective-permute-start | bytes 3145736 | tf_op jit(solution)/shard_map/ppermute | solution.py:637
  542.2 51.4 %collective-permute-start.40 = (bf16[256,2048]{1,0:T(8,128)(2,1)S(1)}, bf16[256,2048]{1,0:T(8,128)(2,1)S(1)}, u32[]{:S(2)}, u32[]{:S(2)}) collective-permute-start(bf16[256,2048]{1,0:T(8,128)(2,1)S(1)} %convert_element_type.398), channel_id=1, source_target_pairs={{0,8},{2,10},{4,12},{6,14},{1,9},{3,11},{5,13},{7,15}} | collective-permute-start | bytes 3145736 | tf_op jit(solution)/shard_map/ppermute | solution.py:637
  546.2 53.2 %collective-permute-start.47 = (bf16[256,2048]{1,0:T(8,128)(2,1)S(1)}, bf16[256,2048]{1,0:T(8,128)(2,1)S(1)}, u32[]{:S(2)}, u32[]{:S(2)}) collective-permute-start(bf16[256,2048]{1,0:T(8,128)(2,1)S(1)} %fusion.104), channel_id=1, source_target_pairs={{0,1},{1,0},{2,3},{3,2},{4,5},{5,4},{6,7},{7,6},{8,9},{9,8},{10,11... | collective-permute-start | bytes 3145736 | tf_op jit(solution)/shard_map/ppermute | solution.py:631
  560.7 134.5 %collective-permute-start.71 = (bf16[2048,512]{1,0:T(8,128)(2,1)}, bf16[2048,512]{1,0:T(8,128)(2,1)}, u32[]{:S(2)}, u32[]{:S(2)}) collective-permute-start(bf16[2048,512]{1,0:T(8,128)(2,1)} %constant_dynamic-slice_fusion.2), channel_id=1, source_target_pairs={{0,1},{1,0},{2,3},{3,2},{4,5},{5,4},{6,7},{7,6},{8,9},{9,8},{10,11... | collective-permute-start | bytes 6291464 | tf_op jit(solution)/shard_map/ppermute | solution.py:631
  591.3 99.9 %collective-permute-start.89 = (bf16[2,256,2048]{2,1,0:T(8,128)(2,1)}, bf16[2,256,2048]{2,1,0:T(8,128)(2,1)}, u32[]{:S(2)}, u32[]{:S(2)}) collective-permute-start(bf16[2,256,2048]{2,1,0:T(8,128)(2,1)} %dynamic-slice_bitcast_fusion.1), channel_id=1, source_target_pairs={{0,1},{1,0},{2,3},{3,2},{4,5},{5,4},{6,7},{7,6},{8,9},{9,8},{10,11... | collective-permute-start | bytes 6291464 | tf_op jit(solution)/shard_map/ppermute | solution.py:631
  595.1 91.3 %collective-permute-start.42 = (bf16[256,2048]{1,0:T(8,128)(2,1)}, bf16[256,2048]{1,0:T(8,128)(2,1)}, u32[]{:S(2)}, u32[]{:S(2)}) collective-permute-start(bf16[256,2048]{1,0:T(8,128)(2,1)} %add_convert_fusion.5), channel_id=1, source_target_pairs={{0,8},{2,10},{4,12},{6,14},{8,16},{10,18},{12,20},{14,22},{1,9},{3... | collective-permute-start | bytes 3145736 | tf_op jit(solution)/shard_map/ppermute | solution.py:637
  597.7 88.8 %collective-permute-start.44 = (bf16[256,2048]{1,0:T(8,128)(2,1)}, bf16[256,2048]{1,0:T(8,128)(2,1)}, u32[]{:S(2)}, u32[]{:S(2)}) collective-permute-start(bf16[256,2048]{1,0:T(8,128)(2,1)} %add_convert_fusion.5), channel_id=1, source_target_pairs={{16,8},{18,10},{20,12},{22,14},{24,16},{26,18},{28,20},{30,22},{17... | collective-permute-start | bytes 3145736 | tf_op jit(solution)/shard_map/ppermute | solution.py:637
  633.3 50.1 %collective-permute-start.48 = (bf16[256,2048]{1,0:T(8,128)(2,1)}, bf16[256,2048]{1,0:T(8,128)(2,1)S(1)}, u32[]{:S(2)}, u32[]{:S(2)}) collective-permute-start(bf16[256,2048]{1,0:T(8,128)(2,1)} %fusion.70), channel_id=1, source_target_pairs={{0,1},{1,0},{2,3},{3,2},{4,5},{5,4},{6,7},{7,6},{8,9},{9,8},{10,11... | collective-permute-start | bytes 3145736 | tf_op jit(solution)/shard_map/ppermute | solution.py:631
  683.4 46.7 %collective-permute-start.80 = (bf16[4,256,1024]{2,1,0:T(8,128)(2,1)}, bf16[4,256,1024]{2,1,0:T(8,128)(2,1)}, u32[]{:S(2)}, u32[]{:S(2)}) collective-permute-start(bf16[4,256,1024]{2,1,0:T(8,128)(2,1)} %dynamic-slice_bitcast_fusion.2), channel_id=1, source_target_pairs={{0,4},{2,6},{4,0},{6,2},{8,12},{10,14},{12,8},{14,10},{16,20},{18,... | collective-permute-start | bytes 6291464 | tf_op jit(solution)/shard_map/ppermute | solution.py:628
  686.4 150.8 %collective-permute-start.55 = (bf16[4,2,128,1536]{3,2,1,0:T(8,128)(2,1)}, bf16[4,2,128,1536]{3,2,1,0:T(8,128)(2,1)S(1)}, u32[]{:S(2)}, u32[]{:S(2)}) collective-permute-start(bf16[4,2,128,1536]{3,2,1,0:T(8,128)(2,1)} %dynamic-slice_bitcast_fusion), channel_id=1, source_target_pairs={{0,2},{2,0},{4,6},{6,4},{8,10},{10,8},{12,14},{14,12},{16,18},{18,... | collective-permute-start | bytes 9437192 | tf_op jit(solution)/shard_map/ppermute | solution.py:625
  686.5 104.4 %collective-permute-start.63 = (bf16[4,2,64,2048]{3,2,1,0:T(8,128)(2,1)}, bf16[4,2,64,2048]{3,2,1,0:T(8,128)(2,1)S(1)}, u32[]{:S(2)}, u32[]{:S(2)}) collective-permute-start(bf16[4,2,64,2048]{3,2,1,0:T(8,128)(2,1)} %dynamic-slice_bitcast_fusion.3), channel_id=1, source_target_pairs={{0,2},{2,0},{4,6},{6,4},{8,10},{10,8},{12,14},{14,12},{16,18},{18,... | collective-permute-start | bytes 6291464 | tf_op jit(solution)/shard_map/ppermute | solution.py:625
  691.2 57.2 %collective-permute-start.45 = (bf16[256,2048]{1,0:T(8,128)(2,1)}, bf16[256,2048]{1,0:T(8,128)(2,1)S(1)}, u32[]{:S(2)}, u32[]{:S(2)}) collective-permute-start(bf16[256,2048]{1,0:T(8,128)(2,1)} %get-tuple-element.99), channel_id=1, source_target_pairs={{8,0},{10,2},{12,4},{14,6},{16,8},{18,10},{20,12},{22,14},{24,16},... | collective-permute-start | bytes 3145736 | tf_op jit(solution)/shard_map/ppermute | solution.py:637
  697.9 51.1 %collective-permute-start.43 = (bf16[256,2048]{1,0:T(8,128)(2,1)S(1)}, bf16[256,2048]{1,0:T(8,128)(2,1)S(1)}, u32[]{:S(2)}, u32[]{:S(2)}) collective-permute-start(bf16[256,2048]{1,0:T(8,128)(2,1)S(1)} %get-tuple-element.98), channel_id=1, source_target_pairs={{0,8},{2,10},{4,12},{6,14},{8,16},{10,18},{12,20},{14,22},{16,24},... | collective-permute-start | bytes 3145736 | tf_op jit(solution)/shard_map/ppermute | solution.py:637
  748.5 46.0 %collective-permute-start.81 = (bf16[4,256,512]{2,1,0:T(8,128)(2,1)}, bf16[4,256,512]{2,1,0:T(8,128)(2,1)S(1)}, u32[]{:S(2)}, u32[]{:S(2)}) collective-permute-start(bf16[4,256,512]{2,1,0:T(8,128)(2,1)} %dynamic-slice_convert_fusion), channel_id=1, source_target_pairs={{0,1},{1,0},{2,3},{3,2},{4,5},{5,4},{6,7},{7,6},{8,9},{9,8},{10,11... | collective-permute-start | bytes 3145736 | tf_op jit(solution)/shard_map/ppermute | solution.py:631
  750.0 38.0 %collective-permute-start.90 = (bf16[256,2048]{1,0:T(8,128)(2,1)}, bf16[256,2048]{1,0:T(8,128)(2,1)S(1)}, u32[]{:S(2)}, u32[]{:S(2)}) collective-permute-start(bf16[256,2048]{1,0:T(8,128)(2,1)} %dynamic-slice_bitcast_fusion.5), channel_id=1, source_target_pairs={{0,4},{2,6},{4,0},{6,2},{8,12},{10,14},{12,8},{14,10},{16,20},{18,... | collective-permute-start | bytes 3145736 | tf_op jit(solution)/shard_map/ppermute | solution.py:628
  796.2 39.3 %collective-permute-start.46 = (bf16[256,2048]{1,0:T(8,128)(2,1)S(1)}, bf16[256,2048]{1,0:T(8,128)(2,1)S(1)}, u32[]{:S(2)}, u32[]{:S(2)}) collective-permute-start(bf16[256,2048]{1,0:T(8,128)(2,1)S(1)} %get-tuple-element.93), channel_id=1, source_target_pairs={{0,1},{1,0},{2,3},{3,2},{4,5},{5,4},{6,7},{7,6},{8,9},{9,8},{10,11... | collective-permute-start | bytes 3145736 | tf_op jit(solution)/shard_map/ppermute | solution.py:631
  839.6 51.1 %collective-permute-start.56 = (bf16[4,128,1536]{2,1,0:T(8,128)(2,1)S(1)}, bf16[4,128,1536]{2,1,0:T(8,128)(2,1)S(1)}, u32[]{:S(2)}, u32[]{:S(2)}) collective-permute-start(bf16[4,128,1536]{2,1,0:T(8,128)(2,1)S(1)} %dynamic-slice_bitcast_fusion.4), channel_id=1, source_target_pairs={{0,4},{2,6},{4,0},{6,2},{8,12},{10,14},{12,8},{14,10},{16,20},{18,... | collective-permute-start | bytes 4718600 | tf_op jit(solution)/shard_map/ppermute | solution.py:628
  859.9 37.2 %collective-permute-start.66 = (bf16[64,2048]{1,0:T(8,128)(2,1)S(1)}, bf16[64,2048]{1,0:T(8,128)(2,1)S(1)}, u32[]{:S(2)}, u32[]{:S(2)}) collective-permute-start(bf16[64,2048]{1,0:T(8,128)(2,1)S(1)} %bitcast_convert_fusion.1), channel_id=1, source_target_pairs={{24,16},{26,18},{28,20},{30,22},{25,17},{27,19},{29,21},{31,23}} | collective-permute-start | bytes 786440 | tf_op jit(solution)/shard_map/ppermute | solution.py:637
  860.6 36.5 %collective-permute-start.65 = (bf16[64,2048]{1,0:T(8,128)(2,1)S(1)}, bf16[64,2048]{1,0:T(8,128)(2,1)S(1)}, u32[]{:S(2)}, u32[]{:S(2)}) collective-permute-start(bf16[64,2048]{1,0:T(8,128)(2,1)S(1)} %bitcast_convert_fusion.1), channel_id=1, source_target_pairs={{0,8},{2,10},{4,12},{6,14},{1,9},{3,11},{5,13},{7,15}} | collective-permute-start | bytes 786440 | tf_op jit(solution)/shard_map/ppermute | solution.py:637
  (134 other events, 2218.3 us)

commit v3 on v2

--- a/solution.py
+++ b/solution.py
@@ -3,6 +3,7 @@
 
 import jax
 import jax.numpy as jnp
+import numpy as np
 from jax import lax
 from jax.experimental import pallas as pl
 from jax.experimental.pallas import tpu as pltpu
@@ -22,15 +23,13 @@
 
 def angle_tables(count, head_dim, lanes):
     half_dim = head_dim // 2
-    freq = jnp.exp(
-        jnp.arange(half_dim, dtype=jnp.float32) * (-2.0 * math.log(ROPE_BASE) / head_dim)
-    )
-    turned = jnp.arange(count, dtype=jnp.int32).astype(jnp.float32)[:, None] * freq[None, :]
-    cosine, sine = jnp.cos(turned), jnp.sin(turned)
+    freq = ROPE_BASE ** (np.arange(half_dim) * (-2.0 / head_dim))
+    turned = np.arange(count)[:, None] * freq[None, :]
+    cosine, sine = np.cos(turned).astype(np.float32), np.sin(turned).astype(np.float32)
     repeats = lanes // head_dim
     return (
-        jnp.tile(jnp.concatenate([cosine, cosine], 1), (1, repeats)),
-        jnp.tile(jnp.concatenate([-sine, sine], 1), (1, repeats)),
+        jnp.asarray(np.tile(np.concatenate([cosine, cosine], 1), (1, repeats))),
+        jnp.asarray(np.tile(np.concatenate([-sine, sine], 1), (1, repeats))),
     )
 
 
@@ -90,8 +89,9 @@
     return (col <= row) & (col < length)
 
 
-def attend_kernel(block, scale, length, q, k, v, cosine, sine, q_gain, k_gain, out, totals):
-    second = pl.program_id(0) % 2 == 1
+def attend_kernel(
+    block, scale, second, length, q, k, v, cosine, sine, q_gain, k_gain, out, totals
+):
     rows = q.shape[0]
     cos, sin = cosine[...], sine[...]
     keys = one_head(head_turn(head_norm(k[...])[0] * k_gain[...], cos, sin), second).astype(BF)
@@ -215,29 +215,6 @@
         pl.BlockSpec((1, LANES), lambda g: (0, 0)),
         pl.BlockSpec((1, LANES), lambda g: (0, 0)),
     ]
-
-
-def attend(length, qkv, tables, gains, q_cols, k_heads):
-    rows = qkv.shape[0]
-    group = q_cols // HEAD // k_heads
-    block = rows // 2
-    return pl.pallas_call(
-        functools.partial(attend_kernel, block, 1.0 / math.sqrt(HEAD)),
-        grid=(k_heads,),
-        in_specs=attention_specs(rows, group, k_heads, q_cols),
-        out_specs=[
-            pl.BlockSpec((rows, group * HEAD), lambda g: (0, g)),
-            pl.BlockSpec((rows, LANES), lambda g: (0, g)),
-        ],
-        out_shape=[
-            jax.ShapeDtypeStruct((rows, q_cols), BF),
-            jax.ShapeDtypeStruct((rows, k_heads * LANES), F32),
-        ],
-        compiler_params=pltpu.CompilerParams(vmem_limit_bytes=40 << 20),
-        cost_estimate=pl.CostEstimate(
-            flops=20 * rows * rows * q_cols, bytes_accessed=8 << 20, transcendentals=rows * rows
-        ),
-    )(length, qkv, qkv, qkv, *tables, *gains)
 
 
 def attend_back(length, qkv, tables, gains, totals, grad_out, q_cols, k_heads):
@@ -406,13 +383,20 @@
     pl.semaphore_wait(barrier, len(devices))
 
 
-def gather_kernel(side, piece, sliced, *refs):
-    w_query, w_key, w_value, w_out, w_gate, w_up, w_down = refs[:7]
-    outs = refs[7:11]
-    qkv, out, units, down = bufs = refs[11:15]
-    load_sems, send_sems, qkv_sems, out_sems, unit_sems, down_sems, store_sems = refs[15:]
+def start_kernel(side, piece, sliced, scale, *refs):
+    w_query, w_key, w_value, w_out, w_gate, w_up, w_down, dm_own = refs[:8]
+    length, hidden, token_half, cosine, sine, q_gain, k_gain, ffn_gain = refs[8:16]
+    outs = refs[16:21]
+    proj, attended, totals, h_one, hidden_two = refs[21:26]
+    qkv, out, units, down, dm = bufs = refs[26:31]
+    part, cross_sent, cross_got = refs[31:34]
+    (
+        load_sems, send_sems, qkv_sems, out_sems, unit_sems, pair_sems, down_sems,
+        line_sems, core_sems, cross_sem, store_sems,
+    ) = refs[34:]
     t, j, c, x = coordinates()
     bits = side.bit_length() - 1
+    strip = side * piece
 
     def at(tt, jj, cc, xx=None):
         return (((tt * side) + jj) * 2 + cc, x if xx is None else xx)
@@ -428,15 +412,24 @@
         at((t + dt) % LINE, j, c ^ dc) for dt in range(LINE) for dc in range(2) if dt or dc
     ]
     mine = block(t, j, c)
-    q_cols, k_cols = w_query.shape[1], w_key.shape[1]
+    depth, q_cols = w_query.shape
+    k_cols = w_key.shape[1]
+    half, width = dm_own.shape
+
+    def rows_of(buf, idx):
+        count = depth if buf is qkv else w_out.shape[0]
+        return buf.at[pl.ds(pl.multiple_of(idx * count, count), count)]
+
+    own_qkv = pl.ds(pl.multiple_of(mine * depth, depth), depth)
     loads = [
-        (w_query, qkv.at[mine, :, pl.ds(0, q_cols)]),
-        (w_key, qkv.at[mine, :, pl.ds(q_cols, k_cols)]),
-        (w_value, qkv.at[mine, :, pl.ds(q_cols + k_cols, k_cols)]),
-        (w_out, out.at[mine]),
+        (w_query, qkv.at[own_qkv, pl.ds(0, q_cols)]),
+        (w_key, qkv.at[own_qkv, pl.ds(q_cols, k_cols)]),
+        (w_value, qkv.at[own_qkv, pl.ds(q_cols + k_cols, k_cols)]),
+        (w_out, rows_of(out, mine)),
         (w_down, down.at[x * side + j]),
+        (dm_own, dm.at[t, pl.ds(0, half)]),
     ]
-    depth = w_query.shape[0]
+    first_unit = len(loads)
 
     def unit_block(which, tt, jj, cc):
         weight = (w_gate, w_up)[which]
@@ -446,9 +439,15 @@
         return weight.at[tt, cc]
 
     def unit_target(which, tt, jj, cc):
-        if sliced:
-            return units.at[which, tt * 2 + cc, :, pl.ds(jj * piece, piece)]
-        return units.at[which, tt * 2 + cc]
+        col = x * strip + (jj * piece if sliced else 0)
+        size = piece if sliced else strip
+        return units.at[
+            which, tt, j, pl.ds(pl.multiple_of(cc * depth, depth), depth),
+            pl.ds(pl.multiple_of(col, size), size),
+        ]
+
+    def unit_pair(which, tt, jj, xx):
+        return units.at[which, tt, jj, :, pl.ds(pl.multiple_of(xx * strip, strip), strip)]
 
     parts = range(side) if sliced else range(1)
     loads += [
@@ -461,61 +460,54 @@
         load.start()
     greet(others + beside + [across])
     sends = Sends(send_sems)
-    for load in loads[:5]:
+    for load in loads[:first_unit]:
         load.wait()
 
     lines = ((qkv, qkv_sems), (out, out_sems))
 
     def spread(buf, sems, tt, r, cond):
         idx = block(tt, j ^ r, c)
+        ref = rows_of(buf, idx)
         for bit in range(bits):
             if (1 << bit) > r:
-                sends.start(buf.at[idx], buf.at[idx], sems.at[idx], beside[bit], cond)
-        sends.start(buf.at[idx], buf.at[idx], sems.at[idx], core, cond)
-
-    def pass_on(buf, sems, tt, to_right, to_left):
-        idx = block(tt, j, c)
+                sends.start(ref, ref, sems.at[idx], beside[bit], cond)
+        sends.start(ref, ref, sems.at[idx], core, cond)
+
+    def pass_on(ref, sem, to_right, to_left):
         if to_right is not False:
-            sends.start(buf.at[idx], buf.at[idx], sems.at[idx], at(t + 1, j, c), to_right)
+            sends.start(ref, ref, sem, at(t + 1, j, c), to_right)
         if to_left is not False:
-            sends.start(buf.at[idx], buf.at[idx], sems.at[idx], at(t - 1, j, c), to_left)
+            sends.start(ref, ref, sem, at(t - 1, j, c), to_left)
 
     def spread_rest(buf, sems, tt, cond):
         for r in range(1, side):
             idx = block(tt, j ^ r, c)
-            when(cond, lambda idx=idx: arrived(buf.at[idx], sems.at[idx], here))
+            when(cond, lambda idx=idx: arrived(rows_of(buf, idx), sems.at[idx], here))
             spread(buf, sems, tt, r, cond)
 
+    def line_places(k):
+        return ((t >= k, t - k, True), (t + k < LINE, t + k, False))
+
+    def forward(ref, sem, cond, rightward):
+        if rightward:
+            pass_on(ref, sem, both(cond, t < LINE - 1), False)
+        else:
+            pass_on(ref, sem, False, both(cond, t > 0))
+
     for buf, sems in lines:
-        pass_on(buf, sems, t, t < LINE - 1, t > 0)
+        pass_on(rows_of(buf, mine), sems.at[mine], t < LINE - 1, t > 0)
         spread(buf, sems, t, 0, None)
     own_down = x * side + j
     sends.start(down.at[own_down], down.at[own_down], down_sems.at[own_down], across)
     for bit in range(bits):
         sends.start(down.at[own_down], down.at[own_down], down_sems.at[own_down], beside[bit])
-    for dt in range(LINE):
-        for dc in range(2):
-            if dt or dc:
-                tt, cc = (t + dt) % LINE, c ^ dc
-                for w in range(2):
-                    for jj in parts:
-                        sends.start(
-                            unit_block(w, tt, jj, cc),
-                            unit_target(w, t, jj, c),
-                            unit_sems.at[w, t * 2 + c, jj],
-                            at(tt, j, cc),
-                        )
     for k in range(1, LINE):
         for buf, sems in lines:
-            from_left, from_right = t >= k, t + k < LINE
-            for cond, tt in ((from_left, t - k), (from_right, t + k)):
+            for cond, tt, rightward in line_places(k):
                 idx = block(tt, j, c)
-                when(cond, lambda idx=idx: arrived(buf.at[idx], sems.at[idx], here))
+                when(cond, lambda idx=idx: arrived(rows_of(buf, idx), sems.at[idx], here))
                 if k < LINE - 1:
-                    if tt is not None and cond is from_left:
-                        pass_on(buf, sems, tt, both(cond, t < LINE - 1), False)
-                    else:
-                        pass_on(buf, sems, tt, False, both(cond, t > 0))
+                    forward(rows_of(buf, idx), sems.at[idx], cond, rightward)
                 spread(buf, sems, tt, 0, cond)
             if k == 1:
                 spread_rest(buf, sems, t, None)
@@ -532,45 +524,185 @@
                             down.at[idx], down.at[idx], down_sems.at[idx], beside[bit]
                         )
                 sends.start(down.at[idx], down.at[idx], down_sems.at[idx], across)
+        if k == LINE - 2:
+            for dt in range(LINE):
+                for dc in range(2):
+                    if dt or dc:
+                        tt, cc = (t + dt) % LINE, c ^ dc
+                        for w in range(2):
+                            for jj in parts:
+                                sends.start(
+                                    unit_block(w, tt, jj, cc),
+                                    unit_target(w, t, jj, c),
+                                    unit_sems.at[w, t * 2 + c, jj],
+                                    at(tt, j, cc),
+                                )
     stores = []
 
-    def store(i):
-        copy = pltpu.make_async_copy(bufs[i], outs[i], store_sems.at[i])
+    def store(source, target):
+        copy = pltpu.make_async_copy(source, target, store_sems.at[len(stores)])
         copy.start()
         stores.append(copy)
 
-    for i, (buf, sems) in enumerate(lines):
+    def send_pair(w, tt, jj, xx, device):
+        ref = unit_pair(w, tt, jj, xx)
+        sends.start(ref, ref, pair_sems.at[w, tt, jj, xx], device)
+
+    def pair_came(w, tt, jj, xx):
+        arrived(unit_pair(w, tt, jj, xx), pair_sems.at[w, tt, jj, xx], here)
+
+    def unit_first(tt):
+        for cc in range(2):
+            mine = jnp.logical_and(tt == t, cc == c)
+            for w in range(2):
+                for jj in parts:
+                    when(
+                        jnp.logical_not(mine),
+                        lambda w=w, cc=cc, jj=jj: arrived(
+                            unit_target(w, tt, jj, cc), unit_sems.at[w, tt * 2 + cc, jj], here
+                        ),
+                    )
+        for w in range(2):
+            for bit in range(bits):
+                send_pair(w, tt, j, x, beside[bit])
+            send_pair(w, tt, j, x, across)
+
+    def unit_second(tt):
+        for r in range(1, side):
+            for w in (1, 0):
+                pair_came(w, tt, j ^ r, x)
+                for bit in range(bits):
+                    if (1 << bit) > r:
+                        send_pair(w, tt, j ^ r, x, beside[bit])
+            send_pair(1, tt, j ^ r, x, across)
+        pair_came(0, tt, j, 1 - x)
+        for bit in range(bits):
+            send_pair(0, tt, j, 1 - x, beside[bit])
+
+    def unit_last(tt):
+        for r in range(1, side):
+            pair_came(0, tt, j ^ r, 1 - x)
+            for bit in range(bits):
+                if (1 << bit) > r:
+                    send_pair(0, tt, j ^ r, 1 - x, beside[bit])
+        for r in range(side):
+            pair_came(1, tt, j ^ r, 1 - x)
+
+    dm_rows = dm.at[t, pl.ds(0, half)]
+
+    def dm_to_core(tt, cond):
+        sends.start(
+            dm.at[tt, pl.ds(0, half)], dm.at[tt, pl.ds(half, half)], core_sems.at[tt], core, cond
+        )
+
+    def dm_step(k):
+        for cond, tt, rightward in line_places(k):
+            ref = dm.at[tt, pl.ds(0, half)]
+            when(cond, lambda ref=ref, tt=tt: arrived(ref, line_sems.at[tt], here))
+            if k < LINE - 1:
+                forward(ref, line_sems.at[tt], cond, rightward)
+            dm_to_core(tt, cond)
+
+    def finish_line(buf, sems):
         spread_rest(buf, sems, t - LINE + 1, t >= LINE - 1)
         spread_rest(buf, sems, t + LINE - 1, t < 1)
         for tt in range(LINE):
             for jj in range(side):
                 idx = block(tt, jj, 1 - c)
-                arrived(buf.at[idx], sems.at[idx], here)
-        store(i)
-    for load in loads[5:]:
+                arrived(rows_of(buf, idx), sems.at[idx], here)
+
+    finish_line(*lines[0])
+    store(qkv, outs[0])
+    for load in loads[first_unit:]:
         load.wait()
-    for dt in range(LINE):
-        for dc in range(2):
-            if dt or dc:
-                tt, cc = (t + dt) % LINE, c ^ dc
-                for w in range(2):
-                    for jj in parts:
-                        arrived(
-                            unit_target(w, tt, jj, cc), unit_sems.at[w, tt * 2 + cc, jj], here
-                        )
-    store(2)
+    unit_first(t)
+    pass_on(dm_rows, line_sems.at[t], t < LINE - 1, t > 0)
+    dm_to_core(t, None)
+
+    tile = 256
+
+    @pl.loop(0, proj.shape[1] // tile)
+    def _(i):
+        cols = pl.ds(pl.multiple_of(i * tile, tile), tile)
+        proj[:, cols] = mm(hidden[...], qkv[:, cols])
+
+    rows = hidden.shape[0]
+    group = q_cols // k_cols * HEAD
+
+    @pl.loop(0, k_cols // HEAD)
+    def _(g):
+        pair = pl.multiple_of(g // 2 * LANES, LANES)
+        wide = pl.ds(pl.multiple_of(g * group, group), group)
+        attend_kernel(
+            rows // 2, scale, g % 2 == 1, length,
+            proj.at[:, wide],
+            proj.at[:, pl.ds(q_cols + pair, LANES)],
+            proj.at[:, pl.ds(q_cols + k_cols + pair, LANES)],
+            cosine, sine, q_gain, k_gain,
+            attended.at[:, wide],
+            totals.at[:, pl.ds(pl.multiple_of(g * LANES, LANES), LANES)],
+        )
+
+    finish_line(*lines[1])
+    store(out, outs[1])
+    wide = 512
+    other_rows = pl.ds(pl.multiple_of((1 - x) * half, half), half)
+    own_rows = pl.ds(pl.multiple_of(x * half, half), half)
+
+    @pl.loop(0, width // wide)
+    def _(i):
+        cols = pl.ds(pl.multiple_of(i * wide, wide), wide)
+        cross_sent[:, cols] = mm(attended[other_rows, :], out[:, cols]).astype(BF)
+
+    sends.start(cross_sent, cross_got, cross_sem, across)
+
+    @pl.loop(0, width // wide)
+    def _(i):
+        cols = pl.ds(pl.multiple_of(i * wide, wide), wide)
+        part[:, cols] = mm(attended[own_rows, :], out[:, cols])
+
+    for k in range(1, LINE):
+        unit_first(slot_place(t, k))
+    dm_step(1)
+    unit_second(t)
+
+    arrived(cross_got, cross_sem, here)
+    step = half // 8
+
+    @pl.loop(0, 8)
+    def _(i):
+        span = pl.ds(pl.multiple_of(i * step, step), step)
+        total = token_half[span, :].astype(F32) + part[span, :] + cross_got[span, :].astype(F32)
+        h_one[span, :] = total
+        hidden_two[span, :] = rms_scale(total, ffn_gain[...]).astype(BF)
+
+    unit_second(slot_place(t, 1))
+    dm_step(2)
+    unit_second(slot_place(t, 2))
+    unit_second(slot_place(t, 3))
+    dm_step(3)
+    for k in range(LINE):
+        unit_last(slot_place(t, k))
+    store(units, outs[2])
     for jj in range(side):
         idx = (1 - x) * side + jj
         arrived(down.at[idx], down_sems.at[idx], here)
-    store(3)
+    store(down, outs[3])
+    for tt in range(LINE):
+        arrived(dm.at[tt, pl.ds(half, half)], core_sems.at[tt], here)
+    store(dm, outs[4])
     sends.wait_sent()
     for copy in stores:
         copy.wait()
 
 
-def gather_weights(n, w_query, w_key, w_value, w_out, w_gate, w_up, w_down):
+def start_layer(n, weights, dm_own, length, hidden, token_half, tables, gains, ffn_gain):
+    w_query, w_key, w_value, w_out, w_gate, w_up, w_down = weights
     side = n // LINE // 2
     depth, piece, width = w_gate.shape[0], w_down.shape[0], w_down.shape[1]
+    rows, half = hidden.shape[0], dm_own.shape[0]
+    q_cols, k_cols = w_query.shape[1], w_key.shape[1]
+    cols = q_cols + 2 * k_cols
     strip = side * piece
     sliced = piece % LANES == 0
     if not sliced:
@@ -581,36 +713,564 @@
             for w in (w_gate, w_up)
         )
     shapes = [
-        (n, depth, w_query.shape[1] + 2 * w_key.shape[1]),
-        (n,) + w_out.shape,
-        (2, LINE * 2, depth, strip),
+        (width, cols),
+        (q_cols, width),
+        (2, LINE, side, 2 * depth, 2 * strip),
         (2 * side, piece, width),
+        (LINE, 2 * half, width),
     ]
     slots = 2 * LINE - 1
     line_sends = 2 * (LINE - 1) + slots * (2 * side - 1)
-    sends = 2 * line_sends + 2 * side - 1 + 14 * side
+    sends = 2 * line_sends + 2 * side - 1 + 14 * side + 3 * LINE + 8 + 8 * side * LINE
     any_space = pl.BlockSpec(memory_space=pl.ANY)
-    moved = 2 * sum(math.prod(shape) for shape in shapes)
+    vmem = pl.BlockSpec(memory_space=pltpu.VMEM)
     return pl.pallas_call(
-        functools.partial(gather_kernel, side, piece, sliced),
-        out_shape=[jax.ShapeDtypeStruct(shape, BF) for shape in shapes],
-        in_specs=[any_space] * 7,
-        out_specs=[any_space] * 4,
+        functools.partial(start_kernel, side, piece, sliced, 1.0 / math.sqrt(HEAD)),
+        out_shape=[jax.ShapeDtypeStruct(shape, BF) for shape in shapes]
+        + [
+            jax.ShapeDtypeStruct((rows, cols), F32),
+            jax.ShapeDtypeStruct((rows, q_cols), BF),
+            jax.ShapeDtypeStruct((rows, k_cols // HEAD * LANES), F32),
+            jax.ShapeDtypeStruct((half, width), F32),
+            jax.ShapeDtypeStruct((half, width), BF),
+        ],
+        in_specs=[any_space] * 8 + [pl.BlockSpec(memory_space=pltpu.SMEM)] + [vmem] * 7,
+        out_specs=[any_space] * 5 + [vmem] * 5,
         scratch_shapes=[pltpu.VMEM(shape, BF) for shape in shapes]
         + [
-            pltpu.SemaphoreType.DMA((5 + 2 * side,)),
+            pltpu.VMEM((half, width), F32),
+            pltpu.VMEM((half, width), BF),
+            pltpu.VMEM((half, width), BF),
+            pltpu.SemaphoreType.DMA((6 + 2 * side,)),
             pltpu.SemaphoreType.DMA((sends,)),
             pltpu.SemaphoreType.DMA((n,)),
             pltpu.SemaphoreType.DMA((n,)),
             pltpu.SemaphoreType.DMA((2, LINE * 2, side)),
+            pltpu.SemaphoreType.DMA((2, LINE, side, 2)),
             pltpu.SemaphoreType.DMA((2 * side,)),
-            pltpu.SemaphoreType.DMA((4,)),
+            pltpu.SemaphoreType.DMA((LINE,)),
+            pltpu.SemaphoreType.DMA((LINE,)),
+            pltpu.SemaphoreType.DMA,
+            pltpu.SemaphoreType.DMA((5,)),
         ],
         compiler_params=pltpu.CompilerParams(
-            collective_id=0, has_side_effects=True, vmem_limit_bytes=moved + (4 << 20)
+            collective_id=0, has_side_effects=True, vmem_limit_bytes=62 << 20
         ),
-        cost_estimate=pl.CostEstimate(flops=0, bytes_accessed=40 * moved, transcendentals=0),
-    )(w_query, w_key, w_value, w_out, w_gate, w_up, w_down)
+        cost_estimate=pl.CostEstimate(
+            flops=2 * rows * width * cols, bytes_accessed=500 << 20, transcendentals=rows * rows
+        ),
+    )(
+        w_query, w_key, w_value, w_out, w_gate, w_up, w_down, dm_own, length, hidden,
+        token_half, *tables, *gains, ffn_gain[None, :],
+    )
+
+
+def feed_kernel(side, *refs):
+    h_own, dm_all, units, down = refs[:4]
+    e_out, f_out, gate_kept, gate_got, up_kept, up_got, g_down = refs[4:11]
+    wg, wu, wd, h_all, dm, act, dg, du, e_stage, f_stage, f_send, f_core = refs[11:23]
+    load_sems, store_sems, send_sems, line_sems, core_sems, back_sems = refs[23:29]
+    done_sems, gate_sems, up_sems = refs[29:]
+    t, j, c, x = coordinates()
+    half, width = h_own.shape
+    unit_count = wd.shape[0]
+    strip = unit_count // 2
+    rows = 2 * half
+    bits = side.bit_length() - 1
+
+    def at(tt, cc, jj=None, xx=None):
+        jj, xx = j if jj is None else jj, x if xx is None else xx
+        return ((tt * side + jj) * 2 + cc, xx)
+
+    here, core, across = at(t, c), at(t, 1 - c), at(t, c, None, 1 - x)
+    beside = at(t, c, j ^ (side // 2))
+    others = [at((t + dt) % LINE, c) for dt in range(1, LINE)]
+    loads = [
+        (h_own, h_all.at[t, pl.ds(0, half)]),
+        (units.at[0], wg), (units.at[1], wu), (dm_all, dm), (down, wd),
+    ]
+    loads = [pltpu.make_async_copy(a, b, load_sems.at[i]) for i, (a, b) in enumerate(loads)]
+    for load in loads:
+        load.start()
+    greet(others + [core, across] + ([beside] if bits else []))
+    sends = Sends(send_sems)
+
+    def own_rows(tt):
+        return h_all.at[tt, pl.ds(0, half)]
+
+    def to_core(tt, cond):
+        sends.start(
+            own_rows(tt), h_all.at[tt, pl.ds(half, half)], core_sems.at[tt], core, cond
+        )
+
+    loads[0].wait()
+    sends.start(own_rows(t), own_rows(t), line_sems.at[t], at(t + 1, c), t < LINE - 1)
+    sends.start(own_rows(t), own_rows(t), line_sems.at[t], at(t - 1, c), t > 0)
+    to_core(t, None)
+    for load in loads[1:]:
+        load.wait()
+
+    tile = min(512, unit_count)
+    wide = min(1024, width)
+    e_stores, f_sent, stores = [], [], []
+
+    def store(source, target):
+        copy = pltpu.make_async_copy(source, target, store_sems.at[len(stores)])
+        copy.start()
+        stores.append(copy)
+        return copy
+
+    for k in range(LINE):
+        tt = slot_place(t, k)
+        if k:
+            for cond, place_of, forward, target in (
+                (t >= k, t - k, t < LINE - 1, t + 1),
+                (t + k < LINE, t + k, t > 0, t - 1),
+            ):
+                when(
+                    cond,
+                    lambda p=place_of: arrived(own_rows(p), line_sems.at[p], here),
+                )
+                if k < LINE - 1:
+                    sends.start(
+                        own_rows(place_of), own_rows(place_of), line_sems.at[place_of],
+                        at(target, c), jnp.logical_and(cond, forward),
+                    )
+                to_core(place_of, cond)
+        arrived(h_all.at[tt, pl.ds(half, half)], core_sems.at[tt], here)
+        if k >= 2:
+            f_sent[k - 2]()
+
+        @pl.loop(0, unit_count // tile)
+        def _(i):
+            cols = pl.ds(pl.multiple_of(i * tile, tile), tile)
+            hidden = h_all[tt]
+            gate = mm(hidden, wg[:, cols])
+            up = mm(hidden, wu[:, cols])
+            grad_act = mm_nt(dm[tt], wd[cols, :])
+            sigma = lax.logistic(gate)
+            silu = gate * sigma
+            act[tt, :, cols] = (silu * up).astype(BF)
+            dg[tt, :, cols] = (grad_act * up * (sigma * (1.0 + gate * (1.0 - sigma)))).astype(BF)
+            du[tt, :, cols] = (grad_act * silu).astype(BF)
+
+        slot = k % 2
+
+        @pl.loop(0, width // wide)
+        def _(i):
+            span = pl.ds(pl.multiple_of(i * wide, wide), wide)
+            grad = mm_nt(dg[tt], wg[span, :]) + mm_nt(du[tt], wu[span, :])
+            f_stage[k, :, span] = grad[:half].astype(BF)
+            f_send[slot, :, span] = grad[half:].astype(BF)
+
+        sends.start(f_send.at[slot], f_core.at[k], back_sems.at[k], core)
+        f_sent.append(lambda copy=sends.made.pop()[1]: copy().wait_send())
+        sends.made.append((None, None))
+        if k:
+            e_stores[k - 1].wait()
+
+        @pl.loop(0, width // wide)
+        def _(i):
+            span = pl.ds(pl.multiple_of(i * wide, wide), wide)
+            e_stage[:, span] = mm(act[tt], wd[:, span]).astype(BF)
+
+        e_stores.append(store(e_stage, e_out.at[tt]))
+        arrived(f_core.at[k], back_sems.at[k], here)
+
+        @pl.loop(0, 4)
+        def _(i):
+            part = pl.ds(pl.multiple_of(i * (half // 4), half // 4), half // 4)
+            f_stage[k, part, :] = (
+                f_stage[k, part, :].astype(F32) + f_core[k, part, :].astype(F32)
+            ).astype(BF)
+
+        if k == 0:
+            store(f_stage.at[0], f_out.at[t])
+        else:
+            sends.start(f_stage.at[k], f_out.at[t], done_sems.at[t], at(tt, c))
+
+    group = width // LINE
+    far = pl.ds(pl.multiple_of((1 - x) * strip, strip), strip)
+    near = pl.ds(pl.multiple_of(x * strip, strip), strip)
+
+    def weight_grad(target, grads, tt, send):
+        @pl.loop(0, 1)
+        def _(i):
+            span = pl.ds(tt * group, group)
+            hidden = h_all[:, :, span].reshape(LINE * rows, group)
+            target[span, :] = mm_tn(hidden, grads[...].reshape(LINE * rows, unit_count)).astype(BF)
+
+        send(tt)
+
+    block = group // side
+
+    def send_gate(tt):
+        span = pl.ds(tt * group, group)
+        sends.start(wg.at[span, far], gate_got.at[span], gate_sems.at[tt], across)
+        store(wg.at[span, near], gate_kept.at[span])
+
+    def send_up(tt):
+        for r in range(side):
+            span = pl.ds(pl.multiple_of(tt * group + (j ^ r) * block, block), block)
+            if r >= side // 2:
+                k = r - side // 2
+                sends.start(wu.at[span], up_got.at[k, tt], up_sems.at[k, tt], beside)
+            else:
+                store(wu.at[span], up_kept.at[r, tt])
+
+    for tt in range(LINE):
+        weight_grad(wg, dg, tt, send_gate)
+        weight_grad(wu, du, tt, send_up)
+    tile = min(256, unit_count)
+
+    @pl.loop(0, unit_count // tile)
+    def _(i):
+        cols = pl.ds(pl.multiple_of(i * tile, tile), tile)
+        units_part = act[:, :, cols].reshape(LINE * rows, tile)
+        wd[cols, :] = mm_tn(units_part, dm[...].reshape(LINE * rows, width)).astype(BF)
+
+    store(wd, g_down)
+    for sent in f_sent[LINE - 2 :]:
+        sent()
+    sends.made = [item for item in sends.made if item[1] is not None]
+    sends.wait_sent()
+    for copy in stores:
+        if all(copy is not early for early in e_stores[:-1]):
+            copy.wait()
+    for dt in range(1, LINE):
+        p = (t + dt) % LINE
+        arrived(f_out.at[p], done_sems.at[p], here)
+    for tt in range(LINE):
+        arrived(gate_got.at[pl.ds(tt * group, group)], gate_sems.at[tt], here)
+        for k in range(side // 2):
+            arrived(up_got.at[k, tt], up_sems.at[k, tt], here)
+
+
+def feed_forward(side, h_own, dm_all, units, down):
+    half, width = h_own.shape
+    unit_count = down.shape[0]
+    strip = unit_count // 2
+    rows = 2 * half
+    group = width // LINE
+    block = group // side
+    any_space = pl.BlockSpec(memory_space=pl.ANY)
+    outs = [
+        (LINE, rows, width),
+        (LINE, half, width),
+        (width, strip),
+        (width, strip),
+        (side // 2, LINE, block, unit_count),
+        (side // 2, LINE, block, unit_count),
+        (unit_count, width),
+    ]
+    held = [
+        (width, unit_count), (width, unit_count), (unit_count, width),
+        (LINE, rows, width), (LINE, rows, width),
+        (LINE, rows, unit_count), (LINE, rows, unit_count), (LINE, rows, unit_count),
+        (rows, width), (LINE, half, width), (2, half, width), (LINE, half, width),
+    ]
+    sends = 3 + 4 * (LINE - 1) + 2 * LINE + LINE + side // 2 * LINE
+    return pl.pallas_call(
+        functools.partial(feed_kernel, side),
+        out_shape=[jax.ShapeDtypeStruct(shape, BF) for shape in outs],
+        in_specs=[any_space] * 4,
+        out_specs=[any_space] * 7,
+        scratch_shapes=[pltpu.VMEM(shape, BF) for shape in held]
+        + [
+            pltpu.SemaphoreType.DMA((5,)),
+            pltpu.SemaphoreType.DMA((2 * LINE + 2 + side // 2 * LINE,)),
+            pltpu.SemaphoreType.DMA((sends,)),
+            pltpu.SemaphoreType.DMA((LINE,)),
+            pltpu.SemaphoreType.DMA((LINE,)),
+            pltpu.SemaphoreType.DMA((LINE,)),
+            pltpu.SemaphoreType.DMA((LINE,)),
+            pltpu.SemaphoreType.DMA((LINE,)),
+            pltpu.SemaphoreType.DMA((side // 2, LINE)),
+        ],
+        compiler_params=pltpu.CompilerParams(
+            collective_id=1, has_side_effects=True, vmem_limit_bytes=63 << 20
+        ),
+        cost_estimate=pl.CostEstimate(
+            flops=18 * LINE * rows * width * unit_count, bytes_accessed=100 << 20,
+            transcendentals=LINE * rows * unit_count,
+        ),
+    )(h_own, dm_all, units, down)
+
+
+def sum_kernel(side, piece, *refs):
+    g_qkv, gate, gate_got, up, up_got, down, down_got, small = refs[:8]
+    q_out, k_out, v_out, gate_out, up_out, down_out, small_out = refs[8:15]
+    (
+        heads, heads_core, heads_side, line_right, line_left,
+        gates, gates_got, gates_side, ups, ups_got, ups_across,
+        downs, downs_got, downs_across, homes, smalls,
+    ) = refs[15:31]
+    load_sems, send_sems, core_sems, side_sems, line_sems, gate_sems, across_sems = refs[31:38]
+    home_sems, small_sems = refs[38:]
+    t, j, c, x = coordinates()
+    bits = side.bit_length() - 1
+    depth, q_cols = q_out.shape
+    k_cols = k_out.shape[1]
+    strip = side * piece
+
+    def at(tt, jj, cc, xx=None):
+        return (((tt * side) + jj) * 2 + cc, x if xx is None else xx)
+
+    def block(tt, jj, cc):
+        return ((tt * side) + jj) * 2 + cc
+
+    here, core, across = at(t, j, c), at(t, j, 1 - c), at(t, j, c, 1 - x)
+    beside = [at(t, j ^ (1 << bit), c) for bit in range(bits)]
+    others = [
+        at((t + dt) % LINE, j, c ^ dc) for dt in range(LINE) for dc in range(2) if dt or dc
+    ]
+    near_col = pl.multiple_of(x * strip, strip)
+    loads = [
+        (g_qkv, heads),
+        (gate, gates),
+        (gate_got, gates_got),
+        (up, ups),
+        (up_got, ups_got),
+        (down, downs),
+        (down_got, downs_got),
+        (small, smalls.at[0]),
+    ]
+    loads = [pltpu.make_async_copy(a, b, load_sems.at[i]) for i, (a, b) in enumerate(loads)]
+    for load in loads:
+        load.start()
+    greet(others + beside + [across])
+    sends = Sends(send_sems)
+
+    def add(target, first, second):
+        count = first.shape[0]
+        step = min(64, count)
+
+        @pl.loop(0, count // step)
+        def _(i):
+            part = pl.ds(pl.multiple_of(i * step, step), step)
+            target[part, :] = (first[part, :].astype(F32) + second[part, :].astype(F32)).astype(
+                target.dtype
+            )
+
+    loads[0].wait()
+    for q in reversed(range(LINE)):
+        tt = slot_place(t, q)
+        for r in range(side):
+            sends.start(
+                heads.at[block(tt, j ^ r, 1 - c)], heads_core.at[tt, j ^ r],
+                core_sems.at[tt, j ^ r], core,
+            )
+    loads[1].wait()
+    loads[2].wait()
+    for tt in range(LINE):
+        for jj in range(side):
+            add(gates.at[tt, jj], gates.at[tt, jj], gates_got.at[tt, jj])
+    for bit in reversed(range(bits)):
+        half = 1 << bit
+        if bit < bits - 1:
+            for r in range(half * 2):
+                arrived(gates_side.at[2 * half - 1 + r], gate_sems.at[2 * half - 1 + r], here)
+                for tt in range(LINE):
+                    add(
+                        gates.at[tt, j ^ r], gates.at[tt, j ^ r],
+                        gates_side.at[2 * half - 1 + r, tt],
+                    )
+        for r in range(half, 2 * half):
+            sends.start(
+                gates.at[:, j ^ r], gates_side.at[half - 1 + r - half],
+                gate_sems.at[half - 1 + r - half], beside[bit],
+            )
+    loads[5].wait()
+    loads[6].wait()
+    for xx in range(2):
+        add(downs.at[xx], downs.at[xx], downs_got.at[xx])
+    loads[3].wait()
+    loads[4].wait()
+    for tt in range(LINE):
+        add(ups.at[tt], ups.at[tt], ups_got.at[tt])
+    far_col = pl.multiple_of((1 - x) * strip, strip)
+    sends.start(
+        ups.at[:, :, pl.ds(far_col, strip)], ups_across, across_sems.at[0], across
+    )
+    sends.start(downs.at[1 - x], downs_across, across_sems.at[1], across)
+
+    loads[7].wait()
+    partners = [core] + beside + [across, at(t ^ 1, j, c), at(t ^ 2, j, c)]
+
+    def small_step(i):
+        if i:
+            arrived(smalls.at[2 * i], small_sems.at[i - 1], here)
+            smalls[2 * i - 1] = smalls[max(2 * i - 3, 0)] + smalls[2 * i]
+        if i < len(partners):
+            source = smalls.at[2 * i - 1] if i else smalls.at[0]
+            sends.start(source, smalls.at[2 * i + 2], small_sems.at[i], partners[i])
+        return i + 1
+
+    def side_first(q):
+        tt = slot_place(t, q)
+        for r in reversed(range(side)):
+            arrived(heads_core.at[tt, j ^ r], core_sems.at[tt, j ^ r], here)
+            mine = heads.at[block(tt, j ^ r, c)]
+            add(mine, mine, heads_core.at[tt, j ^ r])
+            if bits and r >= side // 2:
+                k = side // 2 - 1 + r - side // 2
+                sends.start(mine, heads_side.at[tt, k], side_sems.at[tt, k], beside[bits - 1])
+
+    def side_rest(q):
+        tt = slot_place(t, q)
+        for bit in reversed(range(bits)):
+            half = 1 << bit
+            for r in range(half):
+                arrived(heads_side.at[tt, half - 1 + r], side_sems.at[tt, half - 1 + r], here)
+                mine = heads.at[block(tt, j ^ r, c)]
+                add(mine, mine, heads_side.at[tt, half - 1 + r])
+                if bit and r >= half // 2:
+                    k = half // 2 - 1 + r - half // 2
+                    sends.start(
+                        mine, heads_side.at[tt, k], side_sems.at[tt, k], beside[bit - 1]
+                    )
+        return heads.at[block(tt, j, c)]
+
+    def line_came(i, way, cond, target):
+        line = (line_right, line_left)[way]
+
+        def act():
+            arrived(line.at[i], line_sems.at[way, i], here)
+            add(target, target, line.at[i])
+
+        when(cond, act)
+
+    def line_go(i, way, cond, source):
+        line = (line_right, line_left)[way]
+        sends.start(
+            source, line.at[i], line_sems.at[way, i], at(t + 1 - 2 * way, j, c), cond
+        )
+
+    step = small_step(0)
+    side_first(3)
+    side_first(2)
+    step = small_step(step)
+    p3 = side_rest(3)
+    line_go(0, 0, t == 0, p3)
+    line_go(0, 1, t == 3, p3)
+    side_first(1)
+    step = small_step(step)
+    p2 = side_rest(2)
+    line_came(0, 0, t == 1, p2)
+    line_came(0, 1, t == 2, p2)
+    line_go(1, 0, t <= 1, p2)
+    line_go(1, 1, t >= 2, p2)
+    side_first(0)
+
+    def go_home(which, rows):
+        for tt in range(LINE):
+            for cc in range(2):
+                mine = jnp.logical_and(t == tt, c == cc)
+                source = rows(tt).at[pl.ds(cc * depth, depth)]
+                target = homes.at[which, t * 2 + c]
+                sends.start(
+                    source, target, home_sems.at[which, t * 2 + c], at(tt, j, cc),
+                    jnp.logical_not(mine),
+                )
+
+                @pl.when(mine)
+                def _():
+                    homes[which, tt * 2 + cc] = source[...]
+
+    if bits:
+        arrived(gates_side.at[0], gate_sems.at[0], here)
+        for tt in range(LINE):
+            add(gates.at[tt, j], gates.at[tt, j], gates_side.at[0, tt])
+    go_home(0, lambda tt: gates.at[tt, j])
+    step = small_step(step)
+    p1 = side_rest(1)
+    line_came(1, 0, jnp.logical_and(t >= 1, t <= 2), p3)
+    line_came(1, 1, jnp.logical_and(t >= 1, t <= 2), p1)
+    line_go(2, 0, t == 0, p1)
+    line_go(2, 0, jnp.logical_and(t >= 1, t <= 2), p3)
+    line_go(2, 1, t >= 1, p1)
+    arrived(ups_across, across_sems.at[0], here)
+    for tt in range(LINE):
+        add(ups_across.at[tt], ups.at[tt, :, pl.ds(near_col, strip)], ups_across.at[tt])
+    go_home(1, lambda tt: ups_across.at[tt])
+    while step <= len(partners):
+        step = small_step(step)
+    small_out[...] = smalls[2 * len(partners) - 1]
+    arrived(downs_across, across_sems.at[1], here)
+    add(down_out, downs.at[x], downs_across)
+    p0 = side_rest(0)
+    line_came(2, 0, t >= 1, p0)
+    line_came(2, 1, t <= 2, p0)
+    q_out[...] = p0[:, pl.ds(0, q_cols)].astype(F32)
+    k_out[...] = p0[:, pl.ds(q_cols, k_cols)].astype(F32)
+    v_out[...] = p0[:, pl.ds(q_cols + k_cols, k_cols)].astype(F32)
+    for which, out in enumerate((gate_out, up_out)):
+        for tt in range(LINE):
+            for cc in range(2):
+                mine = jnp.logical_and(t == tt, c == cc)
+                source = homes.at[which, tt * 2 + cc]
+                when(
+                    jnp.logical_not(mine),
+                    lambda w=which, k=tt * 2 + cc, ref=source: arrived(
+                        ref, home_sems.at[w, k], here
+                    ),
+                )
+                for jj in range(side):
+                    out[:, pl.ds(block(tt, jj, cc) * piece, piece)] = source[
+                        :, pl.ds(jj * piece, piece)
+                    ].astype(F32)
+    sends.wait_sent()
+
+
+def sum_gradients(n, piece, q_cols, g_qkv, gate, gate_got, up, up_got, down, down_got, small):
+    side = n // LINE // 2
+    bits = side.bit_length() - 1
+    _, depth, cols = g_qkv.shape
+    k_cols = (cols - q_cols) // 2
+    strip = side * piece
+    width = down.shape[-1]
+    any_space = pl.BlockSpec(memory_space=pl.ANY)
+    steps = bits + 4
+    held = [
+        (n, depth, cols), (LINE, side, depth, cols), (LINE, max(side - 1, 1), depth, cols),
+        (3, depth, cols), (3, depth, cols),
+        (LINE, side, 2 * depth, strip), (LINE, side, 2 * depth, strip),
+        (max(side - 1, 1), LINE, 2 * depth, strip),
+        (LINE, 2 * depth, 2 * strip), (LINE, 2 * depth, 2 * strip), (LINE, 2 * depth, strip),
+        (2, piece, width), (2, piece, width), (piece, width),
+        (2, LINE * 2, depth, strip),
+    ]
+    sends = LINE * (2 * side - 1) + side + 2 + steps + 8 + 4 * LINE + 4
+    return pl.pallas_call(
+        functools.partial(sum_kernel, side, piece),
+        out_shape=[
+            jax.ShapeDtypeStruct((depth, q_cols), F32),
+            jax.ShapeDtypeStruct((depth, k_cols), F32),
+            jax.ShapeDtypeStruct((depth, k_cols), F32),
+            jax.ShapeDtypeStruct((depth, LINE * 2 * strip), F32),
+            jax.ShapeDtypeStruct((depth, LINE * 2 * strip), F32),
+            jax.ShapeDtypeStruct((piece, width), F32),
+            jax.ShapeDtypeStruct(small.shape, F32),
+        ],
+        in_specs=[any_space] * 8,
+        scratch_shapes=[pltpu.VMEM(shape, BF) for shape in held]
+        + [pltpu.VMEM((2 * steps + 1,) + small.shape, F32)]
+        + [
+            pltpu.SemaphoreType.DMA((8,)),
+            pltpu.SemaphoreType.DMA((sends,)),
+            pltpu.SemaphoreType.DMA((LINE, side)),
+            pltpu.SemaphoreType.DMA((LINE, max(side - 1, 1))),
+            pltpu.SemaphoreType.DMA((2, 3)),
+            pltpu.SemaphoreType.DMA((max(side - 1, 1),)),
+            pltpu.SemaphoreType.DMA((2,)),
+            pltpu.SemaphoreType.DMA((2, LINE * 2)),
+            pltpu.SemaphoreType.DMA((steps,)),
+        ],
+        compiler_params=pltpu.CompilerParams(
+            collective_id=2, has_side_effects=True, vmem_limit_bytes=60 << 20
+        ),
+        cost_estimate=pl.CostEstimate(flops=0, bytes_accessed=400 << 20, transcendentals=0),
+    )(g_qkv, gate, gate_got, up, up_got, down, down_got, small)
 
 
 class Links:
@@ -660,6 +1320,20 @@
             jnp.where(t == 0, l3, jnp.where(t == 3, r3, l1)),
         )
 
+    def lines(self):
+        return [[i + k * self.inner for k in range(LINE)] for i in range(self.inner)]
+
+    def line_all(self, value):
+        return lax.all_gather(value, "dp", axis_index_groups=self.lines())
+
+    def line_sum(self, value):
+        return lax.psum_scatter(
+            value, "dp", scatter_dimension=0, axis_index_groups=self.lines()
+        )
+
+    def dp_sum(self, value):
+        return lax.psum_scatter(value, "dp", scatter_dimension=0, tiled=True)
+
     def line_scatter(self, parts):
         t = self.t
         p0, p1, p2, p3 = parts
@@ -699,6 +1373,21 @@
                 for a, b in zip(blocks[:width], blocks[width:])
             ]
         return blocks[0]
+
+    def side_start(self, blocks):
+        for bit in reversed(range(1, len(blocks).bit_length() - 1)):
+            half = 1 << bit
+            blocks = [
+                (a.astype(F32) + self.over(b, bit).astype(F32)).astype(BF)
+                for a, b in zip(blocks[:half], blocks[half:])
+            ]
+        return blocks[0], self.over(blocks[1], 0)
+
+    def side_end(self, kept, got):
+        if kept.shape[0] == 1:
+            return kept[0], got[0]
+        total = (kept.astype(F32) + got.astype(F32)).astype(BF)
+        return self.side_start(list(total))
 
     def pair_order(self, mine, other, where):
         low = jnp.where(where == 0, mine, other)
@@ -784,150 +1473,42 @@
         piece = w_down.shape[0]
         side = net.side
         strip = side * piece
-        qkv_full, wo_full, units, wd = gather_weights(
-            n, w_query, key_weight_matrix, value_weight_matrix, w_out, w_gate, w_up, w_down
-        )
-        qkv_full = qkv_full.reshape(width, q_cols + 2 * k_cols)
-        wo_full = wo_full.reshape(q_cols, width)
-        wd = wd.reshape(2 * strip, width)
-
-        gate_own = units[0].reshape(LINE * 2 * depth, strip)
-        up_own = units[1].reshape(LINE * 2 * depth, strip)
-        gate_pieces, up_pieces = [], []
-        for part in (gate_own, net.cross(gate_own)):
-            gate_pieces.append(net.side_all(part))
-        up_pieces.append(net.side_all(up_own))
-        up_pieces.append([net.cross(part) for part in up_pieces[0]])
-
-        def unit_weight(pieces):
-            def spots(t, j, c, x):
-                return [
-                    (
-                        s * side + r, tt * 2 * depth, 0, 2 * depth, strip,
-                        (tt * side + (j ^ r)) * 2 * depth, (x ^ s) * strip,
-                    )
-                    for s in range(2)
-                    for r in range(side)
-                    for tt in range(LINE)
-                ]
-
-            return place(pieces[0] + pieces[1], spots, (width, 2 * strip))
-
-        wg = unit_weight(gate_pieces)
-        wu = unit_weight(up_pieces)
-
         start = x * half
         half_positions = start + jnp.arange(half, dtype=jnp.int32)
         half_valid = (half_positions < slot_length)[:, None]
         grad_half = lax.dynamic_slice_in_dim(cotangent, start, half, 0)
         grad_half = jnp.where(half_valid, grad_half, jnp.zeros_like(grad_half))
-        grad_blocks = [
-            jnp.concatenate([block, net.core(block)], axis=0)
-            for block in net.line_gather(after(units, grad_half))
-        ]
-
         tables = angle_tables(row_count, head_dim, LANES)
         gains = [jnp.tile(gain, LANES // head_dim)[None, :] for gain in (query_gain, key_gain)]
         inputs = tokens.astype(F32)
+        input_half = lax.dynamic_slice_in_dim(tokens, start, half, 0)
         hidden_state = rms_scale(inputs, attn_gain).astype(BF)
-        qkv = mm(hidden_state, qkv_full)
         length = slot_length[None]
-        o_low, log_totals = attend(length, qkv, tables, gains, q_cols, k_heads)
-        attn_part = mm(o_low, wo_full).reshape(2, half, width)
-        input_half = lax.dynamic_slice_in_dim(inputs, start, half, 0)
-        h_one = input_half + net.cross_sum(attn_part, 0)
-        hidden_two = rms_scale(h_one, ffn_gain).astype(BF)
-
-        hidden_blocks = [
-            jnp.concatenate([block, net.core(block)], axis=0)
-            for block in net.line_gather(hidden_two)
-        ]
-
-        def core_sum(value):
-            low = value[half:].astype(BF)
-            return value[:half] + net.core(low).astype(F32)
-
-        out_parts, grad_parts, acts, grad_gates, grad_ups = [], [], [], [], []
-        for hidden, grad in zip(hidden_blocks, grad_blocks):
-            gate = mm(hidden, wg)
-            up_proj = mm(hidden, wu)
-            sigmoid_gate = jax.nn.sigmoid(gate)
-            silu_gate = gate * sigmoid_gate
-            act = (silu_gate * up_proj).astype(BF)
-            out_parts.append(core_sum(mm(act, wd)))
-            grad_act = mm_nt(grad, wd)
-            silu_slope = sigmoid_gate * (1.0 + gate * (1.0 - sigmoid_gate))
-            grad_gate = (grad_act * up_proj * silu_slope).astype(BF)
-            grad_up = (grad_act * silu_gate).astype(BF)
-            grad_parts.append(core_sum(mm_nt(grad_gate, wg) + mm_nt(grad_up, wu)))
-            acts.append(act)
-            grad_gates.append(grad_gate)
-            grad_ups.append(grad_up)
-
-        grad_hidden_two = net.line_send(grad_parts)
-        out_parts = after(grad_hidden_two, *out_parts)
-        layer_half = (h_one + net.line_scatter(out_parts)).astype(BF)
-        layer_out = net.pair_order(layer_half, net.cross(layer_half), x)
+        weights = (w_query, key_weight_matrix, value_weight_matrix, w_out, w_gate, w_up, w_down)
+        (
+            qkv_full, wo_full, units, wd, grad_all, qkv, o_low, log_totals, h_one, hidden_two,
+        ) = start_layer(
+            n, weights, grad_half, length, hidden_state, input_half, tables, gains, ffn_gain
+        )
+
+        out_parts, grad_parts, gate_kept, gate_got, up_kept, up_got, g_down = feed_forward(
+            side, hidden_two, grad_all, units.reshape(2, width, 2 * strip),
+            wd.reshape(2 * strip, width),
+        )
+        grad_hidden_two = jnp.sum(grad_parts.astype(F32), axis=0)
+        out_mine = out_parts[:, :half].astype(F32) + net.core(out_parts[:, half:]).astype(F32)
+        out_sum = net.line_sum(out_mine.astype(BF))
         norm_two_back = jax.vjp(rms_scale, h_one, ffn_gain)[1]
         grad_h_part, g_ffn_part = norm_two_back(grad_hidden_two)
         grad_h_one = grad_half.astype(F32) + grad_h_part
         grad_attn_half = grad_h_one.astype(BF)
         grad_attn_low = net.pair_order(grad_attn_half, net.cross(grad_attn_half), x)
 
-        acts[0], grad_gates[0], grad_ups[0] = after(
-            grad_parts, acts[0], grad_gates[0], grad_ups[0]
-        )
-        act_all = jnp.concatenate(acts, 0)
-        hidden_all = jnp.concatenate(hidden_blocks, 0)
-        grad_all = jnp.concatenate(grad_blocks, 0)
-        g_gate = mm_tn(hidden_all, jnp.concatenate(grad_gates, 0)).astype(BF)
-        g_up = mm_tn(hidden_all, jnp.concatenate(grad_ups, 0)).astype(BF)
-        g_down = mm_tn(act_all, grad_all).astype(BF)
-
-        def home_units(value):
-            rows = value.reshape(LINE, 2 * depth, strip)
-            blocks = []
-            for shift in range(LINE):
-                block = net.pick(rows, (t + shift) % LINE, 0)
-                block = block if shift == 0 else net.turn(block, shift)
-                block = block.reshape(2, depth, strip)
-                blocks.append(net.pick(block, c, 0))
-                blocks.append(net.core(net.pick(block, 1 - c, 0)))
-            if piece % 128:
-                stacked = jnp.stack(blocks).reshape(LINE, 2, depth, side, piece)
-                order_t = (t - jnp.arange(LINE)) % LINE
-                stacked = jnp.take(stacked, order_t, axis=0)
-                stacked = jnp.take(stacked, c ^ jnp.arange(2), axis=1)
-                return stacked.transpose(2, 0, 3, 1, 4).reshape(depth, LINE * 2 * strip)
-
-            def spots(t, j, c, x):
-                return [
-                    (
-                        2 * shift + s, 0, r * piece, depth, piece, 0,
-                        ((((t - shift) % LINE) * side + r) * 2 + (c ^ s)) * piece,
-                    )
-                    for shift in range(LINE)
-                    for s in range(2)
-                    for r in range(side)
-                ]
-
-            return place(blocks, spots, (depth, LINE * 2 * strip))
-
-        def side_rows(value):
-            rows = value.reshape(LINE, side, 2 * depth, value.shape[1])
-            return [net.pick(rows, j ^ r, 1) for r in range(side)]
-
-        def cross_cols(value):
-            kept = lax.dynamic_slice_in_dim(value, x * strip, strip, value.ndim - 1)
-            sent = lax.dynamic_slice_in_dim(value, (1 - x) * strip, strip, value.ndim - 1)
-            return kept.astype(F32) + net.cross(sent.astype(BF)).astype(F32)
-
-        gate_sum = net.side_sum(side_rows(cross_cols(g_gate).astype(BF))).astype(BF)
-        up_sum = cross_cols(net.side_sum(side_rows(g_up))).astype(BF)
-        g_gate_out = home_units(gate_sum).astype(F32)
-        g_up_out = home_units(up_sum).astype(F32)
-        down_sum = net.cross_sum(g_down.reshape(2, side, piece, width), 0).astype(BF)
-        g_down_out = net.side_sum([net.pick(down_sum, j ^ r, 0) for r in range(side)])
+        near = (LINE, side, 2 * depth, strip)
+        gate_kept, gate_got = gate_kept.reshape(near), gate_got.reshape(near)
+        up_kept, up_got = net.side_end(up_kept, up_got)
+        g_down = g_down.reshape(2, side, piece, width)
+        down_kept, down_got = net.side_start([net.pick(g_down, j ^ r, 1) for r in range(side)])
 
         g_out = mm_tn(o_low, grad_attn_low).astype(BF)
         grad_o_low = mm_nt(grad_attn_low, wo_full).astype(BF)
@@ -938,25 +1519,31 @@
         g_key_part = k_part.reshape(-1, head_dim).sum(0)
         grad_qkv = jnp.concatenate([grad_q, grad_k, grad_v], axis=1)
         g_qkv = mm_tn(hidden_state, grad_qkv).astype(BF)
-        g_out_out = net.sum_rows(g_out)
-        g_qkv_out = net.sum_rows(g_qkv)
-        grad_hidden = mm_nt(grad_qkv, qkv_full).reshape(2, half, width)
-        grad_hidden_half = net.cross_sum(grad_hidden, 0)
-        norm_one_back = jax.vjp(rms_scale, input_half, attn_gain)[1]
-        grad_in_half, g_attn_part = norm_one_back(grad_hidden_half)
-        input_grad_half = (grad_h_one + grad_in_half).astype(BF)
-        input_grad = net.pair_order(input_grad_half, net.cross(input_grad_half), x).astype(F32)
+        g_out_out = net.dp_sum(g_out).astype(F32)
+        layer_half = (h_one + after(g_qkv, out_sum).astype(F32)).astype(BF)
+        layer_out = net.pair_order(layer_half, net.cross(layer_half), x)
+        grad_hidden = mm_nt(grad_qkv, qkv_full)
+        g_attn_part = jnp.sum(grad_hidden * rms_scale(inputs, 1.0), axis=0)
+        low_hidden = grad_hidden.astype(BF)
+        grad_hidden = low_hidden.astype(F32) + net.cross(low_hidden).astype(F32)
         small = jnp.concatenate([g_attn_part, g_ffn_part, g_query_part, g_key_part])
-        small = net.total(small)
+        small = small.reshape(-1, LANES)
+        g_query_w, g_key_w, g_value_w, g_gate_out, g_up_out, g_down_out, small = sum_gradients(
+            n, piece, q_cols, g_qkv.reshape(n, depth, q_cols + 2 * k_cols),
+            gate_kept, gate_got, up_kept, up_got, down_kept, down_got, small,
+        )
+        small = small.reshape(-1)
+        grad_in = jax.vjp(lambda v: rms_scale(v, attn_gain), inputs)[1](grad_hidden)[0]
+        input_grad = grad_attn_low.astype(F32) + grad_in
         return (
             layer_out,
             input_grad,
             small[:width],
             small[2 * width : 2 * width + head_dim],
             small[2 * width + head_dim :],
-            g_qkv_out[:, :q_cols],
-            g_qkv_out[:, q_cols : q_cols + k_cols],
-            g_qkv_out[:, q_cols + k_cols :],
+            g_query_w,
+            g_key_w,
+            g_value_w,
             g_out_out,
             small[width : 2 * width],
             g_gate_out,

time: 945 us -> 723 us (0.77); the launches traced: 935 us -> 729 us
  Pallas kernels: 148 us -> 535 us
  waiting for transfers between devices: 359 us -> 86.1 us
  starting transfers between devices: 132 us -> 3.59 us
  matrix products: 144 us -> 26.4 us
  local copies, waits for them, and re-layouts: 73.1 us -> 27.3 us
  other arithmetic: 75.1 us -> 35.6 us
  between operations: 3.2 us -> 14.7 us
    pallas_call x6 -> x3, Pallas kernels: 122 us -> 509 us  [the longest x1 203 us: start_layer(): pl.pallas_call(functools.partial(start_kernel, side, piece, sliced, 1.0 /...]
    ppermute x43 -> x0, waiting for transfers between devices: 185 us -> none  [along(): return lax.ppermute(value, 'dp', pairs)]
    ppermute x43 -> x0, starting transfers between devices: 110 us -> none  [along(): return lax.ppermute(value, 'dp', pairs)]
    ppermute x9 -> x1, waiting for transfers between devices: 85.2 us -> 11.9 us  [over(): return lax.ppermute(value, 'dp', [(i, i ^ 2 << bit) for i in range(self.n)])]
    dot_general x14 -> x0, matrix products: 52.3 us -> none  [mm(): return jnp.dot(left, right, preferred_element_type=F32)]
    dot_general x5 -> x2, matrix products: 46 us -> 13 us  [mm_tn(): lax.dot_general(left, right, (((0,), (0,)), ((), ())), preferred_element_...]
    dot_general x14 -> x2, matrix products: 46.1 us -> 13.5 us  [mm_nt(): lax.dot_general(left, right, (((1,), (1,)), ((), ())), preferred_element_...]
    ppermute x12 -> x3, waiting for transfers between devices: 85.9 us -> 67 us  [cross(): return lax.ppermute(value, 'tensor', [(0, 1), (1, 0)])]
  transfers between devices with their start and end apart: 91 -> 7, of which waited for: 33 -> 5; matrix products, arithmetic and copies ran while one was open for 26% -> 8% of each run, Pallas kernels for 3% -> 20%
where the time goes in v3:
time: 723 us; the launch traced here: 729 us
  Pallas kernels  535 us (74%)
  waiting for transfers between devices  86.1 us (12%)
  other arithmetic  35.6 us (5%)
  local copies, waits for them, and re-layouts  27.3 us (4%)
  matrix products  26.4 us (4%)
  between operations  14.7 us (2%)
    pallas_call x1, Pallas kernels, start_layer(): pl.pallas_call(functools.partial(start_kernel, side, piece, sliced, 1.0 /...  203 us
    pallas_call x1, Pallas kernels, feed_forward(): pl.pallas_call(functools.partial(feed_kernel, side), out_shape=[jax.Shape...  188 us
    pallas_call x1, Pallas kernels, sum_gradients(): pl.pallas_call(functools.partial(sum_kernel, side, piece), out_shape=[jax...  117 us
    ppermute x3, waiting for transfers between devices, cross(): return lax.ppermute(value, 'tensor', [(0, 1), (1, 0)])  67 us
    pallas_call x1, Pallas kernels, attend_back(): pl.pallas_call(functools.partial(attend_back_kernel, block, 1.0 / math.sq...  26.5 us
    unnamed x70, local copies, waits for them, and re-layouts  14.5 us
  transfers between devices with their start and end apart: 7, of which 5 were waited for; matrix products, arithmetic and copies ran while one was open for 8% of the time, Pallas kernels for 20%

profile of v3, /device:TPU:0, one launch (start us, length us, event | category | flops | bytes accessed | tf_op | source)
XLA Modules:
  0.0 729.0 jit_solution(16757979461114754433)
XLA Ops:
  7.3 1.4 dynamic_slice.16.refs_8_.length
  8.6 0.7 add_compare_fusion
  9.3 2.1 fusion.5
  12.6 1.9 fusion.2.refs_9_
  14.5 1.6 dynamic-slice_select_fusion
  16.1 203.1 %shard_map.255 = (bf16[2048,1536]{1,0:T(8,128)(2,1)}, bf16[1024,2048]{1,0:T(8,128)(2,1)}, bf16[2,4,2,256,1024]{4,3,2,1,0:T(8,128)(2,1)}, bf16[4,256,2048]{2,1,0:...) custom-call(bf16[128,1024]{1,0:T(8,128)(2,1)} %refs_0_.1, ...), custom_call_target="tpu_custom_call" | custom-call | flops 3221225472 | bytes 524288000 | tf_op jit(solution)/shard_map/pallas_call | solution.py:727
  219.2 188.3 %shard_map.256 = (bf16[4,512,2048]{2,1,0:T(8,128)(2,1)}, bf16[4,256,2048]{2,1,0:T(8,128)(2,1)}, bf16[2048,512]{1,0:T(8,128)(2,1)}, bf16[2048,512]{1,0:T(8,128)(2...) custom-call(bf16[256,2048]{1,0:T(8,128)(2,1)} %get-tuple-element.44.refs_0_, ...), custom_call_target="tpu_custom_call" | custom-call | flops 77309411328 | bytes 104857600 | tf_op jit(solution)/shard_map/pallas_call | solution.py:973
  407.5 2.7 slice.25
  410.3 7.1 collective-permute-done
  417.4 4.0 add_convert_fusion
  421.5 1.5 copy-done.8
  423.3 4.0 convert_reduce_fusion
  427.3 0.7 multiply_reduce_fusion
  428.5 0.7 fusion.8
  429.3 0.9 copy-done.16
  430.2 24.2 %collective-permute-done.1 = bf16[256,2048]{1,0:T(8,128)(2,1)S(1)} collective-permute-done((bf16[256,2048]{1,0:T(8,128)(2,1)S(1)}, bf16[256,2048]{1,0:T(8,128)(2,1)S(1)}, u32[]{:S(2)}, u32[]{:S(2)}) %collective-permute-start.1) | collective-permute-done | bytes 1048608 | tf_op jit(solution)/shard_map/ppermute | solution.py:1291
  454.3 1.4 broadcast_select_fusion.3
  455.7 4.5 convolution_convert_fusion.1
  460.2 4.6 convolution_convert_fusion.2.grad_out
  464.8 0.9 copy-done
  466.2 1.9 copy-done.4
  468.1 26.5 %shard_map.257 = (bf16[512,1024]{1,0:T(8,128)(2,1)S(1)}, bf16[512,256]{1,0:T(8,128)(2,1)S(1)}, bf16[512,256]{1,0:T(8,128)(2,1)S(1)}, f32[1,128]{1,0:T(1,128)S(1)}, f32[1,128]{1,0:T(1,128)S(1)}) custom-call(s32[1]{0:T(128)} %dynamic_slice.16.refs_8_.length, f32[512,1536]{1,0:T(8,128)S(1)} %copy-done.4, f32[512,1536]{1,0:T(8,128)S(1)} %copy-done.4, ...), custom_call_target="tpu_custom_call" | custom-call | flops 13421772800 | bytes 10485760 | tf_op jit(solution)/shard_map/pallas_call | solution.py:224
  494.8 8.9 %fusion.14 = (bf16[512,2048]{1,0:T(8,128)(2,1)}, f32[512,2048]{1,0:T(8,128)}) fusion(bf16[512,1536]{1,0:T(8,128)(2,1)S(1)} %constant_dynamic-update-slice_fusion, bf16[2048,1536]{1,0:T(8,128)(2,1)} %get-tuple-element.57), kind=kOutput, calls=%fused_computation.50 | convolution fusion | flops 3222274048 | bytes 14155776 | tf_op jit(solution)/shard_map/dot_general | solution.py:259
  504.2 5.0 dynamic-slice_bitcast_fusion
  509.2 1.1 collective-permute-start.4
  510.8 0.7 reduce.6
  511.6 0.7 reduce.7
  512.4 8.5 %convolution_convert_fusion = bf16[2048,1536]{1,0:T(8,128)(2,1)} fusion(bf16[512,2048]{1,0:T(8,128)(2,1)} %fusion.2.refs_9_, bf16[512,1536]{1,0:T(8,128)(2,1)} %copy-done.20), kind=kOutput, calls=%fused_computation.2 | convolution fusion | flops 3224371200 | bytes 9961472 | tf_op jit(solution)/shard_map/dot_general | solution.py:263
  520.9 30.1 %collective-permute-done.3 = bf16[512,2048]{1,0:T(8,128)(2,1)} collective-permute-done((bf16[512,2048]{1,0:T(8,128)(2,1)}, bf16[512,2048]{1,0:T(8,128)(2,1)}, u32[]{:S(2)}, u32[]{:S(2)}) %collective-permute-start.3) | collective-permute-done | bytes 2097184 | tf_op jit(solution)/shard_map/ppermute | solution.py:1291
  551.0 3.9 fusion.3
  554.9 0.7 concatenate.15
  555.6 11.9 %collective-permute-done.4.refs_6_ = bf16[2,256,2048]{2,1,0:T(8,128)(2,1)} collective-permute-done((bf16[2,256,2048]{2,1,0:T(8,128)(2,1)}, bf16[2,256,2048]{2,1,0:T(8,128)(2,1)}, u32[]{:S(2)}, u32[]{:S(2)}) %collective-permute-start.4) | collective-permute-done | bytes 2097184 | tf_op jit(solution)/shard_map/ppermute | solution.py:1288
  567.5 117.5 %shard_map.258 = (f32[128,1024]{1,0:T(8,128)}, f32[128,256]{1,0:T(8,128)}, f32[128,256]{1,0:T(8,128)}, f32[128,4096]{1,0:T(8,128)}, f32[128,4096]{1,0:T(8,128)}, /*index=5*/f32[256,2048]{1,0:T(8,128)}, f32[33,128]{1,0:T(8,128)}) custom-call(bf16[16,128,1536]{2,1,0:T(8,128)(2,1)} %bitcast.31, bf16[4,2,256,512]{3,2,1,0:T(8,128)(2,1)} %bitcast.33, ...), custom_call_target="tpu_custom_call" | custom-call | bytes 419430400 | tf_op jit(solution)/shard_map/pallas_call | solution.py:1244
  685.0 2.3 add_convert_fusion.1
  687.3 1.7 collective-permute-start.2
  690.3 6.1 fusion.4
  696.3 1.8 convert_element_type.71
  698.1 12.8 %collective-permute-done.2 = bf16[256,2048]{1,0:T(8,128)(2,1)} collective-permute-done((bf16[256,2048]{1,0:T(8,128)(2,1)S(1)}, bf16[256,2048]{1,0:T(8,128)(2,1)}, u32[]{:S(2)}, u32[]{:S(2)}) %collective-permute-start.2) | collective-permute-done | bytes 1048608 | tf_op jit(solution)/shard_map/ppermute | solution.py:1291
  710.9 1.4 broadcast_select_fusion.1
  712.3 1.6 pad_maximum_fusion.1
  713.8 0.8 copy.41
  714.6 0.7 copy.42
  715.3 0.7 copy.43
  715.9 1.3 copy.44
  717.3 1.0 copy-done.18
  718.3 1.3 copy.45
  719.6 1.0 copy-done.17
  720.6 1.3 copy.46
  (84 shorter events, 5.4 us)
Async XLA Ops:
  7.2 5.4 copy-start.6
  7.2 4.2 copy-start.28
  7.2 4.8 copy-start.29
  7.2 5.4 copy-start.25
  7.2 677.8 %reduce-scatter.3.cloned.1.call-start = ((), (), s32[]{:S(2)}) async-start(), calls=%async_computation.2 | async-start | bytes 5242880 | tf_op jit(solution)/shard_map/reduce_scatter | solution.py:1330
  12.6 1.9 copy-start.21
  407.5 9.9 %copy-start.9 = (bf16[4,512,2048]{2,1,0:T(8,128)(2,1)S(1)}, bf16[4,512,2048]{2,1,0:T(8,128)(2,1)}, u32[]{:S(2)}) copy-start(bf16[4,512,2048]{2,1,0:T(8,128)(2,1)} %get-tuple-element.48) | copy-start | bytes 25165828
  410.2 7.2 collective-permute-start
  421.5 1.6 copy-start.8
  421.5 274.8 %reduce-scatter.5.cloned.1.call-start = ((), (), s32[]{:S(2)}) async-start(), calls=%async_computation.3 | async-start | bytes 4456448 | tf_op jit(solution)/shard_map/reduce_scatter | solution.py:1335
  423.3 4.0 copy-start.26
  427.3 1.2 copy-start.15
  429.2 1.0 copy-start.16
  429.2 25.1 %collective-permute-start.1 = (bf16[256,2048]{1,0:T(8,128)(2,1)S(1)}, bf16[256,2048]{1,0:T(8,128)(2,1)S(1)}, u32[]{:S(2)}, u32[]{:S(2)}) collective-permute-start(bf16[256,2048]{1,0:T(8,128)(2,1)S(1)} %fusion.8), channel_id=1, source_target_pairs={{0,1},{1,0},{2,3},{3,2},{4,5},{5,4},{6,7},{7,6},{8,9},{9,8},{10,11... | collective-permute-start | bytes 3145736 | tf_op jit(solution)/shard_map/ppermute | solution.py:1291
  430.2 25.6 %copy-start.30 = (bf16[512,1024]{1,0:T(8,128)(2,1)S(1)}, bf16[512,1024]{1,0:T(8,128)(2,1)}, u32[]{:S(2)}) copy-start(bf16[512,1024]{1,0:T(8,128)(2,1)} %get-tuple-element.69) | copy-start | bytes 3145732
  455.7 4.5 copy-start.10
  455.7 4.5 copy-start.12
  464.8 1.0 copy-start
  464.8 1.0 copy-start.1
  464.8 1.0 copy-start.2
  464.8 1.0 copy-start.3
  464.8 1.4 copy-start.5
  466.2 1.9 copy-start.4
  494.8 9.0 %copy-start.20 = (bf16[512,1536]{1,0:T(8,128)(2,1)}, bf16[512,1536]{1,0:T(8,128)(2,1)S(1)}, u32[]{:S(2)}) copy-start(bf16[512,1536]{1,0:T(8,128)(2,1)S(1)} %constant_dynamic-update-slice_fusion) | copy-start | bytes 4718596
  503.7 47.2 %collective-permute-start.3 = (bf16[512,2048]{1,0:T(8,128)(2,1)}, bf16[512,2048]{1,0:T(8,128)(2,1)}, u32[]{:S(2)}, u32[]{:S(2)}) collective-permute-start(bf16[512,2048]{1,0:T(8,128)(2,1)} %get-tuple-element.87), channel_id=1, source_target_pairs={{0,1},{1,0},{2,3},{3,2},{4,5},{5,4},{6,7},{7,6},{8,9},{9,8},{10,11... | collective-permute-start | bytes 6291464 | tf_op jit(solution)/shard_map/ppermute | solution.py:1291
  509.2 58.2 %collective-permute-start.4 = (bf16[2,256,2048]{2,1,0:T(8,128)(2,1)}, bf16[2,256,2048]{2,1,0:T(8,128)(2,1)}, u32[]{:S(2)}, u32[]{:S(2)}) collective-permute-start(bf16[2,256,2048]{2,1,0:T(8,128)(2,1)} %get-tuple-element.77), channel_id=1, source_target_pairs={{0,4},{2,6},{4,0},{6,2},{8,12},{10,14},{12,8},{14,10},{16,20},{18,... | collective-permute-start | bytes 6291464 | tf_op jit(solution)/shard_map/ppermute | solution.py:1288
  512.4 38.6 %copy-start.7 = (bf16[512,2048]{1,0:T(8,128)(2,1)S(1)}, bf16[512,2048]{1,0:T(8,128)(2,1)}, u32[]{:S(2)}) copy-start(bf16[512,2048]{1,0:T(8,128)(2,1)} %param.16) | copy-start | bytes 6291460
  512.4 38.6 %copy-start.14 = (f32[512,2048]{1,0:T(8,128)S(1)}, f32[512,2048]{1,0:T(8,128)}, u32[]{:S(2)}) copy-start(f32[512,2048]{1,0:T(8,128)} %get-tuple-element.88) | copy-start | bytes 12582916
  685.0 4.1 copy-start.27
  685.0 5.2 copy-start.11
  685.0 5.2 copy-start.13
  687.3 23.5 %collective-permute-start.2 = (bf16[256,2048]{1,0:T(8,128)(2,1)S(1)}, bf16[256,2048]{1,0:T(8,128)(2,1)}, u32[]{:S(2)}, u32[]{:S(2)}) collective-permute-start(bf16[256,2048]{1,0:T(8,128)(2,1)S(1)} %add_convert_fusion.1), channel_id=1, source_target_pairs={{0,1},{1,0},{2,3},{3,2},{4,5},{5,4},{6,7},{7,6},{8,9},{9,8},{10,11... | collective-permute-start | bytes 3145736 | tf_op jit(solution)/shard_map/ppermute | solution.py:1291
  712.2 1.6 copy-start.22
  712.2 2.4 copy-start.24
  712.2 3.0 copy-start.23
  712.2 3.7 copy-start.19
  715.9 2.3 copy-start.18
  718.3 2.3 copy-start.17
Sparse Core Ops, SparseCore 0:
  421.6 74.0 reduce-scatter.2
  500.0 85.7 reduce-scatter.4

commit v4 on v3

--- a/solution.py
+++ b/solution.py
@@ -124,11 +124,9 @@
 
 
 def attend_back_kernel(
-    block, scale, length, q, k, v, cosine, sine, q_gain, k_gain, totals, grad_out,
+    block, scale, second, length, q, k, v, cosine, sine, q_gain, k_gain, totals, grad_out,
     grad_q, grad_k, grad_v, q_gain_grad, k_gain_grad, keys_sum, vals_sum,
 ):
-    step = pl.program_id(0)
-    second = step % 2 == 1
     rows = q.shape[0]
     cos, sin = cosine[...], sine[...]
     k_normed, k_scale = head_norm(k[...])
@@ -137,11 +135,6 @@
     lane = lax.broadcasted_iota(jnp.int32, (block, LANES), 1)
     keys_sum[...] = jnp.zeros_like(keys_sum)
     vals_sum[...] = jnp.zeros_like(vals_sum)
-
-    @pl.when(step == 0)
-    def _():
-        q_gain_grad[...] = jnp.zeros_like(q_gain_grad)
-        k_gain_grad[...] = jnp.zeros_like(k_gain_grad)
 
     for first in range(0, rows, block):
         span = pl.ds(first, block)
@@ -190,65 +183,15 @@
     k_gain_grad[...] += gain_part * 0.5
     keep_low = low_lanes(grad_k.shape)
 
-    @pl.when(step % 2 == 0)
+    @pl.when(jnp.logical_not(second))
     def _():
         grad_k[...] = grad_proj.astype(BF)
         grad_v[...] = vals_grad.astype(BF)
 
-    @pl.when(step % 2 == 1)
+    @pl.when(second)
     def _():
         grad_k[...] = jnp.where(keep_low, grad_k[...].astype(F32), grad_proj).astype(BF)
         grad_v[...] = jnp.where(keep_low, grad_v[...].astype(F32), vals_grad).astype(BF)
-
-
-def attention_specs(rows, group, k_heads, q_cols):
-    wide = group * HEAD
-    k_first = q_cols // LANES
-    v_first = k_first + k_heads * HEAD // LANES
-    return [
-        pl.BlockSpec(memory_space=pltpu.SMEM),
-        pl.BlockSpec((rows, wide), lambda g: (0, g)),
-        pl.BlockSpec((rows, LANES), lambda g: (0, k_first + g // 2)),
-        pl.BlockSpec((rows, LANES), lambda g: (0, v_first + g // 2)),
-        pl.BlockSpec((rows, LANES), lambda g: (0, 0)),
-        pl.BlockSpec((rows, LANES), lambda g: (0, 0)),
-        pl.BlockSpec((1, LANES), lambda g: (0, 0)),
-        pl.BlockSpec((1, LANES), lambda g: (0, 0)),
-    ]
-
-
-def attend_back(length, qkv, tables, gains, totals, grad_out, q_cols, k_heads):
-    rows = qkv.shape[0]
-    group = q_cols // HEAD // k_heads
-    block = rows // 2
-    return pl.pallas_call(
-        functools.partial(attend_back_kernel, block, 1.0 / math.sqrt(HEAD)),
-        grid=(k_heads,),
-        in_specs=attention_specs(rows, group, k_heads, q_cols)
-        + [
-            pl.BlockSpec((rows, LANES), lambda g: (0, g)),
-            pl.BlockSpec((rows, group * HEAD), lambda g: (0, g)),
-        ],
-        out_specs=[
-            pl.BlockSpec((rows, group * HEAD), lambda g: (0, g)),
-            pl.BlockSpec((rows, LANES), lambda g: (0, g // 2)),
-            pl.BlockSpec((rows, LANES), lambda g: (0, g // 2)),
-            pl.BlockSpec((1, LANES), lambda g: (0, 0)),
-            pl.BlockSpec((1, LANES), lambda g: (0, 0)),
-        ],
-        out_shape=[
-            jax.ShapeDtypeStruct((rows, q_cols), BF),
-            jax.ShapeDtypeStruct((rows, k_heads * HEAD), BF),
-            jax.ShapeDtypeStruct((rows, k_heads * HEAD), BF),
-            jax.ShapeDtypeStruct((1, LANES), F32),
-            jax.ShapeDtypeStruct((1, LANES), F32),
-        ],
-        scratch_shapes=[pltpu.VMEM((rows, LANES), F32), pltpu.VMEM((rows, LANES), F32)],
-        compiler_params=pltpu.CompilerParams(vmem_limit_bytes=40 << 20),
-        cost_estimate=pl.CostEstimate(
-            flops=50 * rows * rows * q_cols, bytes_accessed=10 << 20, transcendentals=rows * rows
-        ),
-    )(length, qkv, qkv, qkv, *tables, *gains, totals, grad_out)
 
 
 def mm(left, right):
@@ -385,15 +328,15 @@
 
 def start_kernel(side, piece, sliced, scale, *refs):
     w_query, w_key, w_value, w_out, w_gate, w_up, w_down, dm_own = refs[:8]
-    length, hidden, token_half, cosine, sine, q_gain, k_gain, ffn_gain = refs[8:16]
+    length, tokens, attn_gain, cosine, sine, q_gain, k_gain, ffn_gain = refs[8:16]
     outs = refs[16:21]
-    proj, attended, totals, h_one, hidden_two = refs[21:26]
-    qkv, out, units, down, dm = bufs = refs[26:31]
-    part, cross_sent, cross_got = refs[31:34]
+    proj, attended, totals, h_one, hidden_two, hidden = refs[21:27]
+    qkv, out, units, down, dm = bufs = refs[27:32]
+    part, cross_sent, cross_got = refs[32:35]
     (
         load_sems, send_sems, qkv_sems, out_sems, unit_sems, pair_sems, down_sems,
         line_sems, core_sems, cross_sem, store_sems,
-    ) = refs[34:]
+    ) = refs[35:]
     t, j, c, x = coordinates()
     bits = side.bit_length() - 1
     strip = side * piece
@@ -414,7 +357,8 @@
     mine = block(t, j, c)
     depth, q_cols = w_query.shape
     k_cols = w_key.shape[1]
-    half, width = dm_own.shape
+    rows, width = tokens.shape
+    half = rows // 2
 
     def rows_of(buf, idx):
         count = depth if buf is qkv else w_out.shape[0]
@@ -427,7 +371,7 @@
         (w_value, qkv.at[own_qkv, pl.ds(q_cols + k_cols, k_cols)]),
         (w_out, rows_of(out, mine)),
         (w_down, down.at[x * side + j]),
-        (dm_own, dm.at[t, pl.ds(0, half)]),
+        (dm_own.at[pl.ds(pl.multiple_of(x * half, half), half)], dm.at[t, pl.ds(0, half)]),
     ]
     first_unit = len(loads)
 
@@ -494,49 +438,75 @@
         else:
             pass_on(ref, sem, False, both(cond, t > 0))
 
-    for buf, sems in lines:
+    def set_out(buf, sems):
         pass_on(rows_of(buf, mine), sems.at[mine], t < LINE - 1, t > 0)
         spread(buf, sems, t, 0, None)
+
+    def line_step(buf, sems, k):
+        for cond, tt, rightward in line_places(k):
+            idx = block(tt, j, c)
+            when(cond, lambda idx=idx: arrived(rows_of(buf, idx), sems.at[idx], here))
+            if k < LINE - 1:
+                forward(rows_of(buf, idx), sems.at[idx], cond, rightward)
+            spread(buf, sems, tt, 0, cond)
+        if k == 1:
+            spread_rest(buf, sems, t, None)
+        else:
+            spread_rest(buf, sems, t - k + 1, t >= k - 1)
+            spread_rest(buf, sems, t + k - 1, t + k - 1 < LINE)
+
     own_down = x * side + j
+
+    def down_set_out():
+        for bit in range(bits):
+            sends.start(
+                down.at[own_down], down.at[own_down], down_sems.at[own_down], beside[bit]
+            )
+
+    def down_rest():
+        for r in range(1, side):
+            idx = x * side + (j ^ r)
+            arrived(down.at[idx], down_sems.at[idx], here)
+            for bit in range(bits):
+                if (1 << bit) > r:
+                    sends.start(down.at[idx], down.at[idx], down_sems.at[idx], beside[bit])
+            sends.start(down.at[idx], down.at[idx], down_sems.at[idx], across)
+
+    def units_set_out():
+        for dt in range(LINE):
+            for dc in range(2):
+                if dt or dc:
+                    tt, cc = (t + dt) % LINE, c ^ dc
+                    for w in range(2):
+                        for jj in parts:
+                            sends.start(
+                                unit_block(w, tt, jj, cc),
+                                unit_target(w, t, jj, c),
+                                unit_sems.at[w, t * 2 + c, jj],
+                                at(tt, j, cc),
+                            )
+
+    set_out(*lines[0])
     sends.start(down.at[own_down], down.at[own_down], down_sems.at[own_down], across)
-    for bit in range(bits):
-        sends.start(down.at[own_down], down.at[own_down], down_sems.at[own_down], beside[bit])
-    for k in range(1, LINE):
-        for buf, sems in lines:
-            for cond, tt, rightward in line_places(k):
-                idx = block(tt, j, c)
-                when(cond, lambda idx=idx: arrived(rows_of(buf, idx), sems.at[idx], here))
-                if k < LINE - 1:
-                    forward(rows_of(buf, idx), sems.at[idx], cond, rightward)
-                spread(buf, sems, tt, 0, cond)
-            if k == 1:
-                spread_rest(buf, sems, t, None)
-            else:
-                spread_rest(buf, sems, t - k + 1, t >= k - 1)
-                spread_rest(buf, sems, t + k - 1, t + k - 1 < LINE)
-        if k == 1:
-            for r in range(1, side):
-                idx = x * side + (j ^ r)
-                arrived(down.at[idx], down_sems.at[idx], here)
-                for bit in range(bits):
-                    if (1 << bit) > r:
-                        sends.start(
-                            down.at[idx], down.at[idx], down_sems.at[idx], beside[bit]
-                        )
-                sends.start(down.at[idx], down.at[idx], down_sems.at[idx], across)
-        if k == LINE - 2:
-            for dt in range(LINE):
-                for dc in range(2):
-                    if dt or dc:
-                        tt, cc = (t + dt) % LINE, c ^ dc
-                        for w in range(2):
-                            for jj in parts:
-                                sends.start(
-                                    unit_block(w, tt, jj, cc),
-                                    unit_target(w, t, jj, c),
-                                    unit_sems.at[w, t * 2 + c, jj],
-                                    at(tt, j, cc),
-                                )
+    chunk = rows // 16
+
+    @pl.loop(0, 16)
+    def _(i):
+        span = pl.ds(pl.multiple_of(i * chunk, chunk), chunk)
+        hidden[span, :] = rms_scale(tokens[span, :].astype(F32), attn_gain[...]).astype(BF)
+
+    @pl.loop(0, 8)
+    def _(i):
+        span = pl.ds(pl.multiple_of(i * chunk, chunk), chunk)
+        row = lax.broadcasted_iota(jnp.int32, (chunk, width), 0) + i * chunk + x * half
+        kept = dm[t, span, :].astype(F32)
+        dm[t, span, :] = jnp.where(row < length[0], kept, 0.0).astype(BF)
+
+    line_step(*lines[0], 1)
+    line_step(*lines[0], 2)
+    units_set_out()
+    set_out(*lines[1])
+    line_step(*lines[0], 3)
     stores = []
 
     def store(source, target):
@@ -613,6 +583,7 @@
 
     finish_line(*lines[0])
     store(qkv, outs[0])
+    down_set_out()
     for load in loads[first_unit:]:
         load.wait()
     unit_first(t)
@@ -626,11 +597,10 @@
         cols = pl.ds(pl.multiple_of(i * tile, tile), tile)
         proj[:, cols] = mm(hidden[...], qkv[:, cols])
 
-    rows = hidden.shape[0]
     group = q_cols // k_cols * HEAD
-
-    @pl.loop(0, k_cols // HEAD)
-    def _(g):
+    key_heads = k_cols // HEAD
+
+    def attend_head(g):
         pair = pl.multiple_of(g // 2 * LANES, LANES)
         wide = pl.ds(pl.multiple_of(g * group, group), group)
         attend_kernel(
@@ -643,6 +613,13 @@
             totals.at[:, pl.ds(pl.multiple_of(g * LANES, LANES), LANES)],
         )
 
+    pl.loop(0, key_heads)(attend_head)
+    for k in range(1, LINE):
+        unit_first(slot_place(t, k))
+    down_rest()
+    for k in range(1, LINE):
+        line_step(*lines[1], k)
+
     finish_line(*lines[1])
     store(out, outs[1])
     wide = 512
@@ -661,10 +638,11 @@
         cols = pl.ds(pl.multiple_of(i * wide, wide), wide)
         part[:, cols] = mm(attended[own_rows, :], out[:, cols])
 
+    unit_second(t)
+    dm_step(1)
     for k in range(1, LINE):
-        unit_first(slot_place(t, k))
-    dm_step(1)
-    unit_second(t)
+        unit_second(slot_place(t, k))
+    dm_step(2)
 
     arrived(cross_got, cross_sem, here)
     step = half // 8
@@ -672,14 +650,11 @@
     @pl.loop(0, 8)
     def _(i):
         span = pl.ds(pl.multiple_of(i * step, step), step)
-        total = token_half[span, :].astype(F32) + part[span, :] + cross_got[span, :].astype(F32)
+        rows_here = pl.ds(pl.multiple_of(x * half + i * step, step), step)
+        total = tokens[rows_here, :].astype(F32) + part[span, :] + cross_got[span, :].astype(F32)
         h_one[span, :] = total
         hidden_two[span, :] = rms_scale(total, ffn_gain[...]).astype(BF)
 
-    unit_second(slot_place(t, 1))
-    dm_step(2)
-    unit_second(slot_place(t, 2))
-    unit_second(slot_place(t, 3))
     dm_step(3)
     for k in range(LINE):
         unit_last(slot_place(t, k))
@@ -696,11 +671,11 @@
         copy.wait()
 
 
-def start_layer(n, weights, dm_own, length, hidden, token_half, tables, gains, ffn_gain):
+def start_layer(n, weights, cotangent, length, tokens, attn_gain, tables, gains, ffn_gain):
     w_query, w_key, w_value, w_out, w_gate, w_up, w_down = weights
     side = n // LINE // 2
     depth, piece, width = w_gate.shape[0], w_down.shape[0], w_down.shape[1]
-    rows, half = hidden.shape[0], dm_own.shape[0]
+    rows, half = tokens.shape[0], tokens.shape[0] // 2
     q_cols, k_cols = w_query.shape[1], w_key.shape[1]
     cols = q_cols + 2 * k_cols
     strip = side * piece
@@ -733,9 +708,10 @@
             jax.ShapeDtypeStruct((rows, k_cols // HEAD * LANES), F32),
             jax.ShapeDtypeStruct((half, width), F32),
             jax.ShapeDtypeStruct((half, width), BF),
+            jax.ShapeDtypeStruct((rows, width), BF),
         ],
         in_specs=[any_space] * 8 + [pl.BlockSpec(memory_space=pltpu.SMEM)] + [vmem] * 7,
-        out_specs=[any_space] * 5 + [vmem] * 5,
+        out_specs=[any_space] * 5 + [vmem] * 6,
         scratch_shapes=[pltpu.VMEM(shape, BF) for shape in shapes]
         + [
             pltpu.VMEM((half, width), F32),
@@ -760,17 +736,18 @@
             flops=2 * rows * width * cols, bytes_accessed=500 << 20, transcendentals=rows * rows
         ),
     )(
-        w_query, w_key, w_value, w_out, w_gate, w_up, w_down, dm_own, length, hidden,
-        token_half, *tables, *gains, ffn_gain[None, :],
+        w_query, w_key, w_value, w_out, w_gate, w_up, w_down, cotangent, length, tokens,
+        attn_gain[None, :], *tables, *gains, ffn_gain[None, :],
     )
 
 
 def feed_kernel(side, *refs):
-    h_own, dm_all, units, down = refs[:4]
-    e_out, f_out, gate_kept, gate_got, up_kept, up_got, g_down = refs[4:11]
-    wg, wu, wd, h_all, dm, act, dg, du, e_stage, f_stage, f_send, f_core = refs[11:23]
-    load_sems, store_sems, send_sems, line_sems, core_sems, back_sems = refs[23:29]
-    done_sems, gate_sems, up_sems = refs[29:]
+    h_own, dm_all, units, down, h_one, gain = refs[:6]
+    out_half, dab, gain_part, e_own, e_core, e_line, f_out = refs[6:13]
+    g_down, gate_mid, up_mid, gate_kept, gate_got, up_kept, up_got = refs[13:20]
+    wg, wu, wd, h_all, dm, act, dg, du, e_stage, f_stage, f_send, f_core = refs[20:32]
+    load_sems, store_sems, send_sems, line_sems, core_sems, back_sems = refs[32:38]
+    done_sems, gate_sems, up_sems, mid_sems, last_sems, e_sems, step_sems, dab_sem, row_sems = refs[38:]
     t, j, c, x = coordinates()
     half, width = h_own.shape
     unit_count = wd.shape[0]
@@ -793,32 +770,50 @@
     for load in loads:
         load.start()
     greet(others + [core, across] + ([beside] if bits else []))
-    sends = Sends(send_sems)
+    sends, rows_sent = Sends(send_sems), Sends(row_sems)
 
     def own_rows(tt):
         return h_all.at[tt, pl.ds(0, half)]
 
     def to_core(tt, cond):
-        sends.start(
+        rows_sent.start(
             own_rows(tt), h_all.at[tt, pl.ds(half, half)], core_sems.at[tt], core, cond
         )
 
     loads[0].wait()
-    sends.start(own_rows(t), own_rows(t), line_sems.at[t], at(t + 1, c), t < LINE - 1)
-    sends.start(own_rows(t), own_rows(t), line_sems.at[t], at(t - 1, c), t > 0)
+    rows_sent.start(own_rows(t), own_rows(t), line_sems.at[t], at(t + 1, c), t < LINE - 1)
+    rows_sent.start(own_rows(t), own_rows(t), line_sems.at[t], at(t - 1, c), t > 0)
     to_core(t, None)
     for load in loads[1:]:
         load.wait()
 
     tile = min(512, unit_count)
     wide = min(1024, width)
-    e_stores, f_sent, stores = [], [], []
+    e_waits, f_sent, stores = [], [], []
 
     def store(source, target):
         copy = pltpu.make_async_copy(source, target, store_sems.at[len(stores)])
         copy.start()
         stores.append(copy)
         return copy
+
+    def f_go(k):
+        sends.start(
+            f_stage.at[k], f_out.at[t], done_sems.at[t], at(slot_place(t, k), c)
+        )
+
+    def kept_out(k):
+        copy = pltpu.make_async_copy(
+            e_stage.at[pl.ds(0, half)], e_own.at[k], mid_sems.at[2, 2 * LINE - 1]
+        )
+        copy.start()
+        return copy.wait
+
+    def later(source, target, sem, device):
+        sends.start(source, target, sem, device)
+        copy = sends.made.pop()[1]
+        sends.made.append((None, None))
+        return lambda: copy().wait_send()
 
     for k in range(LINE):
         tt = slot_place(t, k)
@@ -832,11 +827,13 @@
                     lambda p=place_of: arrived(own_rows(p), line_sems.at[p], here),
                 )
                 if k < LINE - 1:
-                    sends.start(
+                    rows_sent.start(
                         own_rows(place_of), own_rows(place_of), line_sems.at[place_of],
                         at(target, c), jnp.logical_and(cond, forward),
                     )
                 to_core(place_of, cond)
+        if k >= 2:
+            f_go(k - 1)
         arrived(h_all.at[tt, pl.ds(half, half)], core_sems.at[tt], here)
         if k >= 2:
             f_sent[k - 2]()
@@ -863,18 +860,19 @@
             f_stage[k, :, span] = grad[:half].astype(BF)
             f_send[slot, :, span] = grad[half:].astype(BF)
 
-        sends.start(f_send.at[slot], f_core.at[k], back_sems.at[k], core)
-        f_sent.append(lambda copy=sends.made.pop()[1]: copy().wait_send())
-        sends.made.append((None, None))
-        if k:
-            e_stores[k - 1].wait()
+        f_sent.append(later(f_send.at[slot], f_core.at[k], back_sems.at[k], core))
+        for wait in e_waits:
+            wait()
 
         @pl.loop(0, width // wide)
         def _(i):
             span = pl.ds(pl.multiple_of(i * wide, wide), wide)
             e_stage[:, span] = mm(act[tt], wd[:, span]).astype(BF)
 
-        e_stores.append(store(e_stage, e_out.at[tt]))
+        e_waits = [
+            kept_out(k),
+            later(e_stage.at[pl.ds(half, half)], e_core.at[k], e_sems.at[k], core),
+        ]
         arrived(f_core.at[k], back_sems.at[k], here)
 
         @pl.loop(0, 4)
@@ -884,10 +882,8 @@
                 f_stage[k, part, :].astype(F32) + f_core[k, part, :].astype(F32)
             ).astype(BF)
 
-        if k == 0:
-            store(f_stage.at[0], f_out.at[t])
-        else:
-            sends.start(f_stage.at[k], f_out.at[t], done_sems.at[t], at(tt, c))
+        if k == LINE - 1:
+            f_go(k)
 
     group = width // LINE
     far = pl.ds(pl.multiple_of((1 - x) * strip, strip), strip)
@@ -903,19 +899,24 @@
         send(tt)
 
     block = group // side
+    whole = side == 2
+
+    def side_rows(tt, jj):
+        return pl.ds(pl.multiple_of(tt * group + jj * block, block), block)
 
     def send_gate(tt):
         span = pl.ds(tt * group, group)
-        sends.start(wg.at[span, far], gate_got.at[span], gate_sems.at[tt], across)
-        store(wg.at[span, near], gate_kept.at[span])
+        sends.start(wg.at[span, far], gate_mid.at[span], gate_sems.at[tt], across)
+        if not whole:
+            store(wg.at[span, near], gate_kept.at[span])
 
     def send_up(tt):
         for r in range(side):
-            span = pl.ds(pl.multiple_of(tt * group + (j ^ r) * block, block), block)
+            span = side_rows(tt, j ^ r)
             if r >= side // 2:
                 k = r - side // 2
-                sends.start(wu.at[span], up_got.at[k, tt], up_sems.at[k, tt], beside)
-            else:
+                sends.start(wu.at[span], up_mid.at[k, tt], up_sems.at[k, tt], beside)
+            elif not whole:
                 store(wu.at[span], up_kept.at[r, tt])
 
     for tt in range(LINE):
@@ -930,23 +931,148 @@
         wd[cols, :] = mm_tn(units_part, dm[...].reshape(LINE * rows, width)).astype(BF)
 
     store(wd, g_down)
+
+    def fetch(pairs):
+        copies = [
+            pltpu.make_async_copy(a, b, mid_sems.at[2, i]) for i, (a, b) in enumerate(pairs)
+        ]
+        for copy in copies:
+            copy.start()
+        for copy in copies:
+            copy.wait()
+
+    def add(target, other):
+        count = target.shape[0]
+        step = min(64, count)
+
+        @pl.loop(0, count // step)
+        def _(i):
+            part = pl.ds(pl.multiple_of(i * step, step), step)
+            target[part, :] = (target[part, :].astype(F32) + other[part, :].astype(F32)).astype(BF)
+
+    upper, lower = pl.ds(0, half), pl.ds(half, half)
+    for wait in e_waits:
+        wait()
+    rows_sent.wait_sent()
+    for k in range(LINE):
+        arrived(e_core.at[k], e_sems.at[k], here)
+    fetch(
+        [(e_own.at[k], h_all.at[k, upper]) for k in range(LINE)]
+        + [(e_core.at[k], h_all.at[k, lower]) for k in range(LINE)]
+    )
+    for k in reversed(range(LINE)):
+        add(h_all.at[k, upper], h_all.at[k, lower])
+
+    def line_came(i, way, cond, k):
+        def act_on():
+            arrived(e_line.at[way, i], step_sems.at[way, i], here)
+            fetch([(e_line.at[way, i], h_all.at[way, lower])])
+            add(h_all.at[k, upper], h_all.at[way, lower])
+
+        when(cond, act_on)
+
+    def line_go(i, way, cond, k):
+        sends.start(
+            h_all.at[k, upper], e_line.at[way, i], step_sems.at[way, i], at(t + 1 - 2 * way, c),
+            cond,
+        )
+
+    inner = jnp.logical_and(t >= 1, t <= 2)
+    line_go(0, 0, t == 0, 3)
+    line_go(0, 1, t == 3, 3)
+
+    for dt in range(1, LINE):
+        p = (t + dt) % LINE
+        arrived(f_out.at[p], done_sems.at[p], here)
+    fetch([(f_out.at[(t + dt) % LINE], f_core.at[dt]) for dt in range(1, LINE)])
+    gain_part[...] = jnp.zeros_like(gain_part)
+    step = half // 16
+
+    @pl.loop(0, 16)
+    def _(i):
+        part = pl.ds(pl.multiple_of(i * step, step), step)
+        grad = f_stage[0, part, :].astype(F32)
+        for dt in range(1, LINE):
+            grad = grad + f_core[dt, part, :].astype(F32)
+        values = h_one[part, :]
+        scale = lax.rsqrt(jnp.mean(values * values, axis=1, keepdims=True) + EPS)
+        gain_part[...] += jnp.sum(grad * values * scale, axis=0, keepdims=True)
+        grad = grad * gain[...]
+        back = jnp.mean(grad * values, axis=1, keepdims=True) * scale * scale
+        grad = dm[t, part, :].astype(F32) + scale * (grad - values * back)
+        e_stage[part, :] = grad.astype(BF)
+
+    own_rows_out = dab.at[pl.ds(pl.multiple_of(x * half, half), half)]
+    store(e_stage.at[upper], own_rows_out)
+    sends.start(e_stage.at[upper], own_rows_out, dab_sem, across)
+    line_came(0, 0, t == 1, 2)
+    line_came(0, 1, t == 2, 2)
+    line_go(1, 0, t <= 1, 2)
+    line_go(1, 1, t >= 2, 2)
+    if whole:
+        copies = []
+        for tt in range(LINE):
+            span = pl.ds(tt * group, group)
+            arrived(gate_mid.at[span], gate_sems.at[tt], here)
+            arrived(up_mid.at[0, tt], up_sems.at[0, tt], here)
+            for i, (source, target) in enumerate(
+                (
+                    (gate_mid.at[span], dg.at[tt, :, pl.ds(0, strip)]),
+                    (up_mid.at[0, tt], du.at[tt, pl.ds(0, block)]),
+                )
+            ):
+                copies.append(pltpu.make_async_copy(source, target, mid_sems.at[i, tt]))
+                copies[-1].start()
+        for tt in range(LINE):
+            mine = side_rows(tt, j)
+            copies[2 * tt].wait()
+            for jj in range(side):
+                span = pl.ds(tt * group + jj * block, block)
+                wg[span, near] = (
+                    wg[span, near].astype(F32)
+                    + dg[tt, pl.ds(jj * block, block), pl.ds(0, strip)].astype(F32)
+                ).astype(BF)
+            sends.start(
+                wg.at[side_rows(tt, 1 - j), near], gate_got.at[tt], last_sems.at[0, tt], beside
+            )
+            store(wg.at[mine, near], gate_kept.at[tt])
+            copies[2 * tt + 1].wait()
+            wu[mine, :] = (
+                wu[mine, :].astype(F32) + du[tt, pl.ds(0, block), :].astype(F32)
+            ).astype(BF)
+            sends.start(wu.at[mine, far], up_got.at[tt], last_sems.at[1, tt], across)
+            store(wu.at[mine, near], up_kept.at[tt])
+    line_came(1, 0, inner, 3)
+    line_came(1, 1, inner, 1)
+    line_go(2, 0, t == 0, 1)
+    line_go(2, 0, inner, 3)
+    line_go(2, 1, t >= 1, 1)
     for sent in f_sent[LINE - 2 :]:
         sent()
     sends.made = [item for item in sends.made if item[1] is not None]
+    for tt in range(LINE):
+        if whole:
+            arrived(gate_got.at[tt], last_sems.at[0, tt], here)
+            arrived(up_got.at[tt], last_sems.at[1, tt], here)
+        else:
+            arrived(gate_mid.at[pl.ds(tt * group, group)], gate_sems.at[tt], here)
+            for k in range(side // 2):
+                arrived(up_mid.at[k, tt], up_sems.at[k, tt], here)
+    arrived(dab.at[pl.ds(pl.multiple_of((1 - x) * half, half), half)], dab_sem, here)
+    line_came(2, 0, t >= 1, 0)
+    line_came(2, 1, t <= 2, 0)
+
+    @pl.loop(0, 16)
+    def _(i):
+        part = pl.ds(pl.multiple_of(i * step, step), step)
+        out_half[part, :] = (h_one[part, :] + h_all[0, part, :].astype(F32)).astype(BF)
+
     sends.wait_sent()
     for copy in stores:
-        if all(copy is not early for early in e_stores[:-1]):
-            copy.wait()
-    for dt in range(1, LINE):
-        p = (t + dt) % LINE
-        arrived(f_out.at[p], done_sems.at[p], here)
-    for tt in range(LINE):
-        arrived(gate_got.at[pl.ds(tt * group, group)], gate_sems.at[tt], here)
-        for k in range(side // 2):
-            arrived(up_got.at[k, tt], up_sems.at[k, tt], here)
-
-
-def feed_forward(side, h_own, dm_all, units, down):
+        copy.wait()
+
+
+def feed_forward(side, h_own, dm_all, units, down, h_one, ffn_gain):
     half, width = h_own.shape
     unit_count = down.shape[0]
     strip = unit_count // 2
@@ -954,31 +1080,33 @@
     group = width // LINE
     block = group // side
     any_space = pl.BlockSpec(memory_space=pl.ANY)
-    outs = [
-        (LINE, rows, width),
-        (LINE, half, width),
-        (width, strip),
-        (width, strip),
-        (side // 2, LINE, block, unit_count),
-        (side // 2, LINE, block, unit_count),
-        (unit_count, width),
-    ]
+    vmem = pl.BlockSpec(memory_space=pltpu.VMEM)
+    mids = [(width, strip), (side // 2, LINE, block, unit_count)]
+    last = (LINE, block, strip)
+    blocks = (LINE, half, width)
+    outs = [blocks, blocks, (2, 3, half, width), blocks, (unit_count, width)] + mids
+    outs += [last] * 4 if side == 2 else [mids[0], (1, LANES), mids[1], (1, LANES)]
     held = [
         (width, unit_count), (width, unit_count), (unit_count, width),
         (LINE, rows, width), (LINE, rows, width),
         (LINE, rows, unit_count), (LINE, rows, unit_count), (LINE, rows, unit_count),
         (rows, width), (LINE, half, width), (2, half, width), (LINE, half, width),
     ]
-    sends = 3 + 4 * (LINE - 1) + 2 * LINE + LINE + side // 2 * LINE
+    sends = 3 + 4 * (LINE - 1) + 3 * LINE + 3 * LINE + side // 2 * LINE + 8
     return pl.pallas_call(
         functools.partial(feed_kernel, side),
-        out_shape=[jax.ShapeDtypeStruct(shape, BF) for shape in outs],
-        in_specs=[any_space] * 4,
-        out_specs=[any_space] * 7,
+        out_shape=[
+            jax.ShapeDtypeStruct((half, width), BF),
+            jax.ShapeDtypeStruct((rows, width), BF),
+            jax.ShapeDtypeStruct((1, width), F32),
+        ]
+        + [jax.ShapeDtypeStruct(shape, BF) for shape in outs],
+        in_specs=[any_space] * 4 + [vmem] * 2,
+        out_specs=[vmem, any_space, vmem] + [any_space] * len(outs),
         scratch_shapes=[pltpu.VMEM(shape, BF) for shape in held]
         + [
             pltpu.SemaphoreType.DMA((5,)),
-            pltpu.SemaphoreType.DMA((2 * LINE + 2 + side // 2 * LINE,)),
+            pltpu.SemaphoreType.DMA((3 * LINE + 2 + side // 2 * LINE,)),
             pltpu.SemaphoreType.DMA((sends,)),
             pltpu.SemaphoreType.DMA((LINE,)),
             pltpu.SemaphoreType.DMA((LINE,)),
@@ -986,6 +1114,12 @@
             pltpu.SemaphoreType.DMA((LINE,)),
             pltpu.SemaphoreType.DMA((LINE,)),
             pltpu.SemaphoreType.DMA((side // 2, LINE)),
+            pltpu.SemaphoreType.DMA((3, 2 * LINE)),
+            pltpu.SemaphoreType.DMA((2, LINE)),
+            pltpu.SemaphoreType.DMA((LINE,)),
+            pltpu.SemaphoreType.DMA((2, 3)),
+            pltpu.SemaphoreType.DMA,
+            pltpu.SemaphoreType.DMA((3 + 4 * (LINE - 1),)),
         ],
         compiler_params=pltpu.CompilerParams(
             collective_id=1, has_side_effects=True, vmem_limit_bytes=63 << 20
@@ -994,19 +1128,20 @@
             flops=18 * LINE * rows * width * unit_count, bytes_accessed=100 << 20,
             transcendentals=LINE * rows * unit_count,
         ),
-    )(h_own, dm_all, units, down)
-
-
-def sum_kernel(side, piece, *refs):
-    g_qkv, gate, gate_got, up, up_got, down, down_got, small = refs[:8]
-    q_out, k_out, v_out, gate_out, up_out, down_out, small_out = refs[8:15]
+    )(h_own, dm_all, units, down, h_one, ffn_gain[None, :])
+
+
+def end_kernel(side, piece, scale, *refs):
+    gate, gate_got, up, up_got, down, down_got, w_qkv, length = refs[:8]
+    hidden, proj, totals, grad_o, cosine, sine, q_gain, k_gain, attn_gain, ffn_part = refs[8:18]
+    q_out, k_out, v_out, gate_out, up_out, down_out, small_out, low_out, low_got_out = refs[18:27]
     (
         heads, heads_core, heads_side, line_right, line_left,
-        gates, gates_got, gates_side, ups, ups_got, ups_across,
-        downs, downs_got, downs_across, homes, smalls,
-    ) = refs[15:31]
-    load_sems, send_sems, core_sems, side_sems, line_sems, gate_sems, across_sems = refs[31:38]
-    home_sems, small_sems = refs[38:]
+        gates, gates_got, ups, ups_got, downs, downs_got, downs_across, homes,
+        grads, weights, low, low_got, wide_out, keys_sum, vals_sum, q_sum, k_sum, smalls,
+    ) = refs[27:50]
+    load_sems, send_sems, core_sems, side_sems, line_sems, across_sems = refs[50:56]
+    home_sems, small_sems, store_sems = refs[56:]
     t, j, c, x = coordinates()
     bits = side.bit_length() - 1
     depth, q_cols = q_out.shape
@@ -1024,17 +1159,13 @@
     others = [
         at((t + dt) % LINE, j, c ^ dc) for dt in range(LINE) for dc in range(2) if dt or dc
     ]
-    near_col = pl.multiple_of(x * strip, strip)
     loads = [
-        (g_qkv, heads),
-        (gate, gates),
-        (gate_got, gates_got),
-        (up, ups),
-        (up_got, ups_got),
-        (down, downs),
-        (down_got, downs_got),
-        (small, smalls.at[0]),
+        (gate, gates), (gate_got, gates_got), (up, ups), (up_got, ups_got),
+        (down.at[:, j], downs) if side == 2 else (down, downs),
+        (w_qkv, weights),
     ]
+    if side != 2:
+        loads.append((down_got, downs_got))
     loads = [pltpu.make_async_copy(a, b, load_sems.at[i]) for i, (a, b) in enumerate(loads)]
     for load in loads:
         load.start()
@@ -1052,49 +1183,99 @@
                 target.dtype
             )
 
-    loads[0].wait()
+    def go_home(which, rows):
+        for tt in range(LINE):
+            for cc in range(2):
+                mine = jnp.logical_and(t == tt, c == cc)
+                source = rows.at[tt, pl.ds(cc * depth, depth)]
+                target = homes.at[which, t * 2 + c]
+                sends.start(
+                    source, target, home_sems.at[which, t * 2 + c], at(tt, j, cc),
+                    jnp.logical_not(mine),
+                )
+
+                @pl.when(mine)
+                def _():
+                    homes[which, tt * 2 + cc] = source[...]
+
+    if side == 2:
+        sends.start(down.at[:, 1 - j], downs_got, across_sems.at[2], beside[0])
+    for which, (mine, got) in enumerate(((gates, gates_got), (ups, ups_got))):
+        loads[2 * which].wait()
+        loads[2 * which + 1].wait()
+        for tt in range(LINE):
+            add(mine.at[tt], mine.at[tt], got.at[tt])
+        go_home(which, mine)
+
+    def down_second():
+        loads[4].wait()
+        if side == 2:
+            arrived(downs_got, across_sems.at[2], here)
+        else:
+            loads[6].wait()
+        for xx in range(2):
+            add(downs.at[xx], downs.at[xx], downs_got.at[xx])
+        sends.start(downs.at[1 - x], downs_across, across_sems.at[0], across)
+
+    q_sum[...] = jnp.zeros_like(q_sum)
+    k_sum[...] = jnp.zeros_like(k_sum)
+    rows = hidden.shape[0]
+    group = q_cols // k_cols * HEAD
+
+    @pl.loop(0, k_cols // HEAD)
+    def _(g):
+        pair = pl.multiple_of(g // 2 * LANES, LANES)
+        wide = pl.ds(pl.multiple_of(g * group, group), group)
+        k_pair = pl.ds(q_cols + pair, LANES)
+        v_pair = pl.ds(q_cols + k_cols + pair, LANES)
+        attend_back_kernel(
+            rows // 2, scale, g % 2 == 1, length,
+            proj.at[:, wide], proj.at[:, k_pair], proj.at[:, v_pair],
+            cosine, sine, q_gain, k_gain,
+            totals.at[:, pl.ds(pl.multiple_of(g * LANES, LANES), LANES)],
+            grad_o.at[:, wide],
+            grads.at[:, wide], grads.at[:, k_pair], grads.at[:, v_pair],
+            q_sum, k_sum, keys_sum, vals_sum,
+        )
+
+    width = hidden.shape[1]
+    place_rows = width // LINE
+    tile = min(256, place_rows)
     for q in reversed(range(LINE)):
         tt = slot_place(t, q)
+
+        @pl.loop(0, place_rows // tile)
+        def _(i):
+            span = pl.ds(pl.multiple_of(tt * place_rows + i * tile, tile), tile)
+            grad = mm_tn(hidden[:, span], grads[...]).astype(BF)
+            first = tt * (2 * side) + i * (tile // depth)
+            heads[pl.ds(first, tile // depth)] = grad.reshape(tile // depth, depth, -1)
+
         for r in range(side):
             sends.start(
                 heads.at[block(tt, j ^ r, 1 - c)], heads_core.at[tt, j ^ r],
                 core_sems.at[tt, j ^ r], core,
             )
-    loads[1].wait()
-    loads[2].wait()
-    for tt in range(LINE):
-        for jj in range(side):
-            add(gates.at[tt, jj], gates.at[tt, jj], gates_got.at[tt, jj])
-    for bit in reversed(range(bits)):
-        half = 1 << bit
-        if bit < bits - 1:
-            for r in range(half * 2):
-                arrived(gates_side.at[2 * half - 1 + r], gate_sems.at[2 * half - 1 + r], here)
-                for tt in range(LINE):
-                    add(
-                        gates.at[tt, j ^ r], gates.at[tt, j ^ r],
-                        gates_side.at[2 * half - 1 + r, tt],
-                    )
-        for r in range(half, 2 * half):
-            sends.start(
-                gates.at[:, j ^ r], gates_side.at[half - 1 + r - half],
-                gate_sems.at[half - 1 + r - half], beside[bit],
-            )
+
     loads[5].wait()
-    loads[6].wait()
-    for xx in range(2):
-        add(downs.at[xx], downs.at[xx], downs_got.at[xx])
-    loads[3].wait()
-    loads[4].wait()
-    for tt in range(LINE):
-        add(ups.at[tt], ups.at[tt], ups_got.at[tt])
-    far_col = pl.multiple_of((1 - x) * strip, strip)
-    sends.start(
-        ups.at[:, :, pl.ds(far_col, strip)], ups_across, across_sems.at[0], across
-    )
-    sends.start(downs.at[1 - x], downs_across, across_sems.at[1], across)
-
-    loads[7].wait()
+    wide = min(512, width)
+    for i in range(width // wide):
+        cols = pl.ds(i * wide, wide)
+        grad = mm_nt(grads[...], weights[cols, :])
+        low[:, cols] = grad.astype(BF)
+        part = jnp.sum(grad * hidden[:, cols].astype(F32), axis=0, keepdims=True)
+        part = part / attn_gain[:, cols]
+        for k in range(wide // LANES):
+            smalls[0, pl.ds(i * (wide // LANES) + k, 1), :] = part[:, k * LANES : (k + 1) * LANES]
+    sends.start(low, low_got, across_sems.at[1], across)
+    down_second()
+    count = width // LANES
+    smalls[0, pl.ds(count, count), :] = ffn_part[...]
+    q_part, k_part = q_sum[...], k_sum[...]
+    q_part = q_part + pltpu.roll(q_part, HEAD, 1)
+    k_part = k_part + pltpu.roll(k_part, HEAD, 1)
+    smalls[0, pl.ds(2 * count, 1), :] = jnp.where(low_lanes(q_part.shape), q_part, k_part)
+
     partners = [core] + beside + [across, at(t ^ 1, j, c), at(t ^ 2, j, c)]
 
     def small_step(i):
@@ -1162,26 +1343,6 @@
     line_go(1, 1, t >= 2, p2)
     side_first(0)
 
-    def go_home(which, rows):
-        for tt in range(LINE):
-            for cc in range(2):
-                mine = jnp.logical_and(t == tt, c == cc)
-                source = rows(tt).at[pl.ds(cc * depth, depth)]
-                target = homes.at[which, t * 2 + c]
-                sends.start(
-                    source, target, home_sems.at[which, t * 2 + c], at(tt, j, cc),
-                    jnp.logical_not(mine),
-                )
-
-                @pl.when(mine)
-                def _():
-                    homes[which, tt * 2 + cc] = source[...]
-
-    if bits:
-        arrived(gates_side.at[0], gate_sems.at[0], here)
-        for tt in range(LINE):
-            add(gates.at[tt, j], gates.at[tt, j], gates_side.at[0, tt])
-    go_home(0, lambda tt: gates.at[tt, j])
     step = small_step(step)
     p1 = side_rest(1)
     line_came(1, 0, jnp.logical_and(t >= 1, t <= 2), p3)
@@ -1189,14 +1350,10 @@
     line_go(2, 0, t == 0, p1)
     line_go(2, 0, jnp.logical_and(t >= 1, t <= 2), p3)
     line_go(2, 1, t >= 1, p1)
-    arrived(ups_across, across_sems.at[0], here)
-    for tt in range(LINE):
-        add(ups_across.at[tt], ups.at[tt, :, pl.ds(near_col, strip)], ups_across.at[tt])
-    go_home(1, lambda tt: ups_across.at[tt])
     while step <= len(partners):
         step = small_step(step)
     small_out[...] = smalls[2 * len(partners) - 1]
-    arrived(downs_across, across_sems.at[1], here)
+    arrived(downs_across, across_sems.at[0], here)
     add(down_out, downs.at[x], downs_across)
     p0 = side_rest(0)
     line_came(2, 0, t >= 1, p0)
@@ -1204,7 +1361,16 @@
     q_out[...] = p0[:, pl.ds(0, q_cols)].astype(F32)
     k_out[...] = p0[:, pl.ds(q_cols, k_cols)].astype(F32)
     v_out[...] = p0[:, pl.ds(q_cols + k_cols, k_cols)].astype(F32)
+    stores = []
+
+    def store(source, target):
+        copy = pltpu.make_async_copy(source, target, store_sems.at[len(stores)])
+        copy.start()
+        stores.append(copy)
+
     for which, out in enumerate((gate_out, up_out)):
+        if which:
+            stores[0].wait()
         for tt in range(LINE):
             for cc in range(2):
                 mine = jnp.logical_and(t == tt, c == cc)
@@ -1216,33 +1382,49 @@
                     ),
                 )
                 for jj in range(side):
-                    out[:, pl.ds(block(tt, jj, cc) * piece, piece)] = source[
+                    wide_out[:, pl.ds(block(tt, jj, cc) * piece, piece)] = source[
                         :, pl.ds(jj * piece, piece)
                     ].astype(F32)
+        store(wide_out, out)
+    arrived(low_got, across_sems.at[1], here)
+    store(low, low_out)
+    store(low_got, low_got_out)
     sends.wait_sent()
-
-
-def sum_gradients(n, piece, q_cols, g_qkv, gate, gate_got, up, up_got, down, down_got, small):
+    for copy in stores[1:]:
+        copy.wait()
+
+
+def end_layer(n, piece, pairs, down, w_qkv, length, hidden, proj, totals, grad_o, tables, gains,
+              attn_gain, ffn_part):
     side = n // LINE // 2
     bits = side.bit_length() - 1
-    _, depth, cols = g_qkv.shape
+    rows, width = hidden.shape
+    cols = w_qkv.shape[1]
+    q_cols = grad_o.shape[1]
+    depth = width // n
     k_cols = (cols - q_cols) // 2
     strip = side * piece
-    width = down.shape[-1]
     any_space = pl.BlockSpec(memory_space=pl.ANY)
+    vmem = pl.BlockSpec(memory_space=pltpu.VMEM)
     steps = bits + 4
+    sides = max(side - 1, 1)
+    home = (LINE, 2 * depth, strip)
     held = [
-        (n, depth, cols), (LINE, side, depth, cols), (LINE, max(side - 1, 1), depth, cols),
+        (n, depth, cols), (LINE, side, depth, cols), (LINE, sides, depth, cols),
         (3, depth, cols), (3, depth, cols),
-        (LINE, side, 2 * depth, strip), (LINE, side, 2 * depth, strip),
-        (max(side - 1, 1), LINE, 2 * depth, strip),
-        (LINE, 2 * depth, 2 * strip), (LINE, 2 * depth, 2 * strip), (LINE, 2 * depth, strip),
+        home, home, home, home,
         (2, piece, width), (2, piece, width), (piece, width),
         (2, LINE * 2, depth, strip),
+        (rows, cols), (width, cols), (rows, width), (rows, width),
     ]
-    sends = LINE * (2 * side - 1) + side + 2 + steps + 8 + 4 * LINE + 4
+    small = (2 * (width // LANES) + 1, LANES)
+    floats = [
+        (depth, LINE * 2 * strip), (rows, LANES), (rows, LANES), (1, LANES), (1, LANES),
+        (2 * steps + 1,) + small,
+    ]
+    sends = LINE * (2 * side - 1) + 3 + steps + 8 + 4 * LINE + 4
     return pl.pallas_call(
-        functools.partial(sum_kernel, side, piece),
+        functools.partial(end_kernel, side, piece, 1.0 / math.sqrt(HEAD)),
         out_shape=[
             jax.ShapeDtypeStruct((depth, q_cols), F32),
             jax.ShapeDtypeStruct((depth, k_cols), F32),
@@ -1250,27 +1432,35 @@
             jax.ShapeDtypeStruct((depth, LINE * 2 * strip), F32),
             jax.ShapeDtypeStruct((depth, LINE * 2 * strip), F32),
             jax.ShapeDtypeStruct((piece, width), F32),
-            jax.ShapeDtypeStruct(small.shape, F32),
+            jax.ShapeDtypeStruct(small, F32),
+            jax.ShapeDtypeStruct((rows, width), BF),
+            jax.ShapeDtypeStruct((rows, width), BF),
         ],
-        in_specs=[any_space] * 8,
+        in_specs=[any_space] * 7 + [pl.BlockSpec(memory_space=pltpu.SMEM)] + [vmem] * 10,
+        out_specs=[vmem] * 3 + [any_space] * 2 + [vmem] * 2 + [any_space] * 2,
         scratch_shapes=[pltpu.VMEM(shape, BF) for shape in held]
-        + [pltpu.VMEM((2 * steps + 1,) + small.shape, F32)]
+        + [pltpu.VMEM(shape, F32) for shape in floats]
         + [
-            pltpu.SemaphoreType.DMA((8,)),
+            pltpu.SemaphoreType.DMA((7,)),
             pltpu.SemaphoreType.DMA((sends,)),
             pltpu.SemaphoreType.DMA((LINE, side)),
-            pltpu.SemaphoreType.DMA((LINE, max(side - 1, 1))),
+            pltpu.SemaphoreType.DMA((LINE, sides)),
             pltpu.SemaphoreType.DMA((2, 3)),
-            pltpu.SemaphoreType.DMA((max(side - 1, 1),)),
-            pltpu.SemaphoreType.DMA((2,)),
+            pltpu.SemaphoreType.DMA((3,)),
             pltpu.SemaphoreType.DMA((2, LINE * 2)),
             pltpu.SemaphoreType.DMA((steps,)),
+            pltpu.SemaphoreType.DMA((4,)),
         ],
         compiler_params=pltpu.CompilerParams(
-            collective_id=2, has_side_effects=True, vmem_limit_bytes=60 << 20
+            collective_id=2, has_side_effects=True, vmem_limit_bytes=62 << 20
         ),
-        cost_estimate=pl.CostEstimate(flops=0, bytes_accessed=400 << 20, transcendentals=0),
-    )(g_qkv, gate, gate_got, up, up_got, down, down_got, small)
+        cost_estimate=pl.CostEstimate(
+            flops=8 * rows * width * cols, bytes_accessed=300 << 20, transcendentals=rows * rows
+        ),
+    )(
+        *pairs, *down, w_qkv, length, hidden, proj, totals, grad_o, *tables, *gains,
+        attn_gain[None, :], ffn_part,
+    )
 
 
 class Links:
@@ -1473,65 +1663,51 @@
         piece = w_down.shape[0]
         side = net.side
         strip = side * piece
-        start = x * half
-        half_positions = start + jnp.arange(half, dtype=jnp.int32)
-        half_valid = (half_positions < slot_length)[:, None]
-        grad_half = lax.dynamic_slice_in_dim(cotangent, start, half, 0)
-        grad_half = jnp.where(half_valid, grad_half, jnp.zeros_like(grad_half))
         tables = angle_tables(row_count, head_dim, LANES)
         gains = [jnp.tile(gain, LANES // head_dim)[None, :] for gain in (query_gain, key_gain)]
         inputs = tokens.astype(F32)
-        input_half = lax.dynamic_slice_in_dim(tokens, start, half, 0)
-        hidden_state = rms_scale(inputs, attn_gain).astype(BF)
         length = slot_length[None]
         weights = (w_query, key_weight_matrix, value_weight_matrix, w_out, w_gate, w_up, w_down)
         (
             qkv_full, wo_full, units, wd, grad_all, qkv, o_low, log_totals, h_one, hidden_two,
+            hidden_state,
         ) = start_layer(
-            n, weights, grad_half, length, hidden_state, input_half, tables, gains, ffn_gain
+            n, weights, cotangent, length, tokens, attn_gain, tables, gains, ffn_gain
         )
 
-        out_parts, grad_parts, gate_kept, gate_got, up_kept, up_got, g_down = feed_forward(
+        (
+            layer_half, grad_attn_low, g_ffn_part, _, _, _, _,
+            g_down, gate_mid, up_mid, gate_kept, gate_got, up_kept, up_got,
+        ) = feed_forward(
             side, hidden_two, grad_all, units.reshape(2, width, 2 * strip),
-            wd.reshape(2 * strip, width),
+            wd.reshape(2 * strip, width), h_one, ffn_gain,
         )
-        grad_hidden_two = jnp.sum(grad_parts.astype(F32), axis=0)
-        out_mine = out_parts[:, :half].astype(F32) + net.core(out_parts[:, half:]).astype(F32)
-        out_sum = net.line_sum(out_mine.astype(BF))
-        norm_two_back = jax.vjp(rms_scale, h_one, ffn_gain)[1]
-        grad_h_part, g_ffn_part = norm_two_back(grad_hidden_two)
-        grad_h_one = grad_half.astype(F32) + grad_h_part
-        grad_attn_half = grad_h_one.astype(BF)
-        grad_attn_low = net.pair_order(grad_attn_half, net.cross(grad_attn_half), x)
-
-        near = (LINE, side, 2 * depth, strip)
-        gate_kept, gate_got = gate_kept.reshape(near), gate_got.reshape(near)
-        up_kept, up_got = net.side_end(up_kept, up_got)
+        layer_out = net.pair_order(layer_half, net.cross(layer_half), x)
+
+        if side != 2:
+            gate_sum = (gate_kept.astype(F32) + gate_mid.astype(F32)).astype(BF)
+            gate_sum = gate_sum.reshape(LINE, side, 2 * depth, strip)
+            gate_kept, gate_got = net.side_start([net.pick(gate_sum, j ^ r, 1) for r in range(side)])
+            up_kept, up_got = net.side_end(up_kept, up_mid)
+            up_sum = (up_kept.astype(F32) + up_got.astype(F32)).astype(BF)
+            up_kept = lax.dynamic_slice_in_dim(up_sum, x * strip, strip, 2)
+            up_got = net.cross(lax.dynamic_slice_in_dim(up_sum, (1 - x) * strip, strip, 2))
         g_down = g_down.reshape(2, side, piece, width)
-        down_kept, down_got = net.side_start([net.pick(g_down, j ^ r, 1) for r in range(side)])
+        down_pair = (g_down, g_down)
+        if side != 2:
+            down_pair = net.side_start([net.pick(g_down, j ^ r, 1) for r in range(side)])
 
         g_out = mm_tn(o_low, grad_attn_low).astype(BF)
         grad_o_low = mm_nt(grad_attn_low, wo_full).astype(BF)
-        grad_q, grad_k, grad_v, q_part, k_part = attend_back(
-            length, qkv, tables, gains, log_totals, grad_o_low, q_cols, k_heads
+        g_out_out = net.dp_sum(g_out).astype(F32)
+        (
+            g_query_w, g_key_w, g_value_w, g_gate_out, g_up_out, g_down_out, small, low, low_got,
+        ) = end_layer(
+            n, piece, (gate_kept, gate_got, up_kept, up_got), down_pair, qkv_full, length,
+            hidden_state, qkv, log_totals, grad_o_low, tables, gains, attn_gain,
+            g_ffn_part.reshape(-1, LANES),
         )
-        g_query_part = q_part.reshape(-1, head_dim).sum(0)
-        g_key_part = k_part.reshape(-1, head_dim).sum(0)
-        grad_qkv = jnp.concatenate([grad_q, grad_k, grad_v], axis=1)
-        g_qkv = mm_tn(hidden_state, grad_qkv).astype(BF)
-        g_out_out = net.dp_sum(g_out).astype(F32)
-        layer_half = (h_one + after(g_qkv, out_sum).astype(F32)).astype(BF)
-        layer_out = net.pair_order(layer_half, net.cross(layer_half), x)
-        grad_hidden = mm_nt(grad_qkv, qkv_full)
-        g_attn_part = jnp.sum(grad_hidden * rms_scale(inputs, 1.0), axis=0)
-        low_hidden = grad_hidden.astype(BF)
-        grad_hidden = low_hidden.astype(F32) + net.cross(low_hidden).astype(F32)
-        small = jnp.concatenate([g_attn_part, g_ffn_part, g_query_part, g_key_part])
-        small = small.reshape(-1, LANES)
-        g_query_w, g_key_w, g_value_w, g_gate_out, g_up_out, g_down_out, small = sum_gradients(
-            n, piece, q_cols, g_qkv.reshape(n, depth, q_cols + 2 * k_cols),
-            gate_kept, gate_got, up_kept, up_got, down_kept, down_got, small,
-        )
+        grad_hidden = low.astype(F32) + low_got.astype(F32)
         small = small.reshape(-1)
         grad_in = jax.vjp(lambda v: rms_scale(v, attn_gain), inputs)[1](grad_hidden)[0]
         input_grad = grad_attn_low.astype(F32) + grad_in

time: 723 us -> 622 us (0.86); the launches traced: 729 us -> 613 us
  waiting for transfers between devices: 86.1 us -> 0.02 us
  Pallas kernels: 535 us -> 555 us
  other arithmetic: 35.6 us -> 16.2 us
  matrix products: 26.4 us -> 11.9 us
  local copies, waits for them, and re-layouts: 27.3 us -> 15.4 us
    ppermute x3 -> x1, waiting for transfers between devices: 67 us -> 0.01 us  [cross(): return lax.ppermute(value, 'tensor', [(0, 1), (1, 0)])]
    pallas_call x1, Pallas kernels: 188 us -> 217 us  [feed_forward(): pl.pallas_call(functools.partial(feed_kernel, side), out_shape=[jax.Shape...]
    ppermute x2 -> x0, waiting for transfers between devices: 19 us -> none  [the longest x1 11.9 us: over(): return lax.ppermute(value, 'dp', [(i, i ^ 2 << bit) for i in range(self.n)])]
    pallas_call x2 -> x1, Pallas kernels: 144 us -> 130 us  [end_layer(): pl.pallas_call(functools.partial(end_kernel, side, piece, 1.0 / math.sqrt...]
    convert_element_type x4 -> x0, other arithmetic: 8.84 us -> none  [the longest x1 4.03 us: body(): out_sum = net.line_sum(out_mine.astype(BF))]
    reduce_sum x5 -> x0, other arithmetic: 8.68 us -> none  [the longest x1 4 us: body(): grad_hidden_two = jnp.sum(grad_parts.astype(F32), axis=0)]
    dot_general x2 -> x1, matrix products: 13.5 us -> 5.53 us  [mm_nt(): lax.dot_general(left, right, (((1,), (1,)), ((), ())), preferred_element_...]
    unnamed x70 -> x24, local copies, waits for them, and re-layouts: 14.5 us -> 10.5 us
  transfers between devices with their start and end apart: 7 -> 2, of which waited for: 5 -> 0; matrix products, arithmetic and copies ran while one was open for 8% -> 3% of each run, Pallas kernels for 20% -> 21%
where the time goes in v4:
time: 622 us; the launch traced here: 613 us
  Pallas kernels  555 us (89%)
  other arithmetic  16.2 us (3%)
  local copies, waits for them, and re-layouts  15.4 us (2%)
  between operations  14.3 us (2%)
  matrix products  11.9 us (2%)
    pallas_call x1, Pallas kernels, feed_forward(): pl.pallas_call(functools.partial(feed_kernel, side), out_shape=[jax.Shape...  217 us
    pallas_call x1, Pallas kernels, start_layer(): pl.pallas_call(functools.partial(start_kernel, side, piece, sliced, 1.0 /...  207 us
    pallas_call x1, Pallas kernels, end_layer(): pl.pallas_call(functools.partial(end_kernel, side, piece, 1.0 / math.sqrt...  130 us
  transfers between devices with their start and end apart: 2, of which 0 were waited for; matrix products, arithmetic and copies ran while one was open for 3% of the time, Pallas kernels for 21%

profile of v4, /device:TPU:0, one launch (start us, length us, event | category | flops | bytes accessed | tf_op | source)
XLA Modules:
  0.0 613.1 jit_solution(5341477290940578009)
XLA Ops:
  7.2 0.0 reduce-scatter.2.cloned.1.call-start
  7.2 0.7 tile.4
  7.9 0.6 broadcast_in_dim_tile.6.refs_13_.refs_14_
  8.5 0.7 tile.5
  9.1 0.6 broadcast_in_dim_tile.7.refs_14_.refs_15_
  9.7 1.2 dynamic_slice.3.refs_8_.refs_7_
  11.0 207.3 %shard_map.255 = (bf16[2048,1536]{1,0:T(8,128)(2,1)}, bf16[1024,2048]{1,0:T(8,128)(2,1)}, bf16[2,4,2,256,1024]{4,3,2,1,0:T(8,128)(2,1)}, bf16[4,256,2048]{2,1,0:...) custom-call(bf16[128,1024]{1,0:T(8,128)(2,1)} %refs_0_.1, ...), custom_call_target="tpu_custom_call" | custom-call | flops 3221225472 | bytes 524288000 | tf_op jit(solution)/shard_map/pallas_call | solution.py:702
  218.2 217.2 %shard_map.256 = (bf16[256,2048]{1,0:T(8,128)(2,1)}, bf16[512,2048]{1,0:T(8,128)(2,1)}, f32[1,2048]{1,0:T(1,128)}, bf16[4,256,2048]{2,1,0:T(8,128)(2,1)}, bf16[4...) custom-call(bf16[256,2048]{1,0:T(8,128)(2,1)} %get-tuple-element.41., ...), custom_call_target="tpu_custom_call" | custom-call | flops 77309411328 | bytes 104857600 | tf_op jit(solution)/shard_map/pallas_call | solution.py:1096
  435.5 6.3 %convolution_convert_fusion = bf16[1024,2048]{1,0:T(8,128)(2,1)} fusion(bf16[512,1024]{1,0:T(8,128)(2,1)} %get-tuple-element.65, bf16[512,2048]{1,0:T(8,128)(2,1)} %get-tuple-element.47), kind=kOutput, calls=%fused_computation.8 | convolution fusion | flops 2149580800 | bytes 7340032 | tf_op jit(solution)/shard_map/dot_general | solution.py:206
  441.8 0.0 copy-start.4
  441.8 0.0 copy-start.1
  441.8 0.0 reduce-scatter.2.cloned.1.call-update
  441.8 1.2 copy-done.4
  443.0 0.5 collective-permute-start
  443.6 0.1 copy-done.1
  443.7 5.5 convolution_convert_fusion.1.refs_11_
  449.2 0.0 copy-start.7
  449.2 130.2 %shard_map.257 = (f32[128,1024]{1,0:T(8,128)}, f32[128,256]{1,0:T(8,128)}, f32[128,256]{1,0:T(8,128)}, f32[128,4096]{1,0:T(8,128)}, f32[128,4096]{1,0:T(8,128)},...) custom-call(bf16[4,256,512]{2,1,0:T(8,128)(2,1)} %get-tuple-element.48.refs_0_,, ...), custom_call_target="tpu_custom_call" | custom-call | flops 12884901888 | bytes 314572800 | tf_op jit(solution)/shard_map/pallas_call | solution.py:1426
  579.5 0.0 copy-start.8
  579.5 0.0 copy-start
  579.5 0.0 copy-done.7
  579.5 4.3 fusion
  583.9 0.0 copy-done.8
  583.9 0.6 fusion.4
  584.4 0.6 slice_bitcast_fusion
  585.1 0.0 copy-done
  585.1 7.0 %fusion.2 = f32[512,2048]{1,0:T(8,128)} fusion(bf16[512,2048]{1,0:T(8,128)(2,1)S(1)} %copy-done, bf16[512,2048]{1,0:T(8,128)(2,1)} %get-tuple-element.47, bf16[512,2048]{1,0:T(8,128)(2,1)} %get-tuple-element.60, bf16[512,2048]{1,0:T(8,128)(2,1)} %get-tuple-element.59, f32[512]{0:T(512)S(1)} %get-tuple-element.78, f32[512]{0:T(512)S(1)} %get-tuple-element.77, ...), kind=kLoop, calls=%fused_computation.6 | loop fusion | flops 11534336 | bytes 12595200 | tf_op jit(solution)/shard_map/add | solution.py:1713
  592.1 0.0 copy-start.6
  592.1 0.0 collective-permute-done
  592.1 1.4 broadcast_select_fusion.1
  593.5 0.0 copy-start.5
  593.5 1.6 pad_maximum_fusion
  595.0 0.0 copy-start.3
  595.1 0.0 reduce-scatter.2.cloned.1.call-done
  595.1 1.9 convert_element_type.27
  597.0 1.9 copy.35
  598.9 0.0 copy-done.6
  598.9 0.7 copy.36
  599.5 0.0 copy-done.5
  599.5 0.7 copy.37
  600.2 0.0 copy-start.2
  600.2 3.3 copy.38
  603.4 0.0 copy-done.3
  603.4 1.3 copy.39
  604.8 0.0 copy-done.2
  604.8 1.3 copy.40
  (1 shorter events, 0.0 us)
Async XLA Ops:
  7.2 587.9 %reduce-scatter.2.cloned.1.call-start = ((), (), s32[]{:S(2)}) async-start(), calls=%async_computation.1 | async-start | bytes 4456448 | tf_op jit(solution)/shard_map/reduce_scatter | solution.py:1525
  441.8 1.2 copy-start.4
  441.8 1.9 copy-start.1
  443.0 149.0 %collective-permute-start = (bf16[256,2048]{1,0:T(8,128)(2,1)S(1)}, bf16[256,2048]{1,0:T(8,128)(2,1)}, u32[]{:S(2)}, u32[]{:S(2)}) collective-permute-start(bf16[256,2048]{1,0:T(8,128)(2,1)S(1)} %copy-done.4), channel_id=1, source_target_pairs={{0,1},{1,0},{2,3},{3,2},{4,5},{5,4},{6,7},{7,6},{8,9},{9,8},{10,11... | collective-permute-start | bytes 3145736 | tf_op jit(solution)/shard_map/ppermute | solution.py:1481
  449.2 130.3 %copy-start.7 = (f32[2048]{0:T(1024)S(1)}, f32[2048]{0:T(1024)}, u32[]{:S(2)}) copy-start(f32[2048]{0:T(1024)} %param.19) | copy-start | bytes 24580
  579.5 4.4 copy-start.8
  579.5 5.6 copy-start
  592.1 6.8 %copy-start.6 = (f32[128,256]{1,0:T(8,128)S(1)}, f32[128,256]{1,0:T(8,128)}, u32[]{:S(2)}) copy-start(f32[128,256]{1,0:T(8,128)} %get-tuple-element.98) | copy-start | bytes 393220
  593.5 6.1 copy-start.5
  595.0 8.4 %copy-start.3 = (f32[128,4096]{1,0:T(8,128)S(1)}, f32[128,4096]{1,0:T(8,128)}, u32[]{:S(2)}) copy-start(f32[128,4096]{1,0:T(8,128)} %get-tuple-element.103) | copy-start | bytes 6291460
  600.2 4.6 copy-start.2
Sparse Core Ops, SparseCore 0:
  441.9 96.9 reduce-scatter.1

commit v5 on v4

--- a/solution.py
+++ b/solution.py
@@ -487,6 +487,7 @@
                             )
 
     set_out(*lines[0])
+    set_out(*lines[1])
     sends.start(down.at[own_down], down.at[own_down], down_sems.at[own_down], across)
     chunk = rows // 16
 
@@ -502,11 +503,12 @@
         kept = dm[t, span, :].astype(F32)
         dm[t, span, :] = jnp.where(row < length[0], kept, 0.0).astype(BF)
 
-    line_step(*lines[0], 1)
-    line_step(*lines[0], 2)
-    units_set_out()
-    set_out(*lines[1])
-    line_step(*lines[0], 3)
+    for k in range(1, LINE):
+        line_step(*lines[0], k)
+        line_step(*lines[1], k)
+        if k == LINE - 2:
+            units_set_out()
+    down_set_out()
     stores = []
 
     def store(source, target):
@@ -537,26 +539,27 @@
                 send_pair(w, tt, j, x, beside[bit])
             send_pair(w, tt, j, x, across)
 
-    def unit_second(tt):
+    def unit_second(tt, by_side):
         for r in range(1, side):
-            for w in (1, 0):
+            for w in range(2):
                 pair_came(w, tt, j ^ r, x)
                 for bit in range(bits):
                     if (1 << bit) > r:
                         send_pair(w, tt, j ^ r, x, beside[bit])
-            send_pair(1, tt, j ^ r, x, across)
-        pair_came(0, tt, j, 1 - x)
-        for bit in range(bits):
-            send_pair(0, tt, j, 1 - x, beside[bit])
-
-    def unit_last(tt):
-        for r in range(1, side):
-            pair_came(0, tt, j ^ r, 1 - x)
+                if w not in by_side:
+                    send_pair(w, tt, j ^ r, x, across)
+        for w in by_side:
+            pair_came(w, tt, j, 1 - x)
             for bit in range(bits):
-                if (1 << bit) > r:
-                    send_pair(0, tt, j ^ r, 1 - x, beside[bit])
-        for r in range(side):
-            pair_came(1, tt, j ^ r, 1 - x)
+                send_pair(w, tt, j, 1 - x, beside[bit])
+
+    def unit_last(tt, by_side):
+        for w in range(2):
+            for r in range(1 if w in by_side else 0, side):
+                pair_came(w, tt, j ^ r, 1 - x)
+                for bit in range(bits):
+                    if w in by_side and (1 << bit) > r:
+                        send_pair(w, tt, j ^ r, 1 - x, beside[bit])
 
     dm_rows = dm.at[t, pl.ds(0, half)]
 
@@ -583,7 +586,6 @@
 
     finish_line(*lines[0])
     store(qkv, outs[0])
-    down_set_out()
     for load in loads[first_unit:]:
         load.wait()
     unit_first(t)
@@ -614,11 +616,6 @@
         )
 
     pl.loop(0, key_heads)(attend_head)
-    for k in range(1, LINE):
-        unit_first(slot_place(t, k))
-    down_rest()
-    for k in range(1, LINE):
-        line_step(*lines[1], k)
 
     finish_line(*lines[1])
     store(out, outs[1])
@@ -638,10 +635,13 @@
         cols = pl.ds(pl.multiple_of(i * wide, wide), wide)
         part[:, cols] = mm(attended[own_rows, :], out[:, cols])
 
-    unit_second(t)
+    for k in range(1, LINE):
+        unit_first(slot_place(t, k))
+    down_rest()
+    unit_second(t, (0,))
     dm_step(1)
     for k in range(1, LINE):
-        unit_second(slot_place(t, k))
+        unit_second(slot_place(t, k), (0, 1))
     dm_step(2)
 
     arrived(cross_got, cross_sem, here)
@@ -657,7 +657,7 @@
 
     dm_step(3)
     for k in range(LINE):
-        unit_last(slot_place(t, k))
+        unit_last(slot_place(t, k), (0, 1) if k else (0,))
     store(units, outs[2])
     for jj in range(side):
         idx = (1 - x) * side + jj
@@ -1134,14 +1134,14 @@
 def end_kernel(side, piece, scale, *refs):
     gate, gate_got, up, up_got, down, down_got, w_qkv, length = refs[:8]
     hidden, proj, totals, grad_o, cosine, sine, q_gain, k_gain, attn_gain, ffn_part = refs[8:18]
-    q_out, k_out, v_out, gate_out, up_out, down_out, small_out, low_out, low_got_out = refs[18:27]
+    q_out, k_out, v_out, homes_out, down_out, small_out, low_out, low_got_out = refs[18:26]
     (
         heads, heads_core, heads_side, line_right, line_left,
         gates, gates_got, ups, ups_got, downs, downs_got, downs_across, homes,
-        grads, weights, low, low_got, wide_out, keys_sum, vals_sum, q_sum, k_sum, smalls,
-    ) = refs[27:50]
-    load_sems, send_sems, core_sems, side_sems, line_sems, across_sems = refs[50:56]
-    home_sems, small_sems, store_sems = refs[56:]
+        grads, weights, low, low_got, keys_sum, vals_sum, q_sum, k_sum, smalls,
+    ) = refs[26:48]
+    load_sems, send_sems, core_sems, side_sems, line_sems, across_sems = refs[48:54]
+    home_sems, small_sems, store_sems = refs[54:]
     t, j, c, x = coordinates()
     bits = side.bit_length() - 1
     depth, q_cols = q_out.shape
@@ -1161,7 +1161,7 @@
     ]
     loads = [
         (gate, gates), (gate_got, gates_got), (up, ups), (up_got, ups_got),
-        (down.at[:, j], downs) if side == 2 else (down, downs),
+        (down.at[x], downs) if side == 2 else (down, downs),
         (w_qkv, weights),
     ]
     if side != 2:
@@ -1199,7 +1199,7 @@
                     homes[which, tt * 2 + cc] = source[...]
 
     if side == 2:
-        sends.start(down.at[:, 1 - j], downs_got, across_sems.at[2], beside[0])
+        sends.start(down.at[1 - x], downs_got, across_sems.at[2], across)
     for which, (mine, got) in enumerate(((gates, gates_got), (ups, ups_got))):
         loads[2 * which].wait()
         loads[2 * which + 1].wait()
@@ -1215,7 +1215,10 @@
             loads[6].wait()
         for xx in range(2):
             add(downs.at[xx], downs.at[xx], downs_got.at[xx])
-        sends.start(downs.at[1 - x], downs_across, across_sems.at[0], across)
+        if side == 2:
+            sends.start(downs.at[1 - j], downs_across, across_sems.at[0], beside[0])
+        else:
+            sends.start(downs.at[1 - x], downs_across, across_sems.at[0], across)
 
     q_sum[...] = jnp.zeros_like(q_sum)
     k_sum[...] = jnp.zeros_like(k_sum)
@@ -1268,7 +1271,6 @@
         for k in range(wide // LANES):
             smalls[0, pl.ds(i * (wide // LANES) + k, 1), :] = part[:, k * LANES : (k + 1) * LANES]
     sends.start(low, low_got, across_sems.at[1], across)
-    down_second()
     count = width // LANES
     smalls[0, pl.ds(count, count), :] = ffn_part[...]
     q_part, k_part = q_sum[...], k_sum[...]
@@ -1342,6 +1344,7 @@
     line_go(1, 0, t <= 1, p2)
     line_go(1, 1, t >= 2, p2)
     side_first(0)
+    down_second()
 
     step = small_step(step)
     p1 = side_rest(1)
@@ -1354,7 +1357,7 @@
         step = small_step(step)
     small_out[...] = smalls[2 * len(partners) - 1]
     arrived(downs_across, across_sems.at[0], here)
-    add(down_out, downs.at[x], downs_across)
+    add(down_out, downs.at[j if side == 2 else x], downs_across)
     p0 = side_rest(0)
     line_came(2, 0, t >= 1, p0)
     line_came(2, 1, t <= 2, p0)
@@ -1368,29 +1371,21 @@
         copy.start()
         stores.append(copy)
 
-    for which, out in enumerate((gate_out, up_out)):
-        if which:
-            stores[0].wait()
+    for which in range(2):
         for tt in range(LINE):
             for cc in range(2):
-                mine = jnp.logical_and(t == tt, c == cc)
-                source = homes.at[which, tt * 2 + cc]
                 when(
-                    jnp.logical_not(mine),
-                    lambda w=which, k=tt * 2 + cc, ref=source: arrived(
-                        ref, home_sems.at[w, k], here
+                    jnp.logical_not(jnp.logical_and(t == tt, c == cc)),
+                    lambda w=which, k=tt * 2 + cc: arrived(
+                        homes.at[w, k], home_sems.at[w, k], here
                     ),
                 )
-                for jj in range(side):
-                    wide_out[:, pl.ds(block(tt, jj, cc) * piece, piece)] = source[
-                        :, pl.ds(jj * piece, piece)
-                    ].astype(F32)
-        store(wide_out, out)
+    store(homes, homes_out)
     arrived(low_got, across_sems.at[1], here)
     store(low, low_out)
     store(low_got, low_got_out)
     sends.wait_sent()
-    for copy in stores[1:]:
+    for copy in stores:
         copy.wait()
 
 
@@ -1419,7 +1414,7 @@
     ]
     small = (2 * (width // LANES) + 1, LANES)
     floats = [
-        (depth, LINE * 2 * strip), (rows, LANES), (rows, LANES), (1, LANES), (1, LANES),
+        (rows, LANES), (rows, LANES), (1, LANES), (1, LANES),
         (2 * steps + 1,) + small,
     ]
     sends = LINE * (2 * side - 1) + 3 + steps + 8 + 4 * LINE + 4
@@ -1429,15 +1424,14 @@
             jax.ShapeDtypeStruct((depth, q_cols), F32),
             jax.ShapeDtypeStruct((depth, k_cols), F32),
             jax.ShapeDtypeStruct((depth, k_cols), F32),
-            jax.ShapeDtypeStruct((depth, LINE * 2 * strip), F32),
-            jax.ShapeDtypeStruct((depth, LINE * 2 * strip), F32),
+            jax.ShapeDtypeStruct((2, LINE * 2, depth, strip), BF),
             jax.ShapeDtypeStruct((piece, width), F32),
             jax.ShapeDtypeStruct(small, F32),
             jax.ShapeDtypeStruct((rows, width), BF),
             jax.ShapeDtypeStruct((rows, width), BF),
         ],
         in_specs=[any_space] * 7 + [pl.BlockSpec(memory_space=pltpu.SMEM)] + [vmem] * 10,
-        out_specs=[vmem] * 3 + [any_space] * 2 + [vmem] * 2 + [any_space] * 2,
+        out_specs=[vmem] * 3 + [any_space] + [vmem] * 2 + [any_space] * 2,
         scratch_shapes=[pltpu.VMEM(shape, BF) for shape in held]
         + [pltpu.VMEM(shape, F32) for shape in floats]
         + [
@@ -1461,6 +1455,51 @@
         *pairs, *down, w_qkv, length, hidden, proj, totals, grad_o, *tables, *gains,
         attn_gain[None, :], ffn_part,
     )
+
+
+def finish_kernel(side, piece, homes, low, low_got, tokens, dab, gain, gate, up, grad):
+    count = gate.shape[0]
+    for which, out in enumerate((gate, up)):
+        for tt in range(LINE):
+            for jj in range(side):
+                for cc in range(2):
+                    col = ((tt * side + jj) * 2 + cc) * piece
+                    out[:, pl.ds(col, piece)] = homes[
+                        which, tt * 2 + cc, pl.ds(0, count), pl.ds(jj * piece, piece)
+                    ].astype(F32)
+    values = tokens[...].astype(F32)
+    scale = lax.rsqrt(jnp.mean(values * values, axis=1, keepdims=True) + EPS)
+    part = (low[...].astype(F32) + low_got[...].astype(F32)) * gain[...]
+    back = jnp.mean(part * values, axis=1, keepdims=True) * scale * scale
+    grad[...] = dab[...].astype(F32) + scale * (part - values * back)
+
+
+def finish(side, piece, homes, low, low_got, tokens, dab, gain):
+    rows, width = tokens.shape
+    depth, strip = homes.shape[2], homes.shape[3]
+    steps = 8 if depth % 128 == 0 else 2
+    columns = LINE * 2 * strip
+    block = pl.BlockSpec((rows // steps, width), lambda i: (i, 0))
+    wide = pl.BlockSpec((depth // steps, columns), lambda i: (i, 0))
+    return pl.pallas_call(
+        functools.partial(finish_kernel, side, piece),
+        grid=(steps,),
+        in_specs=[
+            pl.BlockSpec((2, LINE * 2, depth // steps, strip), lambda i: (0, 0, i, 0)),
+            block, block, block, block,
+            pl.BlockSpec((1, width), lambda i: (0, 0)),
+        ],
+        out_specs=[wide, wide, block],
+        out_shape=[
+            jax.ShapeDtypeStruct((depth, columns), F32),
+            jax.ShapeDtypeStruct((depth, columns), F32),
+            jax.ShapeDtypeStruct((rows, width), F32),
+        ],
+        compiler_params=pltpu.CompilerParams(vmem_limit_bytes=62 << 20),
+        cost_estimate=pl.CostEstimate(
+            flops=20 * rows * width, bytes_accessed=20 << 20, transcendentals=0
+        ),
+    )(homes, low, low_got, tokens, dab, gain[None, :])
 
 
 class Links:
@@ -1665,7 +1704,6 @@
         strip = side * piece
         tables = angle_tables(row_count, head_dim, LANES)
         gains = [jnp.tile(gain, LANES // head_dim)[None, :] for gain in (query_gain, key_gain)]
-        inputs = tokens.astype(F32)
         length = slot_length[None]
         weights = (w_query, key_weight_matrix, value_weight_matrix, w_out, w_gate, w_up, w_down)
         (
@@ -1701,16 +1739,16 @@
         grad_o_low = mm_nt(grad_attn_low, wo_full).astype(BF)
         g_out_out = net.dp_sum(g_out).astype(F32)
         (
-            g_query_w, g_key_w, g_value_w, g_gate_out, g_up_out, g_down_out, small, low, low_got,
+            g_query_w, g_key_w, g_value_w, homes, g_down_out, small, low, low_got,
         ) = end_layer(
             n, piece, (gate_kept, gate_got, up_kept, up_got), down_pair, qkv_full, length,
             hidden_state, qkv, log_totals, grad_o_low, tables, gains, attn_gain,
             g_ffn_part.reshape(-1, LANES),
         )
-        grad_hidden = low.astype(F32) + low_got.astype(F32)
+        g_gate_out, g_up_out, input_grad = finish(
+            side, piece, homes, low, low_got, tokens, grad_attn_low, attn_gain
+        )
         small = small.reshape(-1)
-        grad_in = jax.vjp(lambda v: rms_scale(v, attn_gain), inputs)[1](grad_hidden)[0]
-        input_grad = grad_attn_low.astype(F32) + grad_in
         return (
             layer_out,
             input_grad,

time: 622 us -> 602 us (0.968)
  other arithmetic: 16.2 us -> 4.86 us
    pallas_call x0 -> x1, Pallas kernels: none -> 9.53 us  [finish(): pl.pallas_call(functools.partial(finish_kernel, side, piece), grid=(steps...]
    pallas_call x1, Pallas kernels: 130 us -> 122 us  [end_layer(): pl.pallas_call(functools.partial(end_kernel, side, piece, 1.0 / math.sqrt...]
    add x1 -> x0, other arithmetic: 7.01 us -> none  [body(): input_grad = grad_attn_low.astype(F32) + grad_in]
  transfers between devices with their start and end apart: 2 -> 2, of which waited for: 0 -> 0; matrix products, arithmetic and copies ran while one was open for 3% -> 2% of each run, Pallas kernels for 21% -> 22%
where the time goes in v5:
time: 602 us; the launch traced here: 592 us
  Pallas kernels  550 us (91%)
  between operations  14.6 us (2%)
  matrix products  11.9 us (2%)
  local copies, waits for them, and re-layouts  9.57 us (2%)
    pallas_call x1, Pallas kernels, feed_forward(): pl.pallas_call(functools.partial(feed_kernel, side), out_shape=[jax.Shape...  217 us
    pallas_call x1, Pallas kernels, start_layer(): pl.pallas_call(functools.partial(start_kernel, side, piece, sliced, 1.0 /...  202 us
    pallas_call x1, Pallas kernels, end_layer(): pl.pallas_call(functools.partial(end_kernel, side, piece, 1.0 / math.sqrt...  122 us
  transfers between devices with their start and end apart: 2, of which 0 were waited for; matrix products, arithmetic and copies ran while one was open for 2% of the time, Pallas kernels for 22%

profile of v5, /device:TPU:0, one launch (start us, length us, event | category | flops | bytes accessed | tf_op | source)
XLA Modules:
  0.0 592.5 jit_solution(16922936501421105437)
XLA Ops:
  7.2 0.0 reduce-scatter.2.cloned.1.call-start
  7.2 0.7 tile.4
  7.9 0.6 broadcast_in_dim_tile.6.refs_13_.refs_14_
  8.5 0.7 tile.5
  9.1 0.6 broadcast_in_dim_tile.7.refs_14_.refs_15_
  9.7 1.2 dynamic_slice.3.refs_8_.refs_7_
  11.0 201.7 %shard_map.255 = (bf16[2048,1536]{1,0:T(8,128)(2,1)}, bf16[1024,2048]{1,0:T(8,128)(2,1)}, bf16[2,4,2,256,1024]{4,3,2,1,0:T(8,128)(2,1)}, bf16[4,256,2048]{2,1,0:...) custom-call(bf16[128,1024]{1,0:T(8,128)(2,1)} %refs_0_.1, ...), custom_call_target="tpu_custom_call" | custom-call | flops 3221225472 | bytes 524288000 | tf_op jit(solution)/shard_map/pallas_call | solution.py:702
  212.7 217.2 %shard_map.256 = (bf16[256,2048]{1,0:T(8,128)(2,1)}, bf16[512,2048]{1,0:T(8,128)(2,1)}, f32[1,2048]{1,0:T(1,128)}, bf16[4,256,2048]{2,1,0:T(8,128)(2,1)}, bf16[4...) custom-call(bf16[256,2048]{1,0:T(8,128)(2,1)} %get-tuple-element.43., ...), custom_call_target="tpu_custom_call" | custom-call | flops 77309411328 | bytes 104857600 | tf_op jit(solution)/shard_map/pallas_call | solution.py:1096
  429.9 6.3 %convolution_convert_fusion = bf16[1024,2048]{1,0:T(8,128)(2,1)} fusion(bf16[512,1024]{1,0:T(8,128)(2,1)} %get-tuple-element.69, bf16[512,2048]{1,0:T(8,128)(2,1)} %get-tuple-element.58.dab), kind=kOutput, calls=%fused_computation | convolution fusion | flops 2149580800 | bytes 7340032 | tf_op jit(solution)/shard_map/dot_general | solution.py:206
  436.2 0.0 copy-start.2
  436.2 0.0 copy-start.1
  436.2 0.0 reduce-scatter.2.cloned.1.call-update
  436.2 1.2 copy-done.2
  437.4 1.5 collective-permute-start
  438.9 0.0 copy-done.1
  438.9 5.5 convolution_convert_fusion.1.refs_11_
  444.4 121.7 %shard_map.257 = (f32[128,1024]{1,0:T(8,128)}, f32[128,256]{1,0:T(8,128)}, f32[128,256]{1,0:T(8,128)}, bf16[2,8,128,512]{3,2,1,0:T(8,128)(2,1)}, f32[256,2048]{1...) custom-call(bf16[4,256,512]{2,1,0:T(8,128)(2,1)} %get-tuple-element.49.refs_0_, ...), custom_call_target="tpu_custom_call" | custom-call | flops 12884901888 | bytes 314572800 | tf_op jit(solution)/shard_map/pallas_call | solution.py:1421
  566.1 0.0 copy-start.6
  566.1 9.5 %shard_map.258 = (f32[128,4096]{1,0:T(8,128)}, f32[128,4096]{1,0:T(8,128)}, f32[512,2048]{1,0:T(8,128)}) custom-call(bf16[2,8,128,512]{3,2,1,0:T(8,128)(2,1)} %get-tuple-element.61.homes, bf16[512,2048]{1,0:T(8,128)(2,1)} %get-tuple-element.62.low, bf16[512,2048]{1,0:T(8,128)(2,1)} %get-tuple-element.63.low_got, bf16[512,2048]{1,0:T(8,128)(2,1)} %tokens.1, ...), custom_call_target="tpu_custom_call" | custom-call | flops 20971520 | bytes 20971520 | tf_op jit(solution)/shard_map/pallas_call | solution.py:1484
  575.7 0.0 copy-done.6
  575.7 0.6 fusion
  576.3 0.6 slice_bitcast_fusion
  576.9 0.0 collective-permute-done
  576.9 1.4 broadcast_select_fusion.1
  578.2 0.0 copy-start.3
  578.2 0.0 copy-start.5
  578.3 0.0 copy-start.4
  578.3 1.6 pad_maximum_fusion
  579.8 0.0 copy-start
  579.8 0.0 reduce-scatter.2.cloned.1.call-done
  579.8 1.9 convert_element_type.11
  581.8 0.0 copy-done.3
  581.8 0.8 copy.33
  582.6 0.0 copy-done.5
  582.6 0.7 copy.34
  583.2 0.0 copy-done.4
  583.2 0.7 copy.35
  583.9 0.0 copy-done
  583.9 1.3 copy.36
Async XLA Ops:
  7.2 572.7 %reduce-scatter.2.cloned.1.call-start = ((), (), s32[]{:S(2)}) async-start(), calls=%async_computation.1 | async-start | bytes 4456448 | tf_op jit(solution)/shard_map/reduce_scatter | solution.py:1564
  436.2 1.2 copy-start.2
  436.2 2.7 copy-start.1
  437.4 139.4 %collective-permute-start = (bf16[256,2048]{1,0:T(8,128)(2,1)S(1)}, bf16[256,2048]{1,0:T(8,128)(2,1)}, u32[]{:S(2)}, u32[]{:S(2)}) collective-permute-start(bf16[256,2048]{1,0:T(8,128)(2,1)S(1)} %copy-done.2), channel_id=1, source_target_pairs={{0,1},{1,0},{2,3},{3,2},{4,5},{5,4},{6,7},{7,6},{8,9},{9,8},{10,11... | collective-permute-start | bytes 3145736 | tf_op jit(solution)/shard_map/ppermute | solution.py:1520
  566.1 9.5 %copy-start.6 = (f32[33,128]{1,0:T(8,128)S(1)}, f32[33,128]{1,0:T(8,128)}, u32[]{:S(2)}) copy-start(f32[33,128]{1,0:T(8,128)} %get-tuple-element.65) | copy-start | bytes 50692
  578.2 3.5 copy-start.3
  578.2 4.3 copy-start.5
  578.3 5.0 copy-start.4
  579.8 4.0 copy-start
Sparse Core Ops, SparseCore 0:
  436.3 95.7 reduce-scatter.1

commit v6 on v5

--- a/solution.py
+++ b/solution.py
@@ -1132,16 +1132,17 @@
 
 
 def end_kernel(side, piece, scale, *refs):
-    gate, gate_got, up, up_got, down, down_got, w_qkv, length = refs[:8]
-    hidden, proj, totals, grad_o, cosine, sine, q_gain, k_gain, attn_gain, ffn_part = refs[8:18]
-    q_out, k_out, v_out, homes_out, down_out, small_out, low_out, low_got_out = refs[18:26]
+    gate, gate_got, up, up_got, down, down_got, w_qkv, w_out, dab, length = refs[:10]
+    hidden, proj, totals, cosine, sine, q_gain, k_gain, attn_gain, ffn_part = refs[10:19]
+    q_out, k_out, v_out, homes_out, down_out, small_out, low_out, low_got_out = refs[19:27]
     (
         heads, heads_core, heads_side, line_right, line_left,
         gates, gates_got, ups, ups_got, downs, downs_got, downs_across, homes,
-        grads, weights, low, low_got, keys_sum, vals_sum, q_sum, k_sum, smalls,
-    ) = refs[26:48]
-    load_sems, send_sems, core_sems, side_sems, line_sems, across_sems = refs[48:54]
-    home_sems, small_sems, store_sems = refs[54:]
+        grads, weights, low, low_got, grad_o, out_held, dab_held,
+        keys_sum, vals_sum, q_sum, k_sum, smalls,
+    ) = refs[27:52]
+    load_sems, send_sems, core_sems, side_sems, line_sems, across_sems = refs[52:58]
+    home_sems, small_sems, store_sems = refs[58:]
     t, j, c, x = coordinates()
     bits = side.bit_length() - 1
     depth, q_cols = q_out.shape
@@ -1166,6 +1167,7 @@
     ]
     if side != 2:
         loads.append((down_got, downs_got))
+    loads += [(w_out, out_held), (dab, dab_held)]
     loads = [pltpu.make_async_copy(a, b, load_sems.at[i]) for i, (a, b) in enumerate(loads)]
     for load in loads:
         load.start()
@@ -1219,6 +1221,15 @@
             sends.start(downs.at[1 - j], downs_across, across_sems.at[0], beside[0])
         else:
             sends.start(downs.at[1 - x], downs_across, across_sems.at[0], across)
+
+    loads[-2].wait()
+    loads[-1].wait()
+    tile = min(512, q_cols)
+
+    @pl.loop(0, q_cols // tile)
+    def _(i):
+        cols = pl.ds(pl.multiple_of(i * tile, tile), tile)
+        grad_o[:, cols] = mm_nt(dab_held[...], out_held[cols, :]).astype(BF)
 
     q_sum[...] = jnp.zeros_like(q_sum)
     k_sum[...] = jnp.zeros_like(k_sum)
@@ -1389,13 +1400,13 @@
         copy.wait()
 
 
-def end_layer(n, piece, pairs, down, w_qkv, length, hidden, proj, totals, grad_o, tables, gains,
-              attn_gain, ffn_part):
+def end_layer(n, piece, pairs, down, w_qkv, w_out, dab, length, hidden, proj, totals, tables,
+              gains, attn_gain, ffn_part):
     side = n // LINE // 2
     bits = side.bit_length() - 1
     rows, width = hidden.shape
     cols = w_qkv.shape[1]
-    q_cols = grad_o.shape[1]
+    q_cols = w_out.shape[0]
     depth = width // n
     k_cols = (cols - q_cols) // 2
     strip = side * piece
@@ -1411,6 +1422,7 @@
         (2, piece, width), (2, piece, width), (piece, width),
         (2, LINE * 2, depth, strip),
         (rows, cols), (width, cols), (rows, width), (rows, width),
+        (rows, q_cols), (q_cols, width), (rows, width),
     ]
     small = (2 * (width // LANES) + 1, LANES)
     floats = [
@@ -1430,12 +1442,12 @@
             jax.ShapeDtypeStruct((rows, width), BF),
             jax.ShapeDtypeStruct((rows, width), BF),
         ],
-        in_specs=[any_space] * 7 + [pl.BlockSpec(memory_space=pltpu.SMEM)] + [vmem] * 10,
+        in_specs=[any_space] * 9 + [pl.BlockSpec(memory_space=pltpu.SMEM)] + [vmem] * 9,
         out_specs=[vmem] * 3 + [any_space] + [vmem] * 2 + [any_space] * 2,
         scratch_shapes=[pltpu.VMEM(shape, BF) for shape in held]
         + [pltpu.VMEM(shape, F32) for shape in floats]
         + [
-            pltpu.SemaphoreType.DMA((7,)),
+            pltpu.SemaphoreType.DMA((9,)),
             pltpu.SemaphoreType.DMA((sends,)),
             pltpu.SemaphoreType.DMA((LINE, side)),
             pltpu.SemaphoreType.DMA((LINE, sides)),
@@ -1452,7 +1464,7 @@
             flops=8 * rows * width * cols, bytes_accessed=300 << 20, transcendentals=rows * rows
         ),
     )(
-        *pairs, *down, w_qkv, length, hidden, proj, totals, grad_o, *tables, *gains,
+        *pairs, *down, w_qkv, w_out, dab, length, hidden, proj, totals, *tables, *gains,
         attn_gain[None, :], ffn_part,
     )
 
@@ -1736,13 +1748,12 @@
             down_pair = net.side_start([net.pick(g_down, j ^ r, 1) for r in range(side)])
 
         g_out = mm_tn(o_low, grad_attn_low).astype(BF)
-        grad_o_low = mm_nt(grad_attn_low, wo_full).astype(BF)
         g_out_out = net.dp_sum(g_out).astype(F32)
         (
             g_query_w, g_key_w, g_value_w, homes, g_down_out, small, low, low_got,
         ) = end_layer(
-            n, piece, (gate_kept, gate_got, up_kept, up_got), down_pair, qkv_full, length,
-            hidden_state, qkv, log_totals, grad_o_low, tables, gains, attn_gain,
+            n, piece, (gate_kept, gate_got, up_kept, up_got), down_pair, qkv_full, wo_full,
+            grad_attn_low, length, hidden_state, qkv, log_totals, tables, gains, attn_gain,
             g_ffn_part.reshape(-1, LANES),
         )
         g_gate_out, g_up_out, input_grad = finish(

time: 602 us -> 602 us (level)
  transfers between devices with their start and end apart: 2 -> 2, of which waited for: 0 -> 0; matrix products, arithmetic and copies ran while one was open for 2% -> 1% of each run, Pallas kernels for 22% -> 23%
where the time goes in v6:
time: 602 us; the launch traced here: 593 us
  Pallas kernels  556 us (92%)
  between operations  14.6 us (2%)
  local copies, waits for them, and re-layouts  9.57 us (2%)
  matrix products  6.34 us (1%)
    pallas_call x1, Pallas kernels, feed_forward(): pl.pallas_call(functools.partial(feed_kernel, side), out_shape=[jax.Shape...  217 us
    pallas_call x1, Pallas kernels, start_layer(): pl.pallas_call(functools.partial(start_kernel, side, piece, sliced, 1.0 /...  202 us
    pallas_call x1, Pallas kernels, end_layer(): pl.pallas_call(functools.partial(end_kernel, side, piece, 1.0 / math.sqrt...  127 us
  transfers between devices with their start and end apart: 2, of which 0 were waited for; matrix products, arithmetic and copies ran while one was open for 1% of the time, Pallas kernels for 23%

profile of v6, /device:TPU:0, one launch (start us, length us, event | category | flops | bytes accessed | tf_op | source)
XLA Modules:
  0.0 592.5 jit_solution(4643321453417048982)
XLA Ops:
  7.2 0.0 reduce-scatter.2.cloned.1.call-start
  7.2 0.7 tile.4
  7.9 0.6 broadcast_in_dim_tile.6.refs_13_.refs_15_
  8.5 0.7 tile.5
  9.1 0.6 broadcast_in_dim_tile.7.refs_14_.refs_16_
  9.7 1.2 dynamic_slice.3.refs_8_.refs_9_
  11.0 201.7 %shard_map.255 = (bf16[2048,1536]{1,0:T(8,128)(2,1)}, bf16[1024,2048]{1,0:T(8,128)(2,1)}, bf16[2,4,2,256,1024]{4,3,2,1,0:T(8,128)(2,1)}, bf16[4,256,2048]{2,1,0:...) custom-call(bf16[128,1024]{1,0:T(8,128)(2,1)} %refs_0_.1, ...), custom_call_target="tpu_custom_call" | custom-call | flops 3221225472 | bytes 524288000 | tf_op jit(solution)/shard_map/pallas_call | solution.py:702
  212.6 217.2 %shard_map.256 = (bf16[256,2048]{1,0:T(8,128)(2,1)}, bf16[512,2048]{1,0:T(8,128)(2,1)}, f32[1,2048]{1,0:T(1,128)}, bf16[4,256,2048]{2,1,0:T(8,128)(2,1)}, bf16[4...) custom-call(bf16[256,2048]{1,0:T(8,128)(2,1)} %get-tuple-element.43., ...), custom_call_target="tpu_custom_call" | custom-call | flops 77309411328 | bytes 104857600 | tf_op jit(solution)/shard_map/pallas_call | solution.py:1096
  429.8 6.3 %convolution_convert_fusion = bf16[1024,2048]{1,0:T(8,128)(2,1)} fusion(bf16[512,1024]{1,0:T(8,128)(2,1)} %get-tuple-element.69, bf16[512,2048]{1,0:T(8,128)(2,1)} %get-tuple-element.56.refs_8_.dab), kind=kOutput, calls=%fused_computation | convolution fusion | flops 2149580800 | bytes 7340032 | tf_op jit(solution)/shard_map/dot_general | solution.py:206
  436.2 0.0 copy-start.1
  436.2 0.0 reduce-scatter.2.cloned.1.call-update
  436.2 1.2 copy-done.1
  437.4 1.5 collective-permute-start
  438.9 127.2 %shard_map.257 = (f32[128,1024]{1,0:T(8,128)}, f32[128,256]{1,0:T(8,128)}, f32[128,256]{1,0:T(8,128)}, bf16[2,8,128,512]{3,2,1,0:T(8,128)(2,1)}, f32[256,2048]{1...) custom-call(bf16[4,256,512]{2,1,0:T(8,128)(2,1)} %get-tuple-element.49.refs_0_, ...), custom_call_target="tpu_custom_call" | custom-call | flops 12884901888 | bytes 314572800 | tf_op jit(solution)/shard_map/pallas_call | solution.py:1433
  566.1 0.0 copy-start.5
  566.2 9.5 %shard_map.258 = (f32[128,4096]{1,0:T(8,128)}, f32[128,4096]{1,0:T(8,128)}, f32[512,2048]{1,0:T(8,128)}) custom-call(bf16[2,8,128,512]{3,2,1,0:T(8,128)(2,1)} %get-tuple-element.61.homes, bf16[512,2048]{1,0:T(8,128)(2,1)} %get-tuple-element.62.low, bf16[512,2048]{1,0:T(8,128)(2,1)} %get-tuple-element.63.low_got, bf16[512,2048]{1,0:T(8,128)(2,1)} %tokens.1, ...), custom_call_target="tpu_custom_call" | custom-call | flops 20971520 | bytes 20971520 | tf_op jit(solution)/shard_map/pallas_call | solution.py:1496
  575.7 0.0 copy-done.5
  575.7 0.6 fusion
  576.3 0.6 slice_bitcast_fusion
  576.9 0.0 collective-permute-done
  576.9 1.4 broadcast_select_fusion.1
  578.3 0.0 copy-start.2
  578.3 0.0 copy-start.4
  578.3 0.0 copy-start.3
  578.3 1.6 pad_maximum_fusion
  579.9 0.0 copy-start
  579.9 0.0 reduce-scatter.2.cloned.1.call-done
  579.9 1.9 convert_element_type.7
  581.8 0.0 copy-done.2
  581.8 0.8 copy.33
  582.6 0.0 copy-done.4
  582.6 0.7 copy.34
  583.2 0.0 copy-done.3
  583.2 0.7 copy.35
  583.9 0.0 copy-done
  583.9 1.3 copy.36
Async XLA Ops:
  7.2 572.7 %reduce-scatter.2.cloned.1.call-start = ((), (), s32[]{:S(2)}) async-start(), calls=%async_computation.1 | async-start | bytes 4456448 | tf_op jit(solution)/shard_map/reduce_scatter | solution.py:1576
  436.2 1.2 copy-start.1
  437.4 139.5 %collective-permute-start = (bf16[256,2048]{1,0:T(8,128)(2,1)S(1)}, bf16[256,2048]{1,0:T(8,128)(2,1)}, u32[]{:S(2)}, u32[]{:S(2)}) collective-permute-start(bf16[256,2048]{1,0:T(8,128)(2,1)S(1)} %copy-done.1), channel_id=1, source_target_pairs={{0,1},{1,0},{2,3},{3,2},{4,5},{5,4},{6,7},{7,6},{8,9},{9,8},{10,11... | collective-permute-start | bytes 3145736 | tf_op jit(solution)/shard_map/ppermute | solution.py:1532
  566.1 9.5 %copy-start.5 = (f32[33,128]{1,0:T(8,128)S(1)}, f32[33,128]{1,0:T(8,128)}, u32[]{:S(2)}) copy-start(f32[33,128]{1,0:T(8,128)} %get-tuple-element.65) | copy-start | bytes 50692
  578.3 3.5 copy-start.2
  578.3 4.3 copy-start.4
  578.3 5.0 copy-start.3
  579.9 4.0 copy-start
Sparse Core Ops, SparseCore 0:
  436.3 92.5 reduce-scatter.1

commit v7 on v6

--- a/solution.py
+++ b/solution.py
@@ -656,9 +656,6 @@
         hidden_two[span, :] = rms_scale(total, ffn_gain[...]).astype(BF)
 
     dm_step(3)
-    for k in range(LINE):
-        unit_last(slot_place(t, k), (0, 1) if k else (0,))
-    store(units, outs[2])
     for jj in range(side):
         idx = (1 - x) * side + jj
         arrived(down.at[idx], down_sems.at[idx], here)
@@ -666,6 +663,10 @@
     for tt in range(LINE):
         arrived(dm.at[tt, pl.ds(half, half)], core_sems.at[tt], here)
     store(dm, outs[4])
+    for k in range(LINE):
+        place_of = slot_place(t, k)
+        unit_last(place_of, (0, 1) if k else (0,))
+        store(units.at[:, place_of], outs[2].at[:, place_of])
     sends.wait_sent()
     for copy in stores:
         copy.wait()
@@ -727,7 +728,7 @@
             pltpu.SemaphoreType.DMA((LINE,)),
             pltpu.SemaphoreType.DMA((LINE,)),
             pltpu.SemaphoreType.DMA,
-            pltpu.SemaphoreType.DMA((5,)),
+            pltpu.SemaphoreType.DMA((8,)),
         ],
         compiler_params=pltpu.CompilerParams(
             collective_id=0, has_side_effects=True, vmem_limit_bytes=62 << 20

time: 602 us -> 596 us (0.990)
  no operation moved by 1% of the time
where the time goes in v7:
time: 596 us; the launch traced here: 587 us
  Pallas kernels  550 us (92%)
  between operations  14.6 us (2%)
  local copies, waits for them, and re-layouts  9.57 us (2%)
  matrix products  6.34 us (1%)
    pallas_call x1, Pallas kernels, feed_forward(): pl.pallas_call(functools.partial(feed_kernel, side), out_shape=[jax.Shape...  217 us
    pallas_call x1, Pallas kernels, start_layer(): pl.pallas_call(functools.partial(start_kernel, side, piece, sliced, 1.0 /...  196 us
    pallas_call x1, Pallas kernels, end_layer(): pl.pallas_call(functools.partial(end_kernel, side, piece, 1.0 / math.sqrt...  127 us
  transfers between devices with their start and end apart: 2, of which 0 were waited for; matrix products, arithmetic and copies ran while one was open for 1% of the time, Pallas kernels for 23%

profile of v7, /device:TPU:0, one launch (start us, length us, event | category | flops | bytes accessed | tf_op | source)
XLA Modules:
  0.0 586.6 jit_solution(8662106191943724170)
XLA Ops:
  7.2 0.0 reduce-scatter.2.cloned.1.call-start
  7.2 0.7 tile.4
  7.9 0.6 broadcast_in_dim_tile.6.refs_13_.refs_15_
  8.5 0.7 tile.5
  9.1 0.6 broadcast_in_dim_tile.7.refs_14_.refs_16_
  9.7 1.2 dynamic_slice.3.refs_8_.refs_9_
  11.0 196.3 %shard_map.255 = (bf16[2048,1536]{1,0:T(8,128)(2,1)}, bf16[1024,2048]{1,0:T(8,128)(2,1)}, bf16[2,4,2,256,1024]{4,3,2,1,0:T(8,128)(2,1)}, bf16[4,256,2048]{2,1,0:...) custom-call(bf16[128,1024]{1,0:T(8,128)(2,1)} %refs_0_.1, ...), custom_call_target="tpu_custom_call" | custom-call | flops 3221225472 | bytes 524288000 | tf_op jit(solution)/shard_map/pallas_call | solution.py:703
  207.3 216.7 %shard_map.256 = (bf16[256,2048]{1,0:T(8,128)(2,1)}, bf16[512,2048]{1,0:T(8,128)(2,1)}, f32[1,2048]{1,0:T(1,128)}, bf16[4,256,2048]{2,1,0:T(8,128)(2,1)}, bf16[4...) custom-call(bf16[256,2048]{1,0:T(8,128)(2,1)} %get-tuple-element.43., ...), custom_call_target="tpu_custom_call" | custom-call | flops 77309411328 | bytes 104857600 | tf_op jit(solution)/shard_map/pallas_call | solution.py:1097
  424.0 6.3 %convolution_convert_fusion = bf16[1024,2048]{1,0:T(8,128)(2,1)} fusion(bf16[512,1024]{1,0:T(8,128)(2,1)} %get-tuple-element.69, bf16[512,2048]{1,0:T(8,128)(2,1)} %get-tuple-element.56.refs_8_.dab), kind=kOutput, calls=%fused_computation | convolution fusion | flops 2149580800 | bytes 7340032 | tf_op jit(solution)/shard_map/dot_general | solution.py:206
  430.3 0.0 copy-start.1
  430.3 0.0 reduce-scatter.2.cloned.1.call-update
  430.3 1.2 copy-done.1
  431.5 1.8 collective-permute-start
  433.3 127.0 %shard_map.257 = (f32[128,1024]{1,0:T(8,128)}, f32[128,256]{1,0:T(8,128)}, f32[128,256]{1,0:T(8,128)}, bf16[2,8,128,512]{3,2,1,0:T(8,128)(2,1)}, f32[256,2048]{1...) custom-call(bf16[4,256,512]{2,1,0:T(8,128)(2,1)} %get-tuple-element.49.refs_0_, ...), custom_call_target="tpu_custom_call" | custom-call | flops 12884901888 | bytes 314572800 | tf_op jit(solution)/shard_map/pallas_call | solution.py:1434
  560.3 0.0 copy-start.5
  560.3 9.5 %shard_map.258 = (f32[128,4096]{1,0:T(8,128)}, f32[128,4096]{1,0:T(8,128)}, f32[512,2048]{1,0:T(8,128)}) custom-call(bf16[2,8,128,512]{3,2,1,0:T(8,128)(2,1)} %get-tuple-element.61.homes, bf16[512,2048]{1,0:T(8,128)(2,1)} %get-tuple-element.62.low, bf16[512,2048]{1,0:T(8,128)(2,1)} %get-tuple-element.63.low_got, bf16[512,2048]{1,0:T(8,128)(2,1)} %tokens.1, ...), custom_call_target="tpu_custom_call" | custom-call | flops 20971520 | bytes 20971520 | tf_op jit(solution)/shard_map/pallas_call | solution.py:1497
  569.8 0.0 copy-done.5
  569.8 0.6 fusion
  570.4 0.6 slice_bitcast_fusion
  571.0 0.0 collective-permute-done
  571.0 1.4 broadcast_select_fusion.1
  572.4 0.0 copy-start.2
  572.4 0.0 copy-start.4
  572.4 0.0 copy-start.3
  572.4 1.6 pad_maximum_fusion
  574.0 0.0 copy-start
  574.0 0.0 reduce-scatter.2.cloned.1.call-done
  574.0 1.9 convert_element_type.7
  575.9 0.0 copy-done.2
  575.9 0.8 copy.33
  576.7 0.0 copy-done.4
  576.7 0.7 copy.34
  577.4 0.0 copy-done.3
  577.4 0.7 copy.35
  578.0 0.0 copy-done
  578.0 1.3 copy.36
Async XLA Ops:
  7.2 566.8 %reduce-scatter.2.cloned.1.call-start = ((), (), s32[]{:S(2)}) async-start(), calls=%async_computation.1 | async-start | bytes 4456448 | tf_op jit(solution)/shard_map/reduce_scatter | solution.py:1577
  430.3 1.2 copy-start.1
  431.5 139.5 %collective-permute-start = (bf16[256,2048]{1,0:T(8,128)(2,1)S(1)}, bf16[256,2048]{1,0:T(8,128)(2,1)}, u32[]{:S(2)}, u32[]{:S(2)}) collective-permute-start(bf16[256,2048]{1,0:T(8,128)(2,1)S(1)} %copy-done.1), channel_id=1, source_target_pairs={{0,1},{1,0},{2,3},{3,2},{4,5},{5,4},{6,7},{7,6},{8,9},{9,8},{10,11... | collective-permute-start | bytes 3145736 | tf_op jit(solution)/shard_map/ppermute | solution.py:1533
  560.3 9.5 %copy-start.5 = (f32[33,128]{1,0:T(8,128)S(1)}, f32[33,128]{1,0:T(8,128)}, u32[]{:S(2)}) copy-start(f32[33,128]{1,0:T(8,128)} %get-tuple-element.65) | copy-start | bytes 50692
  572.4 3.5 copy-start.2
  572.4 4.3 copy-start.4
  572.4 5.0 copy-start.3
  574.0 4.0 copy-start
Sparse Core Ops, SparseCore 0:
  430.5 92.1 reduce-scatter.1
